TPU v7x, 32 devices: a whole 2x2x4 slice. The times are simulated.
32 devices in a mesh: rep: 2 (over y), req: 4 (over z), mp: 4 (over x, core).
Axes of the slice: x: 2, y: 2, z: 4, core: 2. Of those that a mesh axis runs over, the one named last changes fastest.
Arguments:
- hidden_in: bfloat16 [128, 2, 8192], P(('rep', 'req'), None, 'mp'), parts along dimension 0, may hold values from -6 to 6
- frozen_query_rows: bfloat16 [128, 2, 8192], P(('rep', 'req'), None, 'mp'), parts along dimension 0, may hold values from -6 to 86
- new_kv: bfloat16 [128, 2, 2, 1024], P(('rep', 'req'), None, None, 'mp'), parts along dimension 0, may hold values from -6 to 31
- adapter_of: int32 [128], P(('rep', 'req')), parts along dimension 0, may hold values from 0 to 7, as said below
- adapter_home: int32 [16], P('rep'), parts along dimension 0, may hold values from 0 to 7, as said below
- a_store: bfloat16 [16, 64, 8192], P(('rep', 'req'), None, 'mp'), parts along dimension 0, may hold values from -0.0625 to 0.0625
- b_store: bfloat16 [16, 64, 8192], P(('rep', 'req'), None, 'mp'), parts along dimension 0, may hold values from -0.75 to 0.75
- kv_pool: bfloat16 [2, 1024, 16, 1024], P(None, ('rep', 'req'), None, 'mp'), parts along dimension 1, may hold values from -6 to 31
- page_table: int32 [128, 8], P(('rep', 'req')), parts along dimension 0, may hold values from 0 to 127, as said below
- cached_len: int32 [128], P(('rep', 'req')), parts along dimension 0, may hold values from 32 to 128
- new_group: int32 [128], P(('rep', 'req')), parts along dimension 0, may hold values from 0 to 3, as said below
Outputs:
- attended: bfloat16 [128, 2, 8192], P(('rep', 'req'), None, 'mp'), parts along dimension 0
- cache: bfloat16 [2, 128, 128, 1024], P(None, ('rep', 'req'), None, 'mp'), parts along dimension 1
There are 2 independent parts, one for each index of `rep`. A program takes and returns all parts, laid end to end along the dimension named above; each array names one. Nothing has to cross between parts.
Inputs may be any that keep to these rules, and one draw needn't show every extreme that they name: A permutation: adapter a lives in store slot adapter_home[a], which belongs to group adapter_home[a] div 2. `adapter_of`: the requests of one group (new rows h * 16 to h * 16 + 15) use adapters of min(16, number of groups) different owners, at most 4 requests an owner, a number reached in every group; all requests of one group whose adapters have one owner use the same adapter. `page_table`: the rows of one group name each of its 128 pages once. `new_group`: A request keeps its slot (row mod 16); the same 4 slots keep their group in every group; every group receives exactly one request into each slot; no group sends more than 3 requests to one other group, and some pair of groups reaches it.
All inputs are finite; a program needn't handle non-finite values.
Results may differ from a plain program's by a relative error of at most 0.0069.
Values may be sent and summed in bfloat16 or wider, within the bound.
No kernel may reach another device: no remote copies, remote signals or barrier semaphores. Data moves between devices by JAX's collectives and lax.ppermute only.
A program may use at most 64 MiB of HBM per device.

v0:
```python
import jax
import jax.numpy as jnp
from jax import lax
from jax.sharding import PartitionSpec as P

HEAD = 128


NEG_FILL = -1e30


def attend(query_vectors, cached_keys, cached_values, length, fresh_kv):
    row_count, step_count, q_width = query_vectors.shape
    context = cached_keys.shape[1]
    kv_width = cached_keys.shape[2]
    kv_heads = kv_width // HEAD
    per_kv = q_width // kv_width
    score_scale = HEAD ** (-0.5)
    q_split = query_vectors.reshape(row_count, step_count, kv_heads, per_kv, HEAD)
    k_split = cached_keys.reshape(row_count, context, kv_heads, HEAD)
    v_split = cached_values.reshape(row_count, context, kv_heads, HEAD)
    new_keys = fresh_kv[:, :, 0].reshape(row_count, step_count, kv_heads, HEAD)
    new_values = fresh_kv[:, :, 1].reshape(row_count, step_count, kv_heads, HEAD)
    old_scores = (
        jnp.einsum("bskgd,bjkd->bskgj", q_split, k_split, preferred_element_type=jnp.float32)
        * score_scale
    )
    visible = jnp.arange(context)[None, :] < length[:, None]
    old_scores = jnp.where(visible[:, None, None, None, :], old_scores, NEG_FILL)
    new_scores = (
        jnp.einsum("bskgd,btkd->bskgt", q_split, new_keys, preferred_element_type=jnp.float32)
        * score_scale
    )
    causal = jnp.arange(step_count)[None, :] <= jnp.arange(step_count)[:, None]
    new_scores = jnp.where(causal[None, :, None, None, :], new_scores, NEG_FILL)
    scores = jnp.concatenate([old_scores, new_scores], axis=-1)
    row_max = jnp.max(scores, axis=-1, keepdims=True)
    weights = jnp.exp(scores - row_max)
    probabilities = (weights / jnp.sum(weights, axis=-1, keepdims=True)).astype(jnp.bfloat16)
    attention_out = jnp.einsum(
        "bskgj,bjkd->bskgd",
        probabilities[..., :context],
        v_split,
        preferred_element_type=jnp.float32,
    )
    attention_out = attention_out + jnp.einsum(
        "bskgt,btkd->bskgd",
        probabilities[..., context:],
        new_values,
        preferred_element_type=jnp.float32,
    )
    return attention_out.reshape(row_count, step_count, q_width).astype(jnp.bfloat16)


def adapter_rank_width(rank_partial_sum):
    return lax.psum(rank_partial_sum, "mp")


def per_device(
    hidden_in,
    frozen_query_rows,
    new_kv,
    adapter_of,
    adapter_home,
    a_store,
    b_store,
    kv_pool,
    page_table,
    cached_len,
    new_group,
):
    groups = lax.axis_size("req")
    my_group = lax.axis_index("req")
    per_group = adapter_of.shape[0]
    store_count = a_store.shape[0]
    context = page_table.shape[1] * kv_pool.shape[2]
    kv_width = kv_pool.shape[3]
    move_cap = -(-(per_group - per_group // 4) // groups)
    group_ids = jnp.arange(groups, dtype=jnp.int32)
    slot_ids = jnp.arange(per_group, dtype=jnp.int32)
    buffer_ids = jnp.arange(groups * move_cap, dtype=jnp.int32)
    adapter_slot = jnp.take(adapter_home, adapter_of)
    owners = adapter_slot // store_count
    local_pick = adapter_slot % store_count
    owner_hit = owners[:, None] == group_ids[None, :]
    wanted = jnp.max(jnp.where(owner_hit, local_pick[:, None], -1), axis=0)
    moving = new_group != my_group
    dest_hit = (new_group[:, None] == group_ids[None, :]) & moving[:, None]
    order_in = jnp.cumsum(dest_hit.astype(jnp.int32), axis=0) - 1
    position = jnp.sum(jnp.where(dest_hit, order_in, 0), axis=1)
    flat_slot = jnp.where(moving, new_group * move_cap + position, -1)
    slot_match = flat_slot[None, :] == buffer_ids[:, None]
    send_src = jnp.where(
        jnp.any(slot_match, axis=1),
        jnp.sum(jnp.where(slot_match, slot_ids[None, :], 0), axis=1),
        -1,
    )
    safe_src = jnp.maximum(send_src, 0)
    send_len = jnp.where(send_src >= 0, jnp.take(cached_len, safe_src), 0)
    got_wanted, got_slots, got_lens = (
        lax.all_to_all(wanted, "req", split_axis=0, concat_axis=0, tiled=True),
        lax.all_to_all(
            send_src.reshape(groups, move_cap), "req", split_axis=0, concat_axis=0, tiled=True
        ),
        lax.all_to_all(
            send_len.reshape(groups, move_cap), "req", split_axis=0, concat_axis=0, tiled=True
        ),
    )
    page_rows = jnp.take(kv_pool, page_table.reshape(-1), axis=1)
    cache_old = page_rows.reshape(2, per_group, context, kv_width)
    incoming = got_slots.reshape(-1)
    in_match = incoming[None, :] == slot_ids[:, None]
    in_index = jnp.sum(jnp.where(in_match, buffer_ids[None, :], 0), axis=1)
    len_new = jnp.where(moving, jnp.take(got_lens.reshape(-1), in_index), cached_len)
    wanted_slot = jnp.maximum(got_wanted, 0)
    a_panels, b_panels = (
        lax.all_to_all(
            jnp.take(a_store, wanted_slot, axis=0), "req", split_axis=0, concat_axis=0, tiled=True
        ),
        lax.all_to_all(
            jnp.take(b_store, wanted_slot, axis=0), "req", split_axis=0, concat_axis=0, tiled=True
        ),
    )
    a_rows = jnp.take(a_panels, owners, axis=0)
    up_panel_rows = jnp.take(b_panels, owners, axis=0)
    rank_slice_product = jnp.einsum(
        "rsd,rkd->rsk", hidden_in, a_rows, preferred_element_type=jnp.float32
    )
    complete_rank_product = adapter_rank_width(rank_slice_product).astype(jnp.bfloat16)
    adapter_query_delta = jnp.einsum(
        "gxj,gjv->gxv", complete_rank_product, up_panel_rows, preferred_element_type=jnp.float32
    )
    query_vectors = (frozen_query_rows.astype(jnp.float32) + adapter_query_delta).astype(
        jnp.bfloat16
    )
    far_cache = jnp.take(cache_old, safe_src, axis=1)
    send_pages = far_cache.reshape(2, groups, move_cap, context, kv_width)
    got_pages = lax.all_to_all(send_pages, "req", split_axis=1, concat_axis=1, tiled=True)
    pooled = jnp.concatenate(
        [cache_old, got_pages.reshape(2, groups * move_cap, context, kv_width)], axis=1
    )
    source = jnp.where(moving, per_group + in_index, slot_ids)
    cache_new = jnp.take(pooled, source, axis=1)
    attended = attend(query_vectors, cache_new[0], cache_new[1], len_new, new_kv)
    return (attended, cache_new)


def solution(mesh):
    placed = (
        P(("rep", "req"), None, "mp"),
        P(("rep", "req"), None, "mp"),
        P(("rep", "req"), None, None, "mp"),
        P(("rep", "req")),
        P("rep"),
        P(("rep", "req"), None, "mp"),
        P(("rep", "req"), None, "mp"),
        P(None, ("rep", "req"), None, "mp"),
        P(("rep", "req"), None),
        P(("rep", "req")),
        P(("rep", "req")),
    )
    return jax.shard_map(
        per_device,
        mesh=mesh,
        in_specs=placed,
        out_specs=(P(("rep", "req"), None, "mp"), P(None, ("rep", "req"), None, "mp")),
        check_vma=False,
    )
```

profile of v0, /device:TPU:0, one launch (start us, length us, event | category | flops | bytes accessed | tf_op | source)
XLA Modules:
  0.0 155.8 jit_solution(11224241576532435948)
XLA Ops:
  4.2 6.3 %all-to-all-start.3 = ((s32[4,1,1]{2,1,0:T(1,128)}), s32[4,1,1]{2,1,0:T(1,128)S(1)}, u32[]{:S(2)}, u32[]{:S(2)}) async-start(s32[4,1,1]{2,1,0:T(1,128)} %copy.112), calls=%async_computation.3 | async-start | bytes 4096 | tf_op jit(solution)/shard_map/all_to_all | solution.py:101
  17.1 5.1 %all-to-all-start = ((s32[4,1,3]{2,1,0:T(1,128)}), s32[4,1,3]{2,1,0:T(1,128)S(1)}, u32[]{:S(2)}, u32[]{:S(2)}) async-start(s32[4,1,3]{2,1,0:T(1,128)} %bitcast), calls=%async_computation | async-start | bytes 4096 | tf_op jit(solution)/shard_map/all_to_all | solution.py:102
  24.0 2.6 %gather_fusion.8 = bf16[4,64,2048]{2,1,0:T(8,128)(2,1)} fusion(bf16[2,64,2048]{2,1,0:T(8,128)(2,1)} %param.21, s32[1024]{0:T(1024)S(1)} %pad_clamp_fusion.1), kind=kCustom, calls=%fused_computation.2.clone | custom fusion | bytes 2097168 | tf_op jit(solution)/shard_map/jit(_take)/gather | solution.py:121
  27.6 4.1 %all-to-all-start.2 = ((s32[4,1,3]{2,1,0:T(1,128)}), s32[4,1,3]{2,1,0:T(1,128)S(1)}, u32[]{:S(2)}, u32[]{:S(2)}) async-start(s32[4,1,3]{2,1,0:T(1,128)} %bitcast.10), calls=%async_computation.2 | async-start | bytes 4096 | tf_op jit(solution)/shard_map/all_to_all | solution.py:105
  31.8 2.8 %broadcast_select_fusion.1 = (bf16[4,64,2048]{2,1,0:T(8,128)(2,1)}, bf16[4,64,2048]{2,1,0:T(8,128)(2,1)}) fusion(bf16[4,64,2048]{2,1,0:T(8,128)(2,1)S(1)} %gather_fusion.6, pred[4]{0:T(512)(128)(4,1)S(1)} %compare_and_fusion.2, bf16[4,64,2048]{2,1,0:T(8,128)(2,1)} %gather_fusion.8), kind=kLoop, calls=%fused_computation.36 | loop fusion | flops 1048576 | bytes 4194308 | tf_op jit(solution)/shard_map/jit(_take)/select_n | solution.py:118
  34.6 2.6 %all-to-all-done.2 = s32[4,1,3]{2,1,0:T(1,128)S(1)} async-done(((s32[4,1,3]{2,1,0:T(1,128)}), s32[4,1,3]{2,1,0:T(1,128)S(1)}, u32[]{:S(2)}, u32[]{:S(2)}) %all-to-all-start.2) | async-done | bytes 80 | tf_op jit(solution)/shard_map/all_to_all | solution.py:105
  37.1 3.5 %all-to-all-start.4 = ((bf16[4,64,2048]{2,1,0:T(8,128)(2,1)}), bf16[4,64,2048]{2,1,0:T(8,128)(2,1)S(1)}, u32[]{:S(2)}, u32[]{:S(2)}) async-start(bf16[4,64,2048]{2,1,0:T(8,128)(2,1)} %get-tuple-element.25), calls=%async_computation.4 | async-start | bytes 2097152 | tf_op jit(solution)/shard_map/all_to_all | solution.py:117
  40.8 23.4 %all-to-all-done.4 = bf16[4,64,2048]{2,1,0:T(8,128)(2,1)S(1)} async-done(((bf16[4,64,2048]{2,1,0:T(8,128)(2,1)}), bf16[4,64,2048]{2,1,0:T(8,128)(2,1)S(1)}, u32[]{:S(2)}, u32[]{:S(2)}) %all-to-all-start.4) | async-done | bytes 1048608 | tf_op jit(solution)/shard_map/all_to_all | solution.py:117
  64.2 4.2 %all-to-all-start.5 = ((bf16[4,64,2048]{2,1,0:T(8,128)(2,1)}), bf16[4,64,2048]{2,1,0:T(8,128)(2,1)}, u32[]{:S(2)}, u32[]{:S(2)}) async-start(bf16[4,64,2048]{2,1,0:T(8,128)(2,1)} %get-tuple-element.26), calls=%async_computation.5 | async-start | bytes 2097152 | tf_op jit(solution)/shard_map/all_to_all | solution.py:120
  68.5 2.0 %gather_fusion = bf16[128,2,16,256]{3,2,1,0:T(8,128)(2,1)} fusion(bf16[2,128,16,256]{3,2,1,0:T(8,128)(2,1)S(1)} %copy-done, s32[1024]{0:T(1024)S(1)} %pad_clamp_fusion.6), kind=kCustom, calls=%fused_computation.4 | custom fusion | bytes 4194816 | tf_op jit(solution)/shard_map/jit(_take)/gather | solution.py:109
  70.5 3.1 %copy.106 = bf16[2,128,16,256]{3,2,1,0:T(8,128)(2,1)} copy(bf16[2,128,16,256]{3,2,0,1:T(8,128)(2,1)} %bitcast.52) | data formatting | bytes 4194304 | tf_op jit(solution)/shard_map/jit(_take)/gather | solution.py:109
  73.9 2.8 %bitcast_select_fusion = bf16[2,16,128,256]{3,2,1,0:T(8,128)(2,1)} fusion(pred[16,128]{1,0:T(8,128)(4,1)S(1)} %broadcast_in_dim.159, bf16[2,16,128,256]{3,2,1,0:T(8,128)(2,1)} %bitcast.51), kind=kLoop, calls=%fused_computation.19 | loop fusion | flops 1048576 | bytes 4196352 | tf_op jit(solution)/shard_map/jit(_take)/select_n | solution.py:109
  76.7 3.4 %gather_fusion.1 = bf16[12,2,128,256]{3,2,1,0:T(8,128)(2,1)} fusion(bf16[2,16,128,256]{3,2,1,0:T(8,128)(2,1)} %bitcast_select_fusion, s32[1024]{0:T(1024)S(1)} %pad_clamp_fusion.5), kind=kCustom, calls=%fused_computation.5 | custom fusion | bytes 3145776 | tf_op jit(solution)/shard_map/jit(_take)/gather | solution.py:136
  81.0 2.9 %copy_select_fusion = bf16[2,4,3,128,256]{4,3,2,0,1:T(8,128)(2,1)} fusion(bf16[2,4,3,128,256]{4,3,0,2,1:T(8,128)(2,1)} %bitcast.54, pred[4,3]{1,0:T(4,128)(4,1)S(1)} %le.81), kind=kLoop, calls=%fused_computation.23 | loop fusion | flops 786432 | bytes 3145740 | tf_op jit(solution)/shard_map/jit(_take)/select_n | solution.py:136
  83.9 9.9 %all-to-all-done.5 = bf16[4,64,2048]{2,1,0:T(8,128)(2,1)} async-done(((bf16[4,64,2048]{2,1,0:T(8,128)(2,1)}), bf16[4,64,2048]{2,1,0:T(8,128)(2,1)}, u32[]{:S(2)}, u32[]{:S(2)}) %all-to-all-start.5) | async-done | bytes 1048608 | tf_op jit(solution)/shard_map/all_to_all | solution.py:120
  93.8 4.3 %all-to-all-start.1 = ((bf16[2,4,3,128,256]{4,3,2,0,1:T(8,128)(2,1)}), bf16[2,4,3,128,256]{4,3,2,0,1:T(8,128)(2,1)}, u32[]{:S(2)}, u32[]{:S(2)}) async-start(bf16[2,4,3,128,256]{4,3,2,0,1:T(8,128)(2,1)} %copy_select_fusion), calls=%async_computation.1 | async-start | bytes 3145728 | tf_op jit(solution)/shard_map/all_to_all | solution.py:138
  103.3 2.8 %gather_fusion.7 = bf16[16,64,2048]{2,1,0:T(8,128)(2,1)} fusion(bf16[4,64,2048]{2,1,0:T(8,128)(2,1)S(1)} %all-to-all-done.4, s32[1024]{0:T(1024)S(1)} %pad_clamp_fusion), kind=kCustom, calls=%fused_computation.1.clone | custom fusion | bytes 8388672 | tf_op jit(solution)/shard_map/jit(_take)/gather | solution.py:124
  106.1 4.0 %gather_fusion.9 = bf16[16,64,2048]{2,1,0:T(8,128)(2,1)} fusion(bf16[4,64,2048]{2,1,0:T(8,128)(2,1)} %all-to-all-done.5, s32[1024]{0:T(1024)S(1)} %pad_clamp_fusion), kind=kCustom, calls=%fused_computation.3.clone | custom fusion | bytes 8388672 | tf_op jit(solution)/shard_map/jit(_take)/gather | solution.py:125
  110.1 3.5 %fusion.20 = f32[16,2,64]{2,1,0:T(2,128)S(1)} fusion(bf16[16,2,2048]{2,1,0:T(2,128)(2,1)S(1)} %copy-done.9, bf16[16,64,2048]{2,1,0:T(8,128)(2,1)} %gather_fusion.7, pred[16]{0:T(512)(128)(4,1)S(1)} %get-tuple-element.16), kind=kOutput, calls=%fused_computation.34 | convolution fusion | flops 10485760 | bytes 4333584 | tf_op jit(solution)/shard_map/rsd,rkd->rsk/dot_general | solution.py:126
  113.6 10.2 %psum.7 = bf16[16,2,64]{2,1,0:T(2,128)(2,1)S(1)} all-reduce(f32[16,2,64]{2,1,0:T(2,128)S(1)} %fusion.20), channel_id=1, replica_groups=mesh['rep'=2,'req'=4,'mp'=4] {'mp'}, use_global_device_ids=true, to_apply=%region_6.9 | all-reduce | flops 2048 | bytes 12288 | tf_op jit(solution)/shard_map/psum | solution.py:56
  123.8 2.9 %fusion.9 = bf16[16,2,2048]{2,1,0:T(2,128)(2,1)S(1)} fusion(bf16[16,64,2048]{2,1,0:T(8,128)(2,1)} %gather_fusion.9, pred[16]{0:T(512)(128)(4,1)S(1)} %get-tuple-element.16, bf16[16,2,2048]{2,1,0:T(2,128)(2,1)S(1)} %copy-done.10, bf16[16,2,64]{2,1,0:T(2,128)(2,1)S(1)} %psum.7), kind=kOutput, calls=%fused_computation.18 | convolution fusion | flops 10682368 | bytes 4460560 | tf_op jit(solution)/shard_map/gxj,gjv->gxv/dot_general | solution.py:130
  127.8 6.8 %all-to-all-done.1 = bf16[2,4,3,128,256]{4,3,2,0,1:T(8,128)(2,1)} async-done(((bf16[2,4,3,128,256]{4,3,2,0,1:T(8,128)(2,1)}), bf16[2,4,3,128,256]{4,3,2,0,1:T(8,128)(2,1)}, u32[]{:S(2)}, u32[]{:S(2)}) %all-to-all-start.1) | async-done | bytes 1572896 | tf_op jit(solution)/shard_map/all_to_all | solution.py:138
  136.7 2.1 %pad_maximum_fusion = bf16[2,28,128,256]{3,2,1,0:T(8,128)(2,1)} fusion(bf16[2,12,128,256]{3,2,1,0:T(8,128)(2,1)S(1)} %bitcast.53, bf16[2,16,128,256]{3,2,1,0:T(8,128)(2,1)S(1)} %copy-done.2), kind=kLoop, calls=%fused_computation.16 | loop fusion | flops 1835008 | bytes 7340032 | tf_op jit(solution)/shard_map/concatenate | solution.py:139
  138.8 4.2 %gather_fusion.2 = bf16[16,2,128,256]{3,2,1,0:T(8,128)(2,1)} fusion(bf16[2,28,128,256]{3,2,1,0:T(8,128)(2,1)} %pad_maximum_fusion, s32[1024]{0:T(1024)} %pad_clamp_fusion.4), kind=kCustom, calls=%fused_computation.6 | custom fusion | bytes 4194368 | tf_op jit(solution)/shard_map/jit(_take)/gather | solution.py:143
  (96 shorter events, 35.3 us)
Async XLA Ops:
  0.6 67.9 %copy-start = (bf16[2,128,16,256]{3,2,1,0:T(8,128)(2,1)S(1)}, bf16[2,128,16,256]{3,2,1,0:T(8,128)(2,1)}, u32[]{:S(2)}) copy-start(bf16[2,128,16,256]{3,2,1,0:T(8,128)(2,1)} %param.22) | copy-start | bytes 6291460
  4.2 12.9 %all-to-all-start.3 = ((s32[4,1,1]{2,1,0:T(1,128)}), s32[4,1,1]{2,1,0:T(1,128)S(1)}, u32[]{:S(2)}, u32[]{:S(2)}) async-start(s32[4,1,1]{2,1,0:T(1,128)} %copy.112), calls=%async_computation.3 | async-start | bytes 4096 | tf_op jit(solution)/shard_map/all_to_all | solution.py:101
  17.1 10.6 %all-to-all-start = ((s32[4,1,3]{2,1,0:T(1,128)}), s32[4,1,3]{2,1,0:T(1,128)S(1)}, u32[]{:S(2)}, u32[]{:S(2)}) async-start(s32[4,1,3]{2,1,0:T(1,128)} %bitcast), calls=%async_computation | async-start | bytes 4096 | tf_op jit(solution)/shard_map/all_to_all | solution.py:102
  27.6 9.5 %all-to-all-start.2 = ((s32[4,1,3]{2,1,0:T(1,128)}), s32[4,1,3]{2,1,0:T(1,128)S(1)}, u32[]{:S(2)}, u32[]{:S(2)}) async-start(s32[4,1,3]{2,1,0:T(1,128)} %bitcast.10), calls=%async_computation.2 | async-start | bytes 4096 | tf_op jit(solution)/shard_map/all_to_all | solution.py:105
  34.6 6.1 %copy-start.5 = (s32[16,8]{0,1:T(8,128)S(1)}, s32[16,8]{0,1:T(8,128)}, u32[]{:S(2)}) copy-start(s32[16,8]{0,1:T(8,128)} %param.23) | copy-start | bytes 1540
  37.1 27.1 %all-to-all-start.4 = ((bf16[4,64,2048]{2,1,0:T(8,128)(2,1)}), bf16[4,64,2048]{2,1,0:T(8,128)(2,1)S(1)}, u32[]{:S(2)}, u32[]{:S(2)}) async-start(bf16[4,64,2048]{2,1,0:T(8,128)(2,1)} %get-tuple-element.25), calls=%async_computation.4 | async-start | bytes 2097152 | tf_op jit(solution)/shard_map/all_to_all | solution.py:117
  64.2 29.5 %all-to-all-start.5 = ((bf16[4,64,2048]{2,1,0:T(8,128)(2,1)}), bf16[4,64,2048]{2,1,0:T(8,128)(2,1)}, u32[]{:S(2)}, u32[]{:S(2)}) async-start(bf16[4,64,2048]{2,1,0:T(8,128)(2,1)} %get-tuple-element.26), calls=%async_computation.5 | async-start | bytes 2097152 | tf_op jit(solution)/shard_map/all_to_all | solution.py:120
  76.7 3.5 %copy-start.4 = (bf16[16,2,2,256]{3,2,1,0:T(2,128)(2,1)S(1)}, bf16[16,2,2,256]{3,2,1,0:T(2,128)(2,1)}, u32[]{:S(2)}) copy-start(bf16[16,2,2,256]{3,2,1,0:T(2,128)(2,1)} %param.17) | copy-start | bytes 98308
  83.9 17.6 %copy-start.7 = (s32[16]{0:T(128)S(1)}, s32[16]{0:T(128)}, u32[]{:S(2)}) copy-start(s32[16]{0:T(128)} %param.25) | copy-start | bytes 196
  83.9 18.8 %copy-start.1 = (s32[16]{0:T(128)S(1)}, s32[16]{0:T(128)}, u32[]{:S(2)}) copy-start(s32[16]{0:T(128)} %param.24) | copy-start | bytes 196
  93.8 40.9 %all-to-all-start.1 = ((bf16[2,4,3,128,256]{4,3,2,0,1:T(8,128)(2,1)}), bf16[2,4,3,128,256]{4,3,2,0,1:T(8,128)(2,1)}, u32[]{:S(2)}, u32[]{:S(2)}) async-start(bf16[2,4,3,128,256]{4,3,2,0,1:T(8,128)(2,1)} %copy_select_fusion), calls=%async_computation.1 | async-start | bytes 3145728 | tf_op jit(solution)/shard_map/all_to_all | solution.py:138
  106.1 4.0 %copy-start.9 = (bf16[16,2,2048]{2,1,0:T(2,128)(2,1)S(1)}, bf16[16,2,2048]{2,1,0:T(2,128)(2,1)}, u32[]{:S(2)}) copy-start(bf16[16,2,2048]{2,1,0:T(2,128)(2,1)} %param.15) | copy-start | bytes 393220
  110.1 13.7 %copy-start.10 = (bf16[16,2,2048]{2,1,0:T(2,128)(2,1)S(1)}, bf16[16,2,2048]{2,1,0:T(2,128)(2,1)}, u32[]{:S(2)}) copy-start(bf16[16,2,2048]{2,1,0:T(2,128)(2,1)} %param.16) | copy-start | bytes 393220
  123.8 3.1 %copy-start.6 = (bf16[16,2,2,128]{3,2,1,0:T(2,128)(2,1)S(1)}, bf16[16,2,2,128]{3,2,1,0:T(2,128)(2,1)}, u32[]{:S(2)}) copy-start(bf16[16,2,2,128]{3,2,1,0:T(2,128)(2,1)} %reshape.370) | copy-start | bytes 49156
  123.8 3.1 %copy-start.11 = (pred[2,2]{1,0:T(4,128)(4,1)S(1)}, pred[2,2]{1,0:T(4,128)(4,1)}, u32[]{:S(2)}) copy-start(pred[2,2]{1,0:T(4,128)(4,1)} %iota_compare_fusion.5) | copy-start | bytes 16
  134.6 2.1 %copy-start.2 = (bf16[2,16,128,256]{3,2,1,0:T(8,128)(2,1)S(1)}, bf16[2,16,128,256]{3,2,1,0:T(8,128)(2,1)}, u32[]{:S(2)}) copy-start(bf16[2,16,128,256]{3,2,1,0:T(8,128)(2,1)} %bitcast_select_fusion) | copy-start | bytes 6291460
  138.8 4.2 %copy-start.8 = (pred[16]{0:T(512)(128)(4,1)S(1)}, pred[16]{0:T(512)(128)(4,1)}, u32[]{:S(2)}) copy-start(pred[16]{0:T(512)(128)(4,1)} %get-tuple-element.19) | copy-start | bytes 52
  152.6 1.7 %copy-start.3 = (bf16[16,2,2,8,130]{4,3,1,2,0:T(8,128)(2,1)S(1)}, bf16[16,2,2,8,130]{4,3,1,2,0:T(8,128)(2,1)}, u32[]{:S(2)}) copy-start(bf16[16,2,2,8,130]{4,3,1,2,0:T(8,128)(2,1)} %divide_convert_fusion) | copy-start | bytes 399364
where the time goes:
time: 157 us; the launch traced here: 156 us
  waiting for transfers between devices  43.7 us (28%)
  local copies, waits for them, and re-layouts  39.6 us (25%)
  starting transfers between devices  27.6 us (18%)
  other arithmetic  24.5 us (16%)
  blocking collectives  10.2 us (6%)
  matrix products  9.32 us (6%)
    all_to_all x1, waiting for transfers between devices, per_device(): lax.all_to_all(jnp.take(a_store, wanted_slot, axis=0), 'req', split_axis=...  23.4 us
    psum x1, blocking collectives, adapter_rank_width(): return lax.psum(rank_partial_sum, 'mp')  10.2 us
    all_to_all x1, waiting for transfers between devices, per_device(): lax.all_to_all(jnp.take(b_store, wanted_slot, axis=0), 'req', split_axis=...  9.87 us
    all_to_all x1, waiting for transfers between devices, per_device(): lax.all_to_all(send_pages, 'req', split_axis=1, concat_axis=1, tiled=True)  6.84 us
    all_to_all x1, starting transfers between devices, per_device(): lax.all_to_all(wanted, 'req', split_axis=0, concat_axis=0, tiled=True)  6.32 us
    gather x2, local copies, waits for them, and re-layouts, per_device(): page_rows = jnp.take(kv_pool, page_table.reshape(-1), axis=1)  5.1 us
    all_to_all x1, starting transfers between devices, per_device(): lax.all_to_all(send_src.reshape(groups, move_cap), 'req', split_axis=0, c...  5.09 us
    all_to_all x1, starting transfers between devices, per_device(): lax.all_to_all(send_pages, 'req', split_axis=1, concat_axis=1, tiled=True)  4.35 us
  transfers between devices with their start and end apart: 6, of which 5 were waited for; matrix products, arithmetic and copies ran while one was open for 31% of the time, Pallas kernels for 0%

commit v1 on v0

v1 whole, which is shorter than its diff:
```python
import functools

import jax
import jax.numpy as jnp
from jax import lax
from jax.experimental import pallas as pl
from jax.experimental.pallas import tpu as pltpu
from jax.sharding import PartitionSpec as P

HEAD = 128
LANES = 128
TILE = 16
NEG_FILL = -1e30
VMEM_LIMIT = 40 * 1024 * 1024

IN_VMEM = pl.BlockSpec(memory_space=pltpu.VMEM)
IN_SMEM = pl.BlockSpec(memory_space=pltpu.SMEM)
IN_PLACE = pl.BlockSpec(memory_space=pl.ANY)
PARAMS = pltpu.CompilerParams(vmem_limit_bytes=VMEM_LIMIT)


def to_tiles(rows):
    count, steps, width = rows.shape
    split = rows.reshape(count, steps, width // LANES, LANES)
    return split.transpose(0, 2, 1, 3).reshape(count, width // LANES * steps, LANES)


def from_tiles(tiles, steps):
    count, depth, _ = tiles.shape
    split = tiles.reshape(count, depth // steps, steps, LANES)
    return split.transpose(0, 2, 1, 3).reshape(count, steps, depth // steps * LANES)


def stage_rows_kernel(dims, adapter_of, adapter_home, new_group, cached_len, hidden, frozen, *refs):
    groups, own_cap, move_cap, stores = dims
    messages, plan = refs[:groups], refs[groups]
    counts, picks, meta, sems = refs[groups + 1 :]
    count, depth, _ = hidden.shape
    me = lax.axis_index("req")
    for i in range(groups * (own_cap + move_cap)):
        plan[i] = -1
    for j in range(groups):
        counts[j] = 0
        counts[groups + j] = 0
        picks[j] = 0
    for r in range(count):
        store = adapter_home[adapter_of[r]]
        j = jnp.bitwise_xor(store // stores, me)
        k = counts[j]
        plan[j * own_cap + k] = r
        counts[j] = k + 1
        picks[j] = store % stores
        to = jnp.bitwise_xor(new_group[r], me)

        @pl.when(to != 0)
        def _(to=to, r=r):
            at = counts[groups + to]
            plan[groups * own_cap + to * move_cap + at] = r
            counts[groups + to] = at + 1

    lane = lax.broadcasted_iota(jnp.int32, (TILE, LANES), 1)
    for j in range(groups):
        for k in range(own_cap):
            source = jnp.maximum(plan[j * own_cap + k], 0)
            for part, rows in enumerate((hidden, frozen)):
                pltpu.make_async_copy(
                    rows.at[source],
                    messages[j].at[pl.ds((part * own_cap + k) * depth, depth)],
                    sems.at[j],
                ).start()
        told = jnp.where(lane == 0, picks[j], 0)
        for k in range(move_cap):
            slot = plan[(groups * own_cap) + j * move_cap + k]
            length = cached_len[jnp.maximum(slot, 0)]
            told = jnp.where(lane == 1 + k, slot, told)
            told = jnp.where(lane == 1 + move_cap + k, length, told)
        meta[j] = told.astype(jnp.float32).astype(jnp.bfloat16)
        pltpu.make_async_copy(
            meta.at[j], messages[j].at[pl.ds(2 * own_cap * depth, TILE)], sems.at[j]
        ).start()
    for j in range(groups):
        pltpu.make_async_copy(messages[j], messages[j], sems.at[j]).wait()


def stage_pages_kernel(dims, partners, plan, table, pool, *refs):
    groups, own_cap, move_cap, _ = dims
    outs, sems = refs[: len(partners)], refs[len(partners)]
    page = pool.shape[2]
    for i, j in enumerate(partners):
        for k in range(move_cap):
            source = jnp.maximum(plan[groups * own_cap + j * move_cap + k], 0)
            for p in range(table.shape[0]):
                pltpu.make_async_copy(
                    pool.at[:, table[p, source]],
                    outs[i].at[k, :, pl.ds(p * page, page)],
                    sems.at[i],
                ).start()
    for i in range(len(partners)):
        pltpu.make_async_copy(outs[i], outs[i], sems.at[i]).wait()


def rank_kernel(dims, cached_len, a_ref, *refs):
    groups, own_cap, move_cap, _ = dims
    messages = refs[:groups]
    partial, told = refs[groups : groups + 2]
    x, meta, meta_scalar, sem = refs[groups + 2 :]
    width = a_ref.shape[1]
    blocks = width // LANES
    depth = 2 * blocks
    per = own_cap * depth
    number = groups * own_cap
    for j in range(groups):
        x[j * per : (j + 1) * per, :] = messages[j][0:per, :].astype(jnp.float32)
        tile = messages[j][2 * per : 2 * per + TILE, :].astype(jnp.float32)
        meta[j : j + 1, :] = tile[0:1, :].astype(jnp.int32)
    copy = pltpu.make_async_copy(meta, meta_scalar, sem)
    copy.start()
    columns = [
        jnp.concatenate([x[pl.ds(2 * c + s, number, stride=depth), :] for s in range(2)], axis=0)
        for c in range(blocks)
    ]
    rows = jnp.concatenate(columns, axis=1).astype(jnp.bfloat16)
    partial[...] = lax.dot_general(
        rows, a_ref[...], (((1,), (1,)), ((), ())), preferred_element_type=jnp.float32
    )
    copy.wait()
    count = cached_len.shape[0]
    for r in range(count):
        told[groups + r] = 0
        told[groups + count + r] = 0
        told[groups + 2 * count + r] = cached_len[r]
    for j in range(groups):
        told[j] = meta_scalar[j, 0]
        for k in range(move_cap):
            slot = meta_scalar[j, 1 + k]
            told[groups + 3 * count + j * move_cap + k] = slot
            if j == 0:
                continue

            @pl.when(slot >= 0)
            def _(slot=slot, j=j, k=k):
                told[groups + slot] = j
                told[groups + count + slot] = k
                told[groups + 2 * count + slot] = meta_scalar[j, 1 + move_cap + k]


def pair_sum(parts):
    while len(parts) > 1:
        parts = [parts[i] + parts[i + 1] for i in range(0, len(parts), 2)]
    return parts[0]


def query_kernel(dims, n_parts, told, b_ref, *refs):
    groups, own_cap, _, stores = dims
    partials, messages = refs[:n_parts], refs[n_parts : n_parts + groups]
    outs, x = refs[n_parts + groups : n_parts + 2 * groups], refs[n_parts + 2 * groups]
    width = b_ref.shape[1]
    rank = b_ref.shape[0] // stores
    blocks = width // LANES
    depth = 2 * blocks
    per = own_cap * depth
    number = groups * own_cap
    full = pair_sum([p[...] for p in partials]).astype(jnp.bfloat16)
    row = lax.broadcasted_iota(jnp.int32, full.shape, 0)
    group_of = (row % number) // own_cap
    pick = jnp.zeros(full.shape, jnp.int32)
    for j in range(groups):
        pick = jnp.where(group_of == j, told[j], pick)
    chosen = lax.broadcasted_iota(jnp.int32, full.shape, 1) // rank == pick
    full = jnp.where(chosen, full.astype(jnp.float32), 0.0).astype(jnp.bfloat16)
    delta = jnp.dot(full, b_ref[...], preferred_element_type=jnp.float32)
    for c in range(blocks):
        for s in range(2):
            x[pl.ds(2 * c + s, number, stride=depth), :] = delta[
                s * number : (s + 1) * number, c * LANES : (c + 1) * LANES
            ]
    for j in range(groups):
        base = messages[j][per : 2 * per, :].astype(jnp.float32)
        outs[j][...] = (base + x[j * per : (j + 1) * per, :]).astype(jnp.bfloat16)


def fresh_rows(new_kv, x, heads):
    x[...] = new_kv[...].astype(jnp.float32)
    number = x.shape[0] // (2 * heads)
    return [
        jnp.concatenate(
            [x[pl.ds(2 * h + part, number, stride=2 * heads), :] for h in range(heads)], axis=1
        ).astype(jnp.bfloat16)
        for part in range(2)
    ]


def attend(query, keys, values, fresh, length, slot):
    depth = query.shape[0]
    context, width = keys.shape
    heads = width // HEAD
    per = depth // heads
    scale = HEAD**-0.5
    blank = jnp.zeros((per, HEAD), query.dtype)
    spread = jnp.concatenate(
        [
            jnp.concatenate(
                [query[h * per : (h + 1) * per] if i == h else blank for i in range(heads)], axis=1
            )
            for h in range(heads)
        ],
        axis=0,
    )
    all_keys = jnp.concatenate([keys, fresh[0]], axis=0)
    all_values = jnp.concatenate([values, fresh[1]], axis=0)
    scores = lax.dot_general(
        spread, all_keys, (((1,), (1,)), ((), ())), preferred_element_type=jnp.float32
    )
    column = lax.broadcasted_iota(jnp.int32, scores.shape, 1)
    step = lax.broadcasted_iota(jnp.int32, scores.shape, 0) % 2
    fresh_at = column - context - 2 * slot
    visible = (column < length) | ((fresh_at >= 0) & (fresh_at <= step))
    scores = jnp.where(visible, scores * scale, NEG_FILL)
    weights = jnp.exp(scores - jnp.max(scores, axis=1, keepdims=True))
    chance = (weights / jnp.sum(weights, axis=1, keepdims=True)).astype(jnp.bfloat16)
    out = jnp.dot(chance, all_values, preferred_element_type=jnp.float32)
    out = jnp.concatenate(
        [out[h * per : (h + 1) * per, h * HEAD : (h + 1) * HEAD] for h in range(heads)], axis=0
    )
    return out.astype(jnp.bfloat16)


def early_kernel(dims, partners, plan, told, table, pool, new_kv, *refs):
    groups, own_cap, move_cap, _ = dims
    queries, refs = refs[:groups], refs[groups:]
    pages, refs = refs[: len(partners)], refs[len(partners) :]
    attended, cache, sorted_queries, kv, x, kv_sems, query_sems, out_sems = refs
    count, depth, _ = attended.shape
    page = pool.shape[2]

    def here(source):
        known = source == 0
        for j in partners:
            known = known | (source == j)
        return known

    for r in range(count):
        source = told[groups + r]

        @pl.when(source == 0)
        def _(r=r):
            for p in range(table.shape[0]):
                pltpu.make_async_copy(
                    pool.at[:, table[p, r]], kv.at[:, r, pl.ds(p * page, page)], kv_sems.at[r]
                ).start()

        for i, j in enumerate(partners):

            @pl.when(source == j)
            def _(r=r, i=i):
                pltpu.make_async_copy(
                    pages[i].at[told[groups + count + r]], kv.at[:, r], kv_sems.at[r]
                ).start()

    for j in range(groups):
        for k in range(own_cap):
            slot = plan[j * own_cap + k]

            @pl.when(slot >= 0)
            def _(j=j, k=k, slot=slot):
                pltpu.make_async_copy(
                    queries[j].at[pl.ds(k * depth, depth)],
                    sorted_queries.at[slot],
                    query_sems.at[slot],
                ).start()

    fresh = fresh_rows(new_kv, x, kv.shape[3] // HEAD)
    for r in range(count):
        pltpu.make_async_copy(sorted_queries.at[r], sorted_queries.at[r], query_sems.at[r]).wait()

        @pl.when(here(told[groups + r]))
        def _(r=r):
            pltpu.make_async_copy(kv.at[:, r], kv.at[:, r], kv_sems.at[r]).wait()
            pltpu.make_async_copy(kv.at[:, r], cache.at[:, r], out_sems.at[r]).start()

    for r in range(count):
        attended[r] = attend(
            sorted_queries[r], kv[0, r], kv[1, r], fresh, told[groups + 2 * count + r], r
        )
    for r in range(count):

        @pl.when(here(told[groups + r]))
        def _(r=r):
            pltpu.make_async_copy(kv.at[:, r], cache.at[:, r], out_sems.at[r]).wait()


def late_kernel(dims, partners, told, new_kv, queries, attended_in, cache_in, *refs):
    groups, _, move_cap, _ = dims
    pages, refs = refs[: len(partners)], refs[len(partners) :]
    attended, cache, results, x, page_sems, out_sems = refs
    count = queries.shape[0]
    kv_width = cache.shape[3]
    copies = []
    for i, j in enumerate(partners):
        for k in range(move_cap):
            slot = told[groups + 3 * count + j * move_cap + k]
            at = jnp.maximum(slot, 0)
            n = i * move_cap + k
            copies.append(
                (
                    slot,
                    at,
                    pltpu.make_async_copy(pages[i].at[k], cache.at[:, at], page_sems.at[n]),
                    pltpu.make_async_copy(results.at[n], attended.at[at], out_sems.at[n]),
                )
            )
            pl.when(slot >= 0)(copies[-1][2].start)
    fresh = fresh_rows(new_kv, x, kv_width // HEAD)
    for n, (slot, at, _, _) in enumerate(copies):
        i, k = divmod(n, move_cap)
        results[n] = attend(
            queries[at], pages[i][k, 0], pages[i][k, 1], fresh, told[groups + 2 * count + at], at
        )
    for slot, _, _, copy in copies:
        pl.when(slot >= 0)(copy.start)
    for slot, _, page_copy, copy in copies:

        @pl.when(slot >= 0)
        def _(page_copy=page_copy, copy=copy):
            page_copy.wait()
            copy.wait()


def swap(x, axis, j):
    return lax.ppermute(x, axis, [(i, i ^ j) for i in range(lax.axis_size(axis))])


def per_device(
    hidden_in,
    frozen_query_rows,
    new_kv,
    adapter_of,
    adapter_home,
    a_store,
    b_store,
    kv_pool,
    page_table,
    cached_len,
    new_group,
):
    groups = lax.axis_size("req")
    shards = lax.axis_size("mp")
    count, steps, width = hidden_in.shape
    stores, rank, _ = a_store.shape
    _, _, page, kv_width = kv_pool.shape
    context = page_table.shape[1] * page
    heads = kv_width // HEAD
    own_cap = -(-count // min(16, groups))
    move_cap = -(-(count - count // 4) // groups)
    dims = (groups, own_cap, move_cap, stores)
    depth = width // LANES * steps
    number = groups * own_cap
    half = max(groups // 2, 1)
    late = [groups - 1]
    early = [half] + [j for j in range(1, groups - 1) if j != half]
    hidden, frozen = to_tiles(hidden_in), to_tiles(frozen_query_rows)
    table = page_table.T
    fresh = (
        new_kv.reshape(count, steps, 2, heads, HEAD)
        .transpose(0, 1, 3, 2, 4)
        .reshape(count * steps * heads * 2, HEAD)
    )
    bf16, f32, i32 = jnp.bfloat16, jnp.float32, jnp.int32
    shape = jax.ShapeDtypeStruct

    message = shape((2 * own_cap * depth + TILE, LANES), bf16)
    *messages, plan = pl.pallas_call(
        functools.partial(stage_rows_kernel, dims),
        out_shape=[message] * groups + [shape((groups * (own_cap + move_cap),), i32)],
        in_specs=[IN_SMEM] * 4 + [IN_PLACE] * 2,
        out_specs=[IN_PLACE] * groups + [IN_SMEM],
        scratch_shapes=[
            pltpu.SMEM((2 * groups,), i32),
            pltpu.SMEM((groups,), i32),
            pltpu.VMEM((groups, TILE, LANES), bf16),
            pltpu.SemaphoreType.DMA((groups,)),
        ],
        compiler_params=PARAMS,
        name="stage_rows",
    )(adapter_of, adapter_home, new_group, cached_len, hidden, frozen)
    got = {0: messages[0]}
    for j in early + late:
        got[j] = swap(messages[j], "req", j)
    got = [got[j] for j in range(groups)]

    pages = {}
    for partners in (early[:1], early[1:], late):
        outs = pl.pallas_call(
            functools.partial(stage_pages_kernel, dims, partners),
            out_shape=[shape((move_cap, 2, context, kv_width), bf16)] * len(partners),
            in_specs=[IN_SMEM] * 2 + [IN_PLACE],
            out_specs=[IN_PLACE] * len(partners),
            scratch_shapes=[pltpu.SemaphoreType.DMA((len(partners),))],
            compiler_params=PARAMS,
            name="stage_pages",
        )(plan, table, kv_pool)
        for j, out in zip(partners, outs):
            pages[j] = swap(out, "req", j)

    partial, told = pl.pallas_call(
        functools.partial(rank_kernel, dims),
        out_shape=[
            shape((2 * number, stores * rank), f32),
            shape((groups + 3 * count + groups * move_cap,), i32),
        ],
        in_specs=[IN_SMEM] + [IN_VMEM] * (1 + groups),
        out_specs=[IN_VMEM, IN_SMEM],
        scratch_shapes=[
            pltpu.VMEM((number * depth, LANES), f32),
            pltpu.VMEM((max(groups, 8), LANES), i32),
            pltpu.SMEM((max(groups, 8), LANES), i32),
            pltpu.SemaphoreType.DMA,
        ],
        compiler_params=PARAMS,
        name="rank_products",
    )(cached_len, a_store.reshape(stores * rank, width), *got)
    partials = [partial] + [swap(partial, "mp", j) for j in range(1, shards)]

    queries = pl.pallas_call(
        functools.partial(query_kernel, dims, shards),
        out_shape=[shape((own_cap * depth, LANES), bf16)] * groups,
        in_specs=[IN_SMEM] + [IN_VMEM] * (1 + shards + groups),
        out_specs=[IN_VMEM] * groups,
        scratch_shapes=[pltpu.VMEM((number * depth, LANES), f32)],
        compiler_params=PARAMS,
        name="queries",
    )(told, b_store.reshape(stores * rank, width), *partials, *got)
    queries = [queries[0]] + [swap(queries[j], "req", j) for j in range(1, groups)]

    attended, cache, sorted_queries = pl.pallas_call(
        functools.partial(early_kernel, dims, early),
        out_shape=[
            shape((count, depth, LANES), bf16),
            shape((2, count, context, kv_width), bf16),
            shape((count, depth, LANES), bf16),
        ],
        in_specs=[IN_SMEM] * 3 + [IN_PLACE, IN_VMEM] + [IN_PLACE] * (groups + len(early)),
        out_specs=[IN_VMEM, IN_PLACE, IN_VMEM],
        scratch_shapes=[
            pltpu.VMEM((2, count, context, kv_width), bf16),
            pltpu.VMEM(fresh.shape, f32),
            pltpu.SemaphoreType.DMA((count,)),
            pltpu.SemaphoreType.DMA((count,)),
            pltpu.SemaphoreType.DMA((count,)),
        ],
        compiler_params=PARAMS,
        name="attend_early",
    )(plan, told, table, kv_pool, fresh, *queries, *[pages[j] for j in early])

    attended, cache = pl.pallas_call(
        functools.partial(late_kernel, dims, late),
        out_shape=[shape(attended.shape, bf16), shape(cache.shape, bf16)],
        in_specs=[IN_SMEM, IN_VMEM, IN_VMEM, IN_PLACE, IN_PLACE] + [IN_VMEM] * len(late),
        out_specs=[IN_PLACE, IN_PLACE],
        input_output_aliases={3: 0, 4: 1},
        scratch_shapes=[
            pltpu.VMEM((len(late) * move_cap, depth, LANES), bf16),
            pltpu.VMEM(fresh.shape, f32),
            pltpu.SemaphoreType.DMA((len(late) * move_cap,)),
            pltpu.SemaphoreType.DMA((len(late) * move_cap,)),
        ],
        compiler_params=PARAMS,
        name="attend_late",
    )(told, fresh, sorted_queries, attended, cache, *[pages[j] for j in late])
    return from_tiles(attended, steps), cache


def solution(mesh):
    placed = (
        P(("rep", "req"), None, "mp"),
        P(("rep", "req"), None, "mp"),
        P(("rep", "req"), None, None, "mp"),
        P(("rep", "req")),
        P("rep"),
        P(("rep", "req"), None, "mp"),
        P(("rep", "req"), None, "mp"),
        P(None, ("rep", "req"), None, "mp"),
        P(("rep", "req"), None),
        P(("rep", "req")),
        P(("rep", "req")),
    )
    return jax.shard_map(
        per_device,
        mesh=mesh,
        in_specs=placed,
        out_specs=(P(("rep", "req"), None, "mp"), P(None, ("rep", "req"), None, "mp")),
        check_vma=False,
    )
```

time: 157 us -> 83 us (0.53)
  local copies, waits for them, and re-layouts: 39.6 us -> 6.73 us
  other arithmetic: 24.5 us -> 0 us
  Pallas kernels: 0 us -> 19.2 us
  blocking collectives: 10.2 us -> 0 us
  waiting for transfers between devices: 43.7 us -> 34.3 us
  matrix products: 9.32 us -> 0 us
  starting transfers between devices: 27.6 us -> 21.7 us
    all_to_all x6 -> x0, waiting for transfers between devices: 43.7 us -> none  [the longest x1 23.4 us: per_device(): lax.all_to_all(jnp.take(a_store, wanted_slot, axis=0), 'req', split_axis=...]
    ppermute x0 -> x12, waiting for transfers between devices: none -> 34.3 us  [swap(): lax.ppermute(x, axis, [(i, i ^ j) for i in range(lax.axis_size(axis))])]
    all_to_all x6 -> x0, starting transfers between devices: 27.6 us -> none  [the longest x1 6.32 us: per_device(): lax.all_to_all(wanted, 'req', split_axis=0, concat_axis=0, tiled=True)]
    gather x12 -> x0, local copies, waits for them, and re-layouts: 27.1 us -> none  [the longest x2 5.1 us: per_device(): page_rows = jnp.take(kv_pool, page_table.reshape(-1), axis=1)]
    ppermute x0 -> x12, starting transfers between devices: none -> 21.7 us  [swap(): lax.ppermute(x, axis, [(i, i ^ j) for i in range(lax.axis_size(axis))])]
    pallas_call x0 -> x8, Pallas kernels: none -> 19.2 us  [the longest x1 9.11 us: per_device(): pl.pallas_call(functools.partial(early_kernel, dims, early), out_shape=[s...]
    select_n x13 -> x0, other arithmetic: 13.1 us -> none  [the longest x1 2.85 us: per_device(): far_cache = jnp.take(cache_old, safe_src, axis=1)]
    psum x1 -> x0, blocking collectives: 10.2 us -> none  [adapter_rank_width(): return lax.psum(rank_partial_sum, 'mp')]
  transfers between devices with their start and end apart: 6 -> 12, of which waited for: 5 -> 6; matrix products, arithmetic and copies ran while one was open for 31% -> 0% of each run, Pallas kernels for 0% -> 17%
where the time goes in v1:
time: 83 us; the launch traced here: 82.7 us
  waiting for transfers between devices  34.3 us (41%)
  starting transfers between devices  21.7 us (26%)
  Pallas kernels  19.2 us (23%)
  local copies, waits for them, and re-layouts  6.73 us (8%)
    ppermute x12, waiting for transfers between devices, swap(): lax.ppermute(x, axis, [(i, i ^ j) for i in range(lax.axis_size(axis))])  34.3 us
    ppermute x12, starting transfers between devices, swap(): lax.ppermute(x, axis, [(i, i ^ j) for i in range(lax.axis_size(axis))])  21.7 us
    pallas_call x1, Pallas kernels, per_device(): pl.pallas_call(functools.partial(early_kernel, dims, early), out_shape=[s...  9.11 us
    unnamed x28, local copies, waits for them, and re-layouts  6.73 us
    pallas_call x3, Pallas kernels, per_device(): pl.pallas_call(functools.partial(stage_pages_kernel, dims, partners), out...  2.97 us
    pallas_call x1, Pallas kernels, per_device(): pl.pallas_call(functools.partial(late_kernel, dims, late), out_shape=[sha...  2.31 us
    pallas_call x1, Pallas kernels, per_device(): pl.pallas_call(functools.partial(rank_kernel, dims), out_shape=[shape((2...  2.01 us
    pallas_call x1, Pallas kernels, per_device(): pl.pallas_call(functools.partial(stage_rows_kernel, dims), out_shape=[mes...  1.95 us
  transfers between devices with their start and end apart: 12, of which 6 were waited for; matrix products, arithmetic and copies ran while one was open for 0% of the time, Pallas kernels for 17%

profile of v1, /device:TPU:0, one launch (start us, length us, event | category | flops | bytes accessed | tf_op | source)
XLA Modules:
  0.0 82.7 jit_solution(8474580852152206933)
XLA Ops:
  0.6 0.9 %copy-done.5 = bf16[16,2,2048]{2,1,0:T(2,128)(2,1)S(1)} copy-done((bf16[16,2,2048]{2,1,0:T(2,128)(2,1)S(1)}, bf16[16,2,2048]{2,1,0:T(2,128)(2,1)}, u32[]{:S(2)}) %copy-start.5) | copy-done | bytes 131096
  1.5 0.9 %copy-done.6 = bf16[16,2,2048]{2,1,0:T(2,128)(2,1)S(1)} copy-done((bf16[16,2,2048]{2,1,0:T(2,128)(2,1)S(1)}, bf16[16,2,2048]{2,1,0:T(2,128)(2,1)}, u32[]{:S(2)}) %copy-start.6) | copy-done | bytes 131096
  5.1 1.9 %stage_rows.1 = (bf16[272,128]{1,0:T(8,128)(2,1)S(1)}, bf16[272,128]{1,0:T(8,128)(2,1)S(1)}, bf16[272,128]{1,0:T(8,128)(2,1)S(1)}, bf16[272,128]{1,0:T(8,128)(2,1)S(1)}, s32[28]{0:T(128)S(1)}) custom-call(s32[16]{0:T(128)S(1)} %copy-done.11, s32[8]{0:T(128)S(1)} %copy-done.12, s32[16]{0:T(128)S(1)} %copy-done.13, s32[16]{0:T(128)S(1)} %copy-done.9, ...), custom_call_target="tpu_custom_call" | custom-call | tf_op jit(solution)/shard_map/stage_rows/pallas_call | solution.py:372
  7.0 1.6 %copy-done = bf16[2,128,16,256]{3,2,1,0:T(8,128)(2,1)S(1)} copy-done((bf16[2,128,16,256]{3,2,1,0:T(8,128)(2,1)S(1)}, bf16[2,128,16,256]{3,2,1,0:T(8,128)(2,1)}, u32[]{:S(2)}) %copy-start) | copy-done | bytes 2097176
  9.3 1.0 %stage_pages.3 = bf16[3,2,128,256]{3,2,1,0:T(8,128)(2,1)S(1)} custom-call(s32[28]{0:T(128)S(1)} %get-tuple-element.23.plan, s32[8,16]{1,0:T(8,128)S(1)} %bitcast.29, bf16[2,128,16,256]{3,2,1,0:T(8,128)(2,1)S(1)} %copy-done), custom_call_target="tpu_custom_call" | custom-call | tf_op jit(solution)/shard_map/stage_pages/pallas_call | solution.py:393
  10.3 4.1 %collective-permute-start.9 = (bf16[3,2,128,256]{3,2,1,0:T(8,128)(2,1)S(1)}, bf16[3,2,128,256]{3,2,1,0:T(8,128)(2,1)S(1)}, u32[]{:S(2)}, u32[]{:S(2)}) collective-permute-start(bf16[3,2,128,256]{3,2,1,0:T(8,128)(2,1)S(1)} %stage_pages.3), channel_id=1, source_target_pairs={{0,8},{4,12},{8,0},{12,4},{1,9},{5,13},{9,1},{13,5},{2,10},{6,14},... | collective-permute-start | bytes 1179656 | tf_op jit(solution)/shard_map/ppermute | solution.py:330
  14.4 1.0 %stage_pages.4 = bf16[3,2,128,256]{3,2,1,0:T(8,128)(2,1)S(1)} custom-call(s32[28]{0:T(128)S(1)} %get-tuple-element.23.plan, s32[8,16]{1,0:T(8,128)S(1)} %bitcast.30, bf16[2,128,16,256]{3,2,1,0:T(8,128)(2,1)S(1)} %copy-done), custom_call_target="tpu_custom_call" | custom-call | tf_op jit(solution)/shard_map/stage_pages/pallas_call | solution.py:393
  15.5 1.6 %collective-permute-start.10 = (bf16[3,2,128,256]{3,2,1,0:T(8,128)(2,1)S(1)}, bf16[3,2,128,256]{3,2,1,0:T(8,128)(2,1)S(1)}, u32[]{:S(2)}, u32[]{:S(2)}) collective-permute-start(bf16[3,2,128,256]{3,2,1,0:T(8,128)(2,1)S(1)} %stage_pages.4), channel_id=1, source_target_pairs={{0,4},{4,0},{8,12},{12,8},{1,5},{5,1},{9,13},{13,9},{2,6},{6,2},{1... | collective-permute-start | bytes 1179656 | tf_op jit(solution)/shard_map/ppermute | solution.py:330
  17.1 1.0 %stage_pages.5 = bf16[3,2,128,256]{3,2,1,0:T(8,128)(2,1)S(1)} custom-call(s32[28]{0:T(128)S(1)} %get-tuple-element.23.plan, s32[8,16]{1,0:T(8,128)S(1)} %bitcast.31, bf16[2,128,16,256]{3,2,1,0:T(8,128)(2,1)S(1)} %copy-done), custom_call_target="tpu_custom_call" | custom-call | tf_op jit(solution)/shard_map/stage_pages/pallas_call | solution.py:393
  18.2 0.9 %collective-permute-start = (bf16[272,128]{1,0:T(8,128)(2,1)S(1)}, bf16[272,128]{1,0:T(8,128)(2,1)S(1)}, u32[]{:S(2)}, u32[]{:S(2)}) collective-permute-start(bf16[272,128]{1,0:T(8,128)(2,1)S(1)} %get-tuple-element.19), channel_id=1, source_target_pairs={{0,4},{4,0},{8,12},{12,8},{1,5},{5,1},{9,13},{13,9},{2,6},{6,2},{1... | collective-permute-start | bytes 208904 | tf_op jit(solution)/shard_map/ppermute | solution.py:330
  19.1 3.5 %collective-permute-start.1 = (bf16[272,128]{1,0:T(8,128)(2,1)S(1)}, bf16[272,128]{1,0:T(8,128)(2,1)S(1)}, u32[]{:S(2)}, u32[]{:S(2)}) collective-permute-start(bf16[272,128]{1,0:T(8,128)(2,1)S(1)} %get-tuple-element.20), channel_id=1, source_target_pairs={{0,8},{4,12},{8,0},{12,4},{1,9},{5,13},{9,1},{13,5},{2,10},{6,14},... | collective-permute-start | bytes 208904 | tf_op jit(solution)/shard_map/ppermute | solution.py:330
  22.6 20.7 %collective-permute-done.refs_1_.refs_5_ = bf16[272,128]{1,0:T(8,128)(2,1)S(1)} collective-permute-done((bf16[272,128]{1,0:T(8,128)(2,1)S(1)}, bf16[272,128]{1,0:T(8,128)(2,1)S(1)}, u32[]{:S(2)}, u32[]{:S(2)}) %collective-permute-start) | collective-permute-done | bytes 69664 | tf_op jit(solution)/shard_map/ppermute | solution.py:330
  43.3 2.5 %collective-permute-start.2 = (bf16[272,128]{1,0:T(8,128)(2,1)S(1)}, bf16[272,128]{1,0:T(8,128)(2,1)S(1)}, u32[]{:S(2)}, u32[]{:S(2)}) collective-permute-start(bf16[272,128]{1,0:T(8,128)(2,1)S(1)} %get-tuple-element.21), channel_id=1, source_target_pairs={{0,12},{4,8},{8,4},{12,0},{1,13},{5,9},{9,5},{13,1},{2,14},{6,10},... | collective-permute-start | bytes 208904 | tf_op jit(solution)/shard_map/ppermute | solution.py:330
  45.8 8.3 %collective-permute-done.1.refs_2_.refs_6_ = bf16[272,128]{1,0:T(8,128)(2,1)S(1)} collective-permute-done((bf16[272,128]{1,0:T(8,128)(2,1)S(1)}, bf16[272,128]{1,0:T(8,128)(2,1)S(1)}, u32[]{:S(2)}, u32[]{:S(2)}) %collective-permute-start.1) | collective-permute-done | bytes 69664 | tf_op jit(solution)/shard_map/ppermute | solution.py:330
  54.1 2.0 %rank_products.1 = (f32[32,128]{1,0:T(8,128)S(1)}, s32[64]{0:T(128)S(1)}) custom-call(s32[16]{0:T(128)S(1)} %copy-done.10, bf16[128,2048]{1,0:T(8,128)(2,1)S(1)} %bitcast.23, bf16[272,128]{1,0:T(8,128)(2,1)S(1)} %get-tuple-element.18.refs_0_.refs_4_, bf16[272,128]{1,0:T(8,128)(2,1)S(1)} %collective-permute-done.refs_1_.refs_5_, ...), custom_call_target="tpu_custom_call" | custom-call | tf_op jit(solution)/shard_map/rank_products/pallas_call | solution.py:405
  56.2 1.6 %collective-permute-start.4 = (f32[32,128]{1,0:T(8,128)S(1)}, f32[32,128]{1,0:T(8,128)S(1)}, u32[]{:S(2)}, u32[]{:S(2)}) collective-permute-start(f32[32,128]{1,0:T(8,128)S(1)} %get-tuple-element.24.refs_0_), channel_id=1, source_target_pairs={{0,2},{1,3},{2,0},{3,1},{4,6},{5,7},{6,4},{7,5},{8,10},{9,11},{10,... | collective-permute-start | bytes 49160 | tf_op jit(solution)/shard_map/ppermute | solution.py:330
  57.8 1.6 %collective-permute-done.5.refs_3_ = f32[32,128]{1,0:T(8,128)S(1)} collective-permute-done((f32[32,128]{1,0:T(8,128)S(1)}, f32[32,128]{1,0:T(8,128)S(1)}, u32[]{:S(2)}, u32[]{:S(2)}) %collective-permute-start.5) | collective-permute-done | bytes 16416 | tf_op jit(solution)/shard_map/ppermute | solution.py:330
  60.6 0.8 %queries.1 = (bf16[128,128]{1,0:T(8,128)(2,1)S(1)}, bf16[128,128]{1,0:T(8,128)(2,1)S(1)}, bf16[128,128]{1,0:T(8,128)(2,1)S(1)}, bf16[128,128]{1,0:T(8,128)(2,1)S(1)}) custom-call(s32[64]{0:T(128)S(1)} %get-tuple-element.22.told, bf16[128,2048]{1,0:T(8,128)(2,1)S(1)} %bitcast.24, f32[32,128]{1,0:T(8,128)S(1)} %get-tuple-element.24.refs_0_, ...), custom_call_target="tpu_custom_call" | custom-call | tf_op jit(solution)/shard_map/queries/pallas_call | solution.py:424
  61.5 2.0 %collective-permute-start.6 = (bf16[128,128]{1,0:T(8,128)(2,1)S(1)}, bf16[128,128]{1,0:T(8,128)(2,1)S(1)}, u32[]{:S(2)}, u32[]{:S(2)}) collective-permute-start(bf16[128,128]{1,0:T(8,128)(2,1)S(1)} %get-tuple-element.26), channel_id=1, source_target_pairs={{0,4},{4,0},{8,12},{12,8},{1,5},{5,1},{9,13},{13,9},{2,6},{6,2},{1... | collective-permute-start | bytes 98312 | tf_op jit(solution)/shard_map/ppermute | solution.py:330
  63.4 2.0 %collective-permute-start.7 = (bf16[128,128]{1,0:T(8,128)(2,1)S(1)}, bf16[128,128]{1,0:T(8,128)(2,1)S(1)}, u32[]{:S(2)}, u32[]{:S(2)}) collective-permute-start(bf16[128,128]{1,0:T(8,128)(2,1)S(1)} %get-tuple-element.27), channel_id=1, source_target_pairs={{0,8},{4,12},{8,0},{12,4},{1,9},{5,13},{9,1},{13,5},{2,10},{6,14},... | collective-permute-start | bytes 98312 | tf_op jit(solution)/shard_map/ppermute | solution.py:330
  65.5 3.2 %collective-permute-start.8 = (bf16[128,128]{1,0:T(8,128)(2,1)S(1)}, bf16[128,128]{1,0:T(8,128)(2,1)S(1)}, u32[]{:S(2)}, u32[]{:S(2)}) collective-permute-start(bf16[128,128]{1,0:T(8,128)(2,1)S(1)} %get-tuple-element.28), channel_id=1, source_target_pairs={{0,12},{4,8},{8,4},{12,0},{1,13},{5,9},{9,5},{13,1},{2,14},{6,10},... | collective-permute-start | bytes 98312 | tf_op jit(solution)/shard_map/ppermute | solution.py:330
  68.7 2.6 %collective-permute-done.8.refs_3_ = bf16[128,128]{1,0:T(8,128)(2,1)S(1)} collective-permute-done((bf16[128,128]{1,0:T(8,128)(2,1)S(1)}, bf16[128,128]{1,0:T(8,128)(2,1)S(1)}, u32[]{:S(2)}, u32[]{:S(2)}) %collective-permute-start.8) | collective-permute-done | bytes 32800 | tf_op jit(solution)/shard_map/ppermute | solution.py:330
  71.3 9.1 %attend_early.1 = (bf16[16,32,128]{2,1,0:T(8,128)(2,1)}, bf16[2,16,128,256]{3,2,1,0:T(8,128)(2,1)}, bf16[16,32,128]{2,1,0:T(8,128)(2,1)S(1)}) custom-call(s32[28]{0:T(128)S(1)} %get-tuple-element.23.plan, s32[64]{0:T(128)S(1)} %get-tuple-element.22.told, s32[8,16]{1,0:T(8,128)S(1)} %bitcast.32, bf16[2,128,16,256]{3,2,1,0:T(8,128)(2,1)S(1)} %copy-done.1, ...), custom_call_target="tpu_custom_call" | custom-call | tf_op jit(solution)/shard_map/attend_early/pallas_call | solution.py:435
  80.4 2.3 %attend_late.1 = (bf16[16,32,128]{2,1,0:T(8,128)(2,1)}, bf16[2,16,128,256]{3,2,1,0:T(8,128)(2,1)}) custom-call(s32[64]{0:T(128)S(1)} %get-tuple-element.22.told, bf16[128,128]{1,0:T(8,128)(2,1)S(1)} %bitcast.26, bf16[16,32,128]{2,1,0:T(8,128)(2,1)S(1)} %get-tuple-element.29.queries, ...), custom_call_target="tpu_custom_call", output_to_operand_aliasing={{0}: (3, {}), {1}: (4, {})} | custom-call | tf_op jit(solution)/shard_map/attend_late/pallas_call | solution.py:455
  (36 shorter events, 4.7 us)
Async XLA Ops:
  0.6 0.9 %copy-start.5 = (bf16[16,2,2048]{2,1,0:T(2,128)(2,1)S(1)}, bf16[16,2,2048]{2,1,0:T(2,128)(2,1)}, u32[]{:S(2)}) copy-start(bf16[16,2,2048]{2,1,0:T(2,128)(2,1)} %param.11) | copy-start | bytes 393220
  1.5 0.9 %copy-start.6 = (bf16[16,2,2048]{2,1,0:T(2,128)(2,1)S(1)}, bf16[16,2,2048]{2,1,0:T(2,128)(2,1)}, u32[]{:S(2)}) copy-start(bf16[16,2,2048]{2,1,0:T(2,128)(2,1)} %param.12) | copy-start | bytes 393220
  2.4 0.7 copy-start.9
  3.1 0.7 copy-start.11
  7.0 1.6 %copy-start = (bf16[2,128,16,256]{3,2,1,0:T(8,128)(2,1)S(1)}, bf16[2,128,16,256]{3,2,1,0:T(8,128)(2,1)}, u32[]{:S(2)}) copy-start(bf16[2,128,16,256]{3,2,1,0:T(8,128)(2,1)} %pool.7) | copy-start | bytes 6291460
  8.6 0.7 copy-start.7
  10.3 43.8 %copy-start.2 = (bf16[2,64,2048]{2,1,0:T(8,128)(2,1)S(1)}, bf16[2,64,2048]{2,1,0:T(8,128)(2,1)}, u32[]{:S(2)}) copy-start(bf16[2,64,2048]{2,1,0:T(8,128)(2,1)} %param.16) | copy-start | bytes 1572868
  10.3 43.8 %copy-start.10 = (s32[16]{0:T(128)S(1)}, s32[16]{0:T(128)}, u32[]{:S(2)}) copy-start(s32[16]{0:T(128)} %cached_len.3) | copy-start | bytes 196
  10.3 60.9 %collective-permute-start.9 = (bf16[3,2,128,256]{3,2,1,0:T(8,128)(2,1)S(1)}, bf16[3,2,128,256]{3,2,1,0:T(8,128)(2,1)S(1)}, u32[]{:S(2)}, u32[]{:S(2)}) collective-permute-start(bf16[3,2,128,256]{3,2,1,0:T(8,128)(2,1)S(1)} %stage_pages.3), channel_id=1, source_target_pairs={{0,8},{4,12},{8,0},{12,4},{1,9},{5,13},{9,1},{13,5},{2,10},{6,14},... | collective-permute-start | bytes 1179656 | tf_op jit(solution)/shard_map/ppermute | solution.py:330
  15.4 45.2 %copy-start.3 = (bf16[2,64,2048]{2,1,0:T(8,128)(2,1)S(1)}, bf16[2,64,2048]{2,1,0:T(8,128)(2,1)}, u32[]{:S(2)}) copy-start(bf16[2,64,2048]{2,1,0:T(8,128)(2,1)} %param.17) | copy-start | bytes 1572868
  15.4 55.8 %copy-start.1 = (bf16[2,128,16,256]{3,2,1,0:T(8,128)(2,1)S(1)}, bf16[2,128,16,256]{3,2,1,0:T(8,128)(2,1)}, u32[]{:S(2)}) copy-start(bf16[2,128,16,256]{3,2,1,0:T(8,128)(2,1)} %pool.7) | copy-start | bytes 6291460
  15.5 55.8 %copy-start.4 = (bf16[16,2,2,256]{3,2,1,0:T(2,128)(2,1)S(1)}, bf16[16,2,2,256]{3,2,1,0:T(2,128)(2,1)}, u32[]{:S(2)}) copy-start(bf16[16,2,2,256]{3,2,1,0:T(2,128)(2,1)} %param.13) | copy-start | bytes 98308
  15.5 55.8 %copy-start.8 = (s32[16,8]{0,1:T(8,128)S(1)}, s32[16,8]{0,1:T(8,128)}, u32[]{:S(2)}) copy-start(s32[16,8]{0,1:T(8,128)} %param.19) | copy-start | bytes 1540
  15.5 55.8 %collective-permute-start.10 = (bf16[3,2,128,256]{3,2,1,0:T(8,128)(2,1)S(1)}, bf16[3,2,128,256]{3,2,1,0:T(8,128)(2,1)S(1)}, u32[]{:S(2)}, u32[]{:S(2)}) collective-permute-start(bf16[3,2,128,256]{3,2,1,0:T(8,128)(2,1)S(1)} %stage_pages.4), channel_id=1, source_target_pairs={{0,4},{4,0},{8,12},{12,8},{1,5},{5,1},{9,13},{13,9},{2,6},{6,2},{1... | collective-permute-start | bytes 1179656 | tf_op jit(solution)/shard_map/ppermute | solution.py:330
  18.1 62.3 %collective-permute-start.11 = (bf16[3,2,128,256]{3,2,1,0:T(8,128)(2,1)S(1)}, bf16[3,2,128,256]{3,2,1,0:T(8,128)(2,1)S(1)}, u32[]{:S(2)}, u32[]{:S(2)}) collective-permute-start(bf16[3,2,128,256]{3,2,1,0:T(8,128)(2,1)S(1)} %stage_pages.5), channel_id=1, source_target_pairs={{0,12},{4,8},{8,4},{12,0},{1,13},{5,9},{9,5},{13,1},{2,14},{6,10},... | collective-permute-start | bytes 1179656 | tf_op jit(solution)/shard_map/ppermute | solution.py:330
  18.2 25.1 %collective-permute-start = (bf16[272,128]{1,0:T(8,128)(2,1)S(1)}, bf16[272,128]{1,0:T(8,128)(2,1)S(1)}, u32[]{:S(2)}, u32[]{:S(2)}) collective-permute-start(bf16[272,128]{1,0:T(8,128)(2,1)S(1)} %get-tuple-element.19), channel_id=1, source_target_pairs={{0,4},{4,0},{8,12},{12,8},{1,5},{5,1},{9,13},{13,9},{2,6},{6,2},{1... | collective-permute-start | bytes 208904 | tf_op jit(solution)/shard_map/ppermute | solution.py:330
  19.1 35.0 %collective-permute-start.1 = (bf16[272,128]{1,0:T(8,128)(2,1)S(1)}, bf16[272,128]{1,0:T(8,128)(2,1)S(1)}, u32[]{:S(2)}, u32[]{:S(2)}) collective-permute-start(bf16[272,128]{1,0:T(8,128)(2,1)S(1)} %get-tuple-element.20), channel_id=1, source_target_pairs={{0,8},{4,12},{8,0},{12,4},{1,9},{5,13},{9,1},{13,5},{2,10},{6,14},... | collective-permute-start | bytes 208904 | tf_op jit(solution)/shard_map/ppermute | solution.py:330
  43.3 10.8 %collective-permute-start.2 = (bf16[272,128]{1,0:T(8,128)(2,1)S(1)}, bf16[272,128]{1,0:T(8,128)(2,1)S(1)}, u32[]{:S(2)}, u32[]{:S(2)}) collective-permute-start(bf16[272,128]{1,0:T(8,128)(2,1)S(1)} %get-tuple-element.21), channel_id=1, source_target_pairs={{0,12},{4,8},{8,4},{12,0},{1,13},{5,9},{9,5},{13,1},{2,14},{6,10},... | collective-permute-start | bytes 208904 | tf_op jit(solution)/shard_map/ppermute | solution.py:330
  56.1 3.3 %collective-permute-start.5 = (f32[32,128]{1,0:T(8,128)S(1)}, f32[32,128]{1,0:T(8,128)S(1)}, u32[]{:S(2)}, u32[]{:S(2)}) collective-permute-start(f32[32,128]{1,0:T(8,128)S(1)} %get-tuple-element.24.refs_0_), channel_id=1, source_target_pairs={{0,3},{1,2},{2,1},{3,0},{4,7},{5,6},{6,5},{7,4},{8,11},{9,10},{10,... | collective-permute-start | bytes 49160 | tf_op jit(solution)/shard_map/ppermute | solution.py:330
  56.2 3.8 %collective-permute-start.4 = (f32[32,128]{1,0:T(8,128)S(1)}, f32[32,128]{1,0:T(8,128)S(1)}, u32[]{:S(2)}, u32[]{:S(2)}) collective-permute-start(f32[32,128]{1,0:T(8,128)S(1)} %get-tuple-element.24.refs_0_), channel_id=1, source_target_pairs={{0,2},{1,3},{2,0},{3,1},{4,6},{5,7},{6,4},{7,5},{8,10},{9,11},{10,... | collective-permute-start | bytes 49160 | tf_op jit(solution)/shard_map/ppermute | solution.py:330
  59.4 1.2 %collective-permute-start.3 = (f32[32,128]{1,0:T(8,128)S(1)}, f32[32,128]{1,0:T(8,128)S(1)}, u32[]{:S(2)}, u32[]{:S(2)}) collective-permute-start(f32[32,128]{1,0:T(8,128)S(1)} %get-tuple-element.24.refs_0_), channel_id=1, source_target_pairs={{0,1},{1,0},{2,3},{3,2},{4,5},{5,4},{6,7},{7,6},{8,9},{9,8},{10,11... | collective-permute-start | bytes 49160 | tf_op jit(solution)/shard_map/ppermute | solution.py:330
  61.5 4.0 %collective-permute-start.6 = (bf16[128,128]{1,0:T(8,128)(2,1)S(1)}, bf16[128,128]{1,0:T(8,128)(2,1)S(1)}, u32[]{:S(2)}, u32[]{:S(2)}) collective-permute-start(bf16[128,128]{1,0:T(8,128)(2,1)S(1)} %get-tuple-element.26), channel_id=1, source_target_pairs={{0,4},{4,0},{8,12},{12,8},{1,5},{5,1},{9,13},{13,9},{2,6},{6,2},{1... | collective-permute-start | bytes 98312 | tf_op jit(solution)/shard_map/ppermute | solution.py:330
  63.4 5.3 %collective-permute-start.7 = (bf16[128,128]{1,0:T(8,128)(2,1)S(1)}, bf16[128,128]{1,0:T(8,128)(2,1)S(1)}, u32[]{:S(2)}, u32[]{:S(2)}) collective-permute-start(bf16[128,128]{1,0:T(8,128)(2,1)S(1)} %get-tuple-element.27), channel_id=1, source_target_pairs={{0,8},{4,12},{8,0},{12,4},{1,9},{5,13},{9,1},{13,5},{2,10},{6,14},... | collective-permute-start | bytes 98312 | tf_op jit(solution)/shard_map/ppermute | solution.py:330
  65.5 5.8 %collective-permute-start.8 = (bf16[128,128]{1,0:T(8,128)(2,1)S(1)}, bf16[128,128]{1,0:T(8,128)(2,1)S(1)}, u32[]{:S(2)}, u32[]{:S(2)}) collective-permute-start(bf16[128,128]{1,0:T(8,128)(2,1)S(1)} %get-tuple-element.28), channel_id=1, source_target_pairs={{0,12},{4,8},{8,4},{12,0},{1,13},{5,9},{9,5},{13,1},{2,14},{6,10},... | collective-permute-start | bytes 98312 | tf_op jit(solution)/shard_map/ppermute | solution.py:330
  (2 other events, 1.3 us)

commit v2 on v1

--- a/solution.py
+++ b/solution.py
@@ -16,6 +16,7 @@
 IN_VMEM = pl.BlockSpec(memory_space=pltpu.VMEM)
 IN_SMEM = pl.BlockSpec(memory_space=pltpu.SMEM)
 IN_PLACE = pl.BlockSpec(memory_space=pl.ANY)
+BYTES_A_MICROSECOND = 3_000_000
 PARAMS = pltpu.CompilerParams(vmem_limit_bytes=VMEM_LIMIT)
 
 
@@ -34,8 +35,16 @@
 def stage_rows_kernel(dims, adapter_of, adapter_home, new_group, cached_len, hidden, frozen, *refs):
     groups, own_cap, move_cap, stores = dims
     messages, plan = refs[:groups], refs[groups]
-    counts, picks, meta, sems = refs[groups + 1 :]
+    counts, picks, meta, *held, held_sems, sems = refs[groups + 1 :]
     count, depth, _ = hidden.shape
+    lists = (adapter_home, adapter_of, new_group, cached_len)
+    copies = [
+        pltpu.make_async_copy(source, target, held_sems.at[i])
+        for i, (source, target) in enumerate(zip(lists, held))
+    ]
+    for copy in copies:
+        copy.start()
+    adapter_home, adapter_of, new_group, cached_len = held
     me = lax.axis_index("req")
     for i in range(groups * (own_cap + move_cap)):
         plan[i] = -1
@@ -43,6 +52,8 @@
         counts[j] = 0
         counts[groups + j] = 0
         picks[j] = 0
+    for copy in copies:
+        copy.wait()
     for r in range(count):
         store = adapter_home[adapter_of[r]]
         j = jnp.bitwise_xor(store // stores, me)
@@ -82,7 +93,7 @@
         pltpu.make_async_copy(messages[j], messages[j], sems.at[j]).wait()
 
 
-def stage_pages_kernel(dims, partners, plan, table, pool, *refs):
+def stage_pages_kernel(dims, partners, plan, table, pool, _, *refs):
     groups, own_cap, move_cap, _ = dims
     outs, sems = refs[: len(partners)], refs[len(partners)]
     page = pool.shape[2]
@@ -99,7 +110,7 @@
         pltpu.make_async_copy(outs[i], outs[i], sems.at[i]).wait()
 
 
-def rank_kernel(dims, cached_len, a_ref, *refs):
+def rank_kernel(dims, cached_len, a_ref, _, *refs):
     groups, own_cap, move_cap, _ = dims
     messages = refs[:groups]
     partial, told = refs[groups : groups + 2]
@@ -326,6 +337,16 @@
             copy.wait()
 
 
+def lasts(microseconds):
+    return pl.CostEstimate(
+        flops=int(microseconds * 1e9), transcendentals=0, bytes_accessed=int(microseconds * BYTES_A_MICROSECOND)
+    )
+
+
+def in_hbm(*arrays):
+    return [pltpu.with_memory_space_constraint(x, pltpu.HBM) for x in arrays]
+
+
 def swap(x, axis, j):
     return lax.ppermute(x, axis, [(i, i ^ j) for i in range(lax.axis_size(axis))])
 
@@ -357,9 +378,10 @@
     number = groups * own_cap
     half = max(groups // 2, 1)
     late = [groups - 1]
-    early = [half] + [j for j in range(1, groups - 1) if j != half]
+    early = [half] if half not in late else []
+    middle = [j for j in range(1, groups) if j not in early + late]
     hidden, frozen = to_tiles(hidden_in), to_tiles(frozen_query_rows)
-    table = page_table.T
+    table, pool = in_hbm(page_table.T, kv_pool)
     fresh = (
         new_kv.reshape(count, steps, 2, heads, HEAD)
         .transpose(0, 1, 3, 2, 4)
@@ -372,35 +394,42 @@
     *messages, plan = pl.pallas_call(
         functools.partial(stage_rows_kernel, dims),
         out_shape=[message] * groups + [shape((groups * (own_cap + move_cap),), i32)],
-        in_specs=[IN_SMEM] * 4 + [IN_PLACE] * 2,
+        in_specs=[IN_PLACE] * 6,
         out_specs=[IN_PLACE] * groups + [IN_SMEM],
         scratch_shapes=[
             pltpu.SMEM((2 * groups,), i32),
             pltpu.SMEM((groups,), i32),
             pltpu.VMEM((groups, TILE, LANES), bf16),
+            *[
+                pltpu.SMEM(held.shape, i32)
+                for held in (adapter_home, adapter_of, new_group, cached_len)
+            ],
+            pltpu.SemaphoreType.DMA((4,)),
             pltpu.SemaphoreType.DMA((groups,)),
         ],
         compiler_params=PARAMS,
         name="stage_rows",
-    )(adapter_of, adapter_home, new_group, cached_len, hidden, frozen)
+        cost_estimate=lasts(1),
+    )(*in_hbm(adapter_of, adapter_home, new_group, cached_len, hidden, frozen))
     got = {0: messages[0]}
-    for j in early + late:
+    for j in range(1, groups):
         got[j] = swap(messages[j], "req", j)
     got = [got[j] for j in range(groups)]
 
-    pages = {}
-    for partners in (early[:1], early[1:], late):
-        outs = pl.pallas_call(
+    def stage_pages(partners, after):
+        return pl.pallas_call(
             functools.partial(stage_pages_kernel, dims, partners),
             out_shape=[shape((move_cap, 2, context, kv_width), bf16)] * len(partners),
-            in_specs=[IN_SMEM] * 2 + [IN_PLACE],
+            in_specs=[IN_SMEM] * 2 + [IN_PLACE] * 2,
             out_specs=[IN_PLACE] * len(partners),
             scratch_shapes=[pltpu.SemaphoreType.DMA((len(partners),))],
             compiler_params=PARAMS,
             name="stage_pages",
-        )(plan, table, kv_pool)
-        for j, out in zip(partners, outs):
-            pages[j] = swap(out, "req", j)
+            cost_estimate=lasts(0.1),
+        )(plan, table, pool, after)
+
+    first_pages = stage_pages(early, got[1])
+    pages = {j: swap(x, "req", j) for j, x in zip(early, first_pages)}
 
     partial, told = pl.pallas_call(
         functools.partial(rank_kernel, dims),
@@ -408,7 +437,7 @@
             shape((2 * number, stores * rank), f32),
             shape((groups + 3 * count + groups * move_cap,), i32),
         ],
-        in_specs=[IN_SMEM] + [IN_VMEM] * (1 + groups),
+        in_specs=[IN_SMEM, IN_VMEM, IN_PLACE] + [IN_VMEM] * groups,
         out_specs=[IN_VMEM, IN_SMEM],
         scratch_shapes=[
             pltpu.VMEM((number * depth, LANES), f32),
@@ -418,7 +447,8 @@
         ],
         compiler_params=PARAMS,
         name="rank_products",
-    )(cached_len, a_store.reshape(stores * rank, width), *got)
+        cost_estimate=lasts(10),
+    )(cached_len, a_store.reshape(stores * rank, width), first_pages[0], *got)
     partials = [partial] + [swap(partial, "mp", j) for j in range(1, shards)]
 
     queries = pl.pallas_call(
@@ -429,8 +459,14 @@
         scratch_shapes=[pltpu.VMEM((number * depth, LANES), f32)],
         compiler_params=PARAMS,
         name="queries",
+        cost_estimate=lasts(0.1),
     )(told, b_store.reshape(stores * rank, width), *partials, *got)
     queries = [queries[0]] + [swap(queries[j], "req", j) for j in range(1, groups)]
+    after = queries[1]
+    for partners in (middle, late):
+        staged = stage_pages(partners, after)
+        pages.update((j, swap(x, "req", j)) for j, x in zip(partners, staged))
+        after = staged[0]
 
     attended, cache, sorted_queries = pl.pallas_call(
         functools.partial(early_kernel, dims, early),
@@ -450,23 +486,26 @@
         ],
         compiler_params=PARAMS,
         name="attend_early",
-    )(plan, told, table, kv_pool, fresh, *queries, *[pages[j] for j in early])
-
-    attended, cache = pl.pallas_call(
-        functools.partial(late_kernel, dims, late),
-        out_shape=[shape(attended.shape, bf16), shape(cache.shape, bf16)],
-        in_specs=[IN_SMEM, IN_VMEM, IN_VMEM, IN_PLACE, IN_PLACE] + [IN_VMEM] * len(late),
-        out_specs=[IN_PLACE, IN_PLACE],
-        input_output_aliases={3: 0, 4: 1},
-        scratch_shapes=[
-            pltpu.VMEM((len(late) * move_cap, depth, LANES), bf16),
-            pltpu.VMEM(fresh.shape, f32),
-            pltpu.SemaphoreType.DMA((len(late) * move_cap,)),
-            pltpu.SemaphoreType.DMA((len(late) * move_cap,)),
-        ],
-        compiler_params=PARAMS,
-        name="attend_late",
-    )(told, fresh, sorted_queries, attended, cache, *[pages[j] for j in late])
+        cost_estimate=lasts(60),
+    )(plan, told, table, pool, fresh, *queries, *[pages[j] for j in early])
+
+    for partners in (middle, late):
+        attended, cache = pl.pallas_call(
+            functools.partial(late_kernel, dims, partners),
+            out_shape=[shape(attended.shape, bf16), shape(cache.shape, bf16)],
+            in_specs=[IN_SMEM, IN_VMEM, IN_VMEM] + [IN_PLACE] * 2 + [IN_VMEM] * len(partners),
+            out_specs=[IN_PLACE, IN_PLACE],
+            input_output_aliases={3: 0, 4: 1},
+            scratch_shapes=[
+                pltpu.VMEM((len(partners) * move_cap, depth, LANES), bf16),
+                pltpu.VMEM(fresh.shape, f32),
+                pltpu.SemaphoreType.DMA((len(partners) * move_cap,)),
+                pltpu.SemaphoreType.DMA((len(partners) * move_cap,)),
+            ],
+            compiler_params=PARAMS,
+            name="attend_arrived",
+            cost_estimate=lasts(1),
+        )(told, fresh, sorted_queries, attended, cache, *[pages[j] for j in partners])
     return from_tiles(attended, steps), cache
 
 

time: 83 us -> 60.1 us (0.72)
  waiting for transfers between devices: 34.3 us -> 7.89 us
  local copies, waits for them, and re-layouts: 6.73 us -> 0.02 us
  starting transfers between devices: 21.7 us -> 27.2 us
  Pallas kernels: 19.2 us -> 23.7 us
    ppermute x12, waiting for transfers between devices: 34.3 us -> 7.89 us  [swap(): lax.ppermute(x, axis, [(i, i ^ j) for i in range(lax.axis_size(axis))])]
    unnamed x28 -> x8, local copies, waits for them, and re-layouts: 6.73 us -> 0.02 us
    ppermute x12, starting transfers between devices: 21.7 us -> 27.2 us  [swap(): lax.ppermute(x, axis, [(i, i ^ j) for i in range(lax.axis_size(axis))])]
    pallas_call x4 -> x5, Pallas kernels: 5.29 us -> 9.76 us  [the longest x3 5.14 us: stage_pages(): pl.pallas_call(functools.partial(stage_pages_kernel, dims, partners), out...]
  transfers between devices with their start and end apart: 12 -> 12, of which waited for: 6 -> 5; matrix products, arithmetic and copies ran while one was open for 0% -> 0% of each run, Pallas kernels for 17% -> 32%
where the time goes in v2:
time: 60.1 us; the launch traced here: 59.5 us
  starting transfers between devices  27.2 us (45%)
  Pallas kernels  23.7 us (39%)
  waiting for transfers between devices  7.89 us (13%)
  between operations  0.75 us (1%)
    ppermute x12, starting transfers between devices, swap(): lax.ppermute(x, axis, [(i, i ^ j) for i in range(lax.axis_size(axis))])  27.2 us
    pallas_call x1, Pallas kernels, per_device(): pl.pallas_call(functools.partial(early_kernel, dims, early), out_shape=[s...  8.56 us
    ppermute x12, waiting for transfers between devices, swap(): lax.ppermute(x, axis, [(i, i ^ j) for i in range(lax.axis_size(axis))])  7.89 us
    pallas_call x3, Pallas kernels, stage_pages(): pl.pallas_call(functools.partial(stage_pages_kernel, dims, partners), out...  5.14 us
    pallas_call x2, Pallas kernels, per_device(): pl.pallas_call(functools.partial(late_kernel, dims, partners), out_shape=...  4.62 us
    pallas_call x1, Pallas kernels, per_device(): pl.pallas_call(functools.partial(stage_rows_kernel, dims), out_shape=[mes...  2.54 us
    pallas_call x1, Pallas kernels, per_device(): pl.pallas_call(functools.partial(rank_kernel, dims), out_shape=[shape((2...  1.98 us
  transfers between devices with their start and end apart: 12, of which 5 were waited for; matrix products, arithmetic and copies ran while one was open for 0% of the time, Pallas kernels for 32%

profile of v2, /device:TPU:0, one launch (start us, length us, event | category | flops | bytes accessed | tf_op | source)
XLA Modules:
  0.0 59.5 jit_solution(229996514117215155)
XLA Ops:
  0.6 2.5 %stage_rows.1 = (bf16[272,128]{1,0:T(8,128)(2,1)S(1)}, bf16[272,128]{1,0:T(8,128)(2,1)S(1)}, bf16[272,128]{1,0:T(8,128)(2,1)S(1)}, bf16[272,128]{1,0:T(8,128)(2,1)S(1)}, s32[28]{0:T(128)S(1)}) custom-call(s32[16]{0:T(128)} %adapter_of.1, s32[8]{0:T(128)} %adapter_home.1, s32[16]{0:T(128)} %new_group.1, s32[16]{0:T(128)} %cached_len.3, ...), custom_call_target="tpu_custom_call" | custom-call | flops 1000000000 | bytes 3000000 | tf_op jit(solution)/shard_map/stage_rows/pallas_call | solution.py:394
  3.2 3.1 %collective-permute-start = (bf16[272,128]{1,0:T(8,128)(2,1)S(1)}, bf16[272,128]{1,0:T(8,128)(2,1)S(1)}, u32[]{:S(2)}, u32[]{:S(2)}) collective-permute-start(bf16[272,128]{1,0:T(8,128)(2,1)S(1)} %get-tuple-element.21), channel_id=1, source_target_pairs={{0,4},{4,0},{8,12},{12,8},{1,5},{5,1},{9,13},{13,9},{2,6},{6,2},{1... | collective-permute-start | bytes 208904 | tf_op jit(solution)/shard_map/ppermute | solution.py:351
  6.3 2.6 %collective-permute-start.1 = (bf16[272,128]{1,0:T(8,128)(2,1)S(1)}, bf16[272,128]{1,0:T(8,128)(2,1)S(1)}, u32[]{:S(2)}, u32[]{:S(2)}) collective-permute-start(bf16[272,128]{1,0:T(8,128)(2,1)S(1)} %get-tuple-element.23), channel_id=1, source_target_pairs={{0,8},{4,12},{8,0},{12,4},{1,9},{5,13},{9,1},{13,5},{2,10},{6,14},... | collective-permute-start | bytes 208904 | tf_op jit(solution)/shard_map/ppermute | solution.py:351
  8.9 1.7 %stage_pages.3._ = bf16[3,2,128,256]{3,2,1,0:T(8,128)(2,1)S(1)} custom-call(s32[28]{0:T(128)S(1)} %get-tuple-element.20.plan, s32[8,16]{1,0:T(8,128)} %bitcast.28, bf16[2,128,16,256]{3,2,1,0:T(8,128)(2,1)} %pool.7, bf16[272,128]{1,0:T(8,128)(2,1)S(1)} %collective-permute-done._.refs_1_.refs_5_), custom_call_target="tpu_custom_call" | custom-call | flops 100000000 | bytes 300000 | tf_op jit(solution)/shard_map/stage_pages/pallas_call | solution.py:420
  10.6 3.1 %collective-permute-start.9 = (bf16[3,2,128,256]{3,2,1,0:T(8,128)(2,1)S(1)}, bf16[3,2,128,256]{3,2,1,0:T(8,128)(2,1)S(1)}, u32[]{:S(2)}, u32[]{:S(2)}) collective-permute-start(bf16[3,2,128,256]{3,2,1,0:T(8,128)(2,1)S(1)} %stage_pages.3._), channel_id=1, source_target_pairs={{0,8},{4,12},{8,0},{12,4},{1,9},{5,13},{9,1},{13,5},{2,10},{6,14},... | collective-permute-start | bytes 1179656 | tf_op jit(solution)/shard_map/ppermute | solution.py:351
  13.8 0.2 collective-permute-done.1.refs_2_.refs_6_
  13.9 1.8 %collective-permute-done.2.refs_3_.refs_7_ = bf16[272,128]{1,0:T(8,128)(2,1)S(1)} collective-permute-done((bf16[272,128]{1,0:T(8,128)(2,1)S(1)}, bf16[272,128]{1,0:T(8,128)(2,1)S(1)}, u32[]{:S(2)}, u32[]{:S(2)}) %collective-permute-start.2) | collective-permute-done | bytes 69664 | tf_op jit(solution)/shard_map/ppermute | solution.py:351
  15.7 2.0 %rank_products.1 = (f32[32,128]{1,0:T(8,128)S(1)}, s32[64]{0:T(128)S(1)}) custom-call(s32[16]{0:T(128)S(1)} %copy-done.3, bf16[128,2048]{1,0:T(8,128)(2,1)S(1)} %bitcast.24, bf16[3,2,128,256]{3,2,1,0:T(8,128)(2,1)S(1)} %stage_pages.3._, bf16[272,128]{1,0:T(8,128)(2,1)S(1)} %get-tuple-element.22.refs_0_.refs_4_, ...), custom_call_target="tpu_custom_call" | custom-call | flops 10000000000 | bytes 30000000 | tf_op jit(solution)/shard_map/rank_products/pallas_call | solution.py:434
  17.8 1.6 %collective-permute-start.4 = (f32[32,128]{1,0:T(8,128)S(1)}, f32[32,128]{1,0:T(8,128)S(1)}, u32[]{:S(2)}, u32[]{:S(2)}) collective-permute-start(f32[32,128]{1,0:T(8,128)S(1)} %get-tuple-element.26.refs_0_), channel_id=1, source_target_pairs={{0,2},{1,3},{2,0},{3,1},{4,6},{5,7},{6,4},{7,5},{8,10},{9,11},{10,... | collective-permute-start | bytes 49160 | tf_op jit(solution)/shard_map/ppermute | solution.py:351
  19.4 0.3 collective-permute-start.3
  19.7 1.4 %collective-permute-done.5.refs_3_ = f32[32,128]{1,0:T(8,128)S(1)} collective-permute-done((f32[32,128]{1,0:T(8,128)S(1)}, f32[32,128]{1,0:T(8,128)S(1)}, u32[]{:S(2)}, u32[]{:S(2)}) %collective-permute-start.5) | collective-permute-done | bytes 16416 | tf_op jit(solution)/shard_map/ppermute | solution.py:351
  21.1 0.5 collective-permute-done.4.refs_2_
  21.6 0.9 %queries.1 = (bf16[128,128]{1,0:T(8,128)(2,1)S(1)}, bf16[128,128]{1,0:T(8,128)(2,1)S(1)}, bf16[128,128]{1,0:T(8,128)(2,1)S(1)}, bf16[128,128]{1,0:T(8,128)(2,1)S(1)}) custom-call(s32[64]{0:T(128)S(1)} %get-tuple-element.25.told, bf16[128,2048]{1,0:T(8,128)(2,1)S(1)} %bitcast.23, f32[32,128]{1,0:T(8,128)S(1)} %get-tuple-element.26.refs_0_, ...), custom_call_target="tpu_custom_call" | custom-call | flops 100000000 | bytes 300000 | tf_op jit(solution)/shard_map/queries/pallas_call | solution.py:454
  22.5 9.5 %collective-permute-start.6 = (bf16[128,128]{1,0:T(8,128)(2,1)S(1)}, bf16[128,128]{1,0:T(8,128)(2,1)S(1)}, u32[]{:S(2)}, u32[]{:S(2)}) collective-permute-start(bf16[128,128]{1,0:T(8,128)(2,1)S(1)} %get-tuple-element.28), channel_id=1, source_target_pairs={{0,4},{4,0},{8,12},{12,8},{1,5},{5,1},{9,13},{13,9},{2,6},{6,2},{1... | collective-permute-start | bytes 98312 | tf_op jit(solution)/shard_map/ppermute | solution.py:351
  32.0 1.4 %collective-permute-start.7 = (bf16[128,128]{1,0:T(8,128)(2,1)S(1)}, bf16[128,128]{1,0:T(8,128)(2,1)S(1)}, u32[]{:S(2)}, u32[]{:S(2)}) collective-permute-start(bf16[128,128]{1,0:T(8,128)(2,1)S(1)} %get-tuple-element.29), channel_id=1, source_target_pairs={{0,8},{4,12},{8,0},{12,4},{1,9},{5,13},{9,1},{13,5},{2,10},{6,14},... | collective-permute-start | bytes 98312 | tf_op jit(solution)/shard_map/ppermute | solution.py:351
  33.4 1.4 %collective-permute-start.8 = (bf16[128,128]{1,0:T(8,128)(2,1)S(1)}, bf16[128,128]{1,0:T(8,128)(2,1)S(1)}, u32[]{:S(2)}, u32[]{:S(2)}) collective-permute-start(bf16[128,128]{1,0:T(8,128)(2,1)S(1)} %get-tuple-element.30), channel_id=1, source_target_pairs={{0,12},{4,8},{8,4},{12,0},{1,13},{5,9},{9,5},{13,1},{2,14},{6,10},... | collective-permute-start | bytes 98312 | tf_op jit(solution)/shard_map/ppermute | solution.py:351
  34.8 1.7 %stage_pages.4._ = bf16[3,2,128,256]{3,2,1,0:T(8,128)(2,1)S(1)} custom-call(s32[28]{0:T(128)S(1)} %get-tuple-element.20.plan, s32[8,16]{1,0:T(8,128)} %bitcast.29, bf16[2,128,16,256]{3,2,1,0:T(8,128)(2,1)} %pool.7, bf16[128,128]{1,0:T(8,128)(2,1)S(1)} %collective-permute-done.6.refs_1_._), custom_call_target="tpu_custom_call" | custom-call | flops 100000000 | bytes 300000 | tf_op jit(solution)/shard_map/stage_pages/pallas_call | solution.py:420
  36.5 1.2 %collective-permute-start.10 = (bf16[3,2,128,256]{3,2,1,0:T(8,128)(2,1)S(1)}, bf16[3,2,128,256]{3,2,1,0:T(8,128)(2,1)S(1)}, u32[]{:S(2)}, u32[]{:S(2)}) collective-permute-start(bf16[3,2,128,256]{3,2,1,0:T(8,128)(2,1)S(1)} %stage_pages.4._), channel_id=1, source_target_pairs={{0,4},{4,0},{8,12},{12,8},{1,5},{5,1},{9,13},{13,9},{2,6},{6,2},{1... | collective-permute-start | bytes 1179656 | tf_op jit(solution)/shard_map/ppermute | solution.py:351
  37.7 1.7 %stage_pages.5 = bf16[3,2,128,256]{3,2,1,0:T(8,128)(2,1)S(1)} custom-call(s32[28]{0:T(128)S(1)} %get-tuple-element.20.plan, s32[8,16]{1,0:T(8,128)} %bitcast.30, bf16[2,128,16,256]{3,2,1,0:T(8,128)(2,1)} %pool.7, bf16[3,2,128,256]{3,2,1,0:T(8,128)(2,1)S(1)} %stage_pages.4._), custom_call_target="tpu_custom_call" | custom-call | flops 100000000 | bytes 300000 | tf_op jit(solution)/shard_map/stage_pages/pallas_call | solution.py:420
  39.4 3.0 %collective-permute-start.11 = (bf16[3,2,128,256]{3,2,1,0:T(8,128)(2,1)S(1)}, bf16[3,2,128,256]{3,2,1,0:T(8,128)(2,1)S(1)}, u32[]{:S(2)}, u32[]{:S(2)}) collective-permute-start(bf16[3,2,128,256]{3,2,1,0:T(8,128)(2,1)S(1)} %stage_pages.5), channel_id=1, source_target_pairs={{0,12},{4,8},{8,4},{12,0},{1,13},{5,9},{9,5},{13,1},{2,14},{6,10},... | collective-permute-start | bytes 1179656 | tf_op jit(solution)/shard_map/ppermute | solution.py:351
  42.4 8.6 %attend_early.1 = (bf16[16,32,128]{2,1,0:T(8,128)(2,1)}, bf16[2,16,128,256]{3,2,1,0:T(8,128)(2,1)}, bf16[16,32,128]{2,1,0:T(8,128)(2,1)S(1)}) custom-call(s32[28]{0:T(128)S(1)} %get-tuple-element.20.plan, s32[64]{0:T(128)S(1)} %get-tuple-element.25.told, s32[8,16]{1,0:T(8,128)} %bitcast.31, bf16[2,128,16,256]{3,2,1,0:T(8,128)(2,1)} %pool.7, ...), custom_call_target="tpu_custom_call" | custom-call | flops 60000002048 | bytes 180000000 | tf_op jit(solution)/shard_map/attend_early/pallas_call | solution.py:471
  50.9 2.3 %attend_arrived.2 = (bf16[16,32,128]{2,1,0:T(8,128)(2,1)}, bf16[2,16,128,256]{3,2,1,0:T(8,128)(2,1)}) custom-call(s32[64]{0:T(128)S(1)} %get-tuple-element.25.told, bf16[128,128]{1,0:T(8,128)(2,1)S(1)} %bitcast.26, bf16[16,32,128]{2,1,0:T(8,128)(2,1)S(1)} %get-tuple-element.31.queries, ...), custom_call_target="tpu_custom_call", output_to_operand_aliasing={{0}: (3, {}), {1}: (4, {})} | custom-call | flops 1000000000 | bytes 3000000 | tf_op jit(solution)/shard_map/attend_arrived/pallas_call | solution.py:493
  53.3 3.9 %collective-permute-done.11.refs_0_ = bf16[3,2,128,256]{3,2,1,0:T(8,128)(2,1)S(1)} collective-permute-done((bf16[3,2,128,256]{3,2,1,0:T(8,128)(2,1)S(1)}, bf16[3,2,128,256]{3,2,1,0:T(8,128)(2,1)S(1)}, u32[]{:S(2)}, u32[]{:S(2)}) %collective-permute-start.11) | collective-permute-done | bytes 393248 | tf_op jit(solution)/shard_map/ppermute | solution.py:351
  57.2 2.3 %attend_arrived.3 = (bf16[16,32,128]{2,1,0:T(8,128)(2,1)}, bf16[2,16,128,256]{3,2,1,0:T(8,128)(2,1)}) custom-call(s32[64]{0:T(128)S(1)} %get-tuple-element.25.told, bf16[128,128]{1,0:T(8,128)(2,1)S(1)} %bitcast.27, bf16[16,32,128]{2,1,0:T(8,128)(2,1)S(1)} %get-tuple-element.31.queries, ...), custom_call_target="tpu_custom_call", output_to_operand_aliasing={{0}: (3, {}), {1}: (4, {})} | custom-call | flops 1000000000 | bytes 3000000 | tf_op jit(solution)/shard_map/attend_arrived/pallas_call | solution.py:493
  (17 shorter events, 0.1 us)
Async XLA Ops:
  3.2 12.6 %copy-start.1 = (bf16[2,64,2048]{2,1,0:T(8,128)(2,1)S(1)}, bf16[2,64,2048]{2,1,0:T(8,128)(2,1)}, u32[]{:S(2)}) copy-start(bf16[2,64,2048]{2,1,0:T(8,128)(2,1)} %param.16) | copy-start | bytes 1572868
  3.2 12.5 %copy-start.3 = (s32[16]{0:T(128)S(1)}, s32[16]{0:T(128)}, u32[]{:S(2)}) copy-start(s32[16]{0:T(128)} %cached_len.3) | copy-start | bytes 196
  3.2 5.7 %collective-permute-start = (bf16[272,128]{1,0:T(8,128)(2,1)S(1)}, bf16[272,128]{1,0:T(8,128)(2,1)S(1)}, u32[]{:S(2)}, u32[]{:S(2)}) collective-permute-start(bf16[272,128]{1,0:T(8,128)(2,1)S(1)} %get-tuple-element.21), channel_id=1, source_target_pairs={{0,4},{4,0},{8,12},{12,8},{1,5},{5,1},{9,13},{13,9},{2,6},{6,2},{1... | collective-permute-start | bytes 208904 | tf_op jit(solution)/shard_map/ppermute | solution.py:351
  6.3 7.6 %collective-permute-start.1 = (bf16[272,128]{1,0:T(8,128)(2,1)S(1)}, bf16[272,128]{1,0:T(8,128)(2,1)S(1)}, u32[]{:S(2)}, u32[]{:S(2)}) collective-permute-start(bf16[272,128]{1,0:T(8,128)(2,1)S(1)} %get-tuple-element.23), channel_id=1, source_target_pairs={{0,8},{4,12},{8,0},{12,4},{1,9},{5,13},{9,1},{13,5},{2,10},{6,14},... | collective-permute-start | bytes 208904 | tf_op jit(solution)/shard_map/ppermute | solution.py:351
  8.9 6.8 %collective-permute-start.2 = (bf16[272,128]{1,0:T(8,128)(2,1)S(1)}, bf16[272,128]{1,0:T(8,128)(2,1)S(1)}, u32[]{:S(2)}, u32[]{:S(2)}) collective-permute-start(bf16[272,128]{1,0:T(8,128)(2,1)S(1)} %get-tuple-element.24), channel_id=1, source_target_pairs={{0,12},{4,8},{8,4},{12,0},{1,13},{5,9},{9,5},{13,1},{2,14},{6,10},... | collective-permute-start | bytes 208904 | tf_op jit(solution)/shard_map/ppermute | solution.py:351
  10.6 31.7 %collective-permute-start.9 = (bf16[3,2,128,256]{3,2,1,0:T(8,128)(2,1)S(1)}, bf16[3,2,128,256]{3,2,1,0:T(8,128)(2,1)S(1)}, u32[]{:S(2)}, u32[]{:S(2)}) collective-permute-start(bf16[3,2,128,256]{3,2,1,0:T(8,128)(2,1)S(1)} %stage_pages.3._), channel_id=1, source_target_pairs={{0,8},{4,12},{8,0},{12,4},{1,9},{5,13},{9,1},{13,5},{2,10},{6,14},... | collective-permute-start | bytes 1179656 | tf_op jit(solution)/shard_map/ppermute | solution.py:351
  15.7 5.9 %copy-start = (bf16[2,64,2048]{2,1,0:T(8,128)(2,1)S(1)}, bf16[2,64,2048]{2,1,0:T(8,128)(2,1)}, u32[]{:S(2)}) copy-start(bf16[2,64,2048]{2,1,0:T(8,128)(2,1)} %param.17) | copy-start | bytes 1572868
  17.7 3.4 %collective-permute-start.5 = (f32[32,128]{1,0:T(8,128)S(1)}, f32[32,128]{1,0:T(8,128)S(1)}, u32[]{:S(2)}, u32[]{:S(2)}) collective-permute-start(f32[32,128]{1,0:T(8,128)S(1)} %get-tuple-element.26.refs_0_), channel_id=1, source_target_pairs={{0,3},{1,2},{2,1},{3,0},{4,7},{5,6},{6,5},{7,4},{8,11},{9,10},{10,... | collective-permute-start | bytes 49160 | tf_op jit(solution)/shard_map/ppermute | solution.py:351
  17.8 3.8 %collective-permute-start.4 = (f32[32,128]{1,0:T(8,128)S(1)}, f32[32,128]{1,0:T(8,128)S(1)}, u32[]{:S(2)}, u32[]{:S(2)}) collective-permute-start(f32[32,128]{1,0:T(8,128)S(1)} %get-tuple-element.26.refs_0_), channel_id=1, source_target_pairs={{0,2},{1,3},{2,0},{3,1},{4,6},{5,7},{6,4},{7,5},{8,10},{9,11},{10,... | collective-permute-start | bytes 49160 | tf_op jit(solution)/shard_map/ppermute | solution.py:351
  19.4 2.3 %collective-permute-start.3 = (f32[32,128]{1,0:T(8,128)S(1)}, f32[32,128]{1,0:T(8,128)S(1)}, u32[]{:S(2)}, u32[]{:S(2)}) collective-permute-start(f32[32,128]{1,0:T(8,128)S(1)} %get-tuple-element.26.refs_0_), channel_id=1, source_target_pairs={{0,1},{1,0},{2,3},{3,2},{4,5},{5,4},{6,7},{7,6},{8,9},{9,8},{10,11... | collective-permute-start | bytes 49160 | tf_op jit(solution)/shard_map/ppermute | solution.py:351
  22.5 12.3 %collective-permute-start.6 = (bf16[128,128]{1,0:T(8,128)(2,1)S(1)}, bf16[128,128]{1,0:T(8,128)(2,1)S(1)}, u32[]{:S(2)}, u32[]{:S(2)}) collective-permute-start(bf16[128,128]{1,0:T(8,128)(2,1)S(1)} %get-tuple-element.28), channel_id=1, source_target_pairs={{0,4},{4,0},{8,12},{12,8},{1,5},{5,1},{9,13},{13,9},{2,6},{6,2},{1... | collective-permute-start | bytes 98312 | tf_op jit(solution)/shard_map/ppermute | solution.py:351
  32.0 10.4 %collective-permute-start.7 = (bf16[128,128]{1,0:T(8,128)(2,1)S(1)}, bf16[128,128]{1,0:T(8,128)(2,1)S(1)}, u32[]{:S(2)}, u32[]{:S(2)}) collective-permute-start(bf16[128,128]{1,0:T(8,128)(2,1)S(1)} %get-tuple-element.29), channel_id=1, source_target_pairs={{0,8},{4,12},{8,0},{12,4},{1,9},{5,13},{9,1},{13,5},{2,10},{6,14},... | collective-permute-start | bytes 98312 | tf_op jit(solution)/shard_map/ppermute | solution.py:351
  33.4 9.0 %copy-start.2 = (bf16[16,2,2,256]{3,2,1,0:T(2,128)(2,1)S(1)}, bf16[16,2,2,256]{3,2,1,0:T(2,128)(2,1)}, u32[]{:S(2)}) copy-start(bf16[16,2,2,256]{3,2,1,0:T(2,128)(2,1)} %param.13) | copy-start | bytes 98308
  33.4 9.0 %collective-permute-start.8 = (bf16[128,128]{1,0:T(8,128)(2,1)S(1)}, bf16[128,128]{1,0:T(8,128)(2,1)S(1)}, u32[]{:S(2)}, u32[]{:S(2)}) collective-permute-start(bf16[128,128]{1,0:T(8,128)(2,1)S(1)} %get-tuple-element.30), channel_id=1, source_target_pairs={{0,12},{4,8},{8,4},{12,0},{1,13},{5,9},{9,5},{13,1},{2,14},{6,10},... | collective-permute-start | bytes 98312 | tf_op jit(solution)/shard_map/ppermute | solution.py:351
  36.5 14.4 %collective-permute-start.10 = (bf16[3,2,128,256]{3,2,1,0:T(8,128)(2,1)S(1)}, bf16[3,2,128,256]{3,2,1,0:T(8,128)(2,1)S(1)}, u32[]{:S(2)}, u32[]{:S(2)}) collective-permute-start(bf16[3,2,128,256]{3,2,1,0:T(8,128)(2,1)S(1)} %stage_pages.4._), channel_id=1, source_target_pairs={{0,4},{4,0},{8,12},{12,8},{1,5},{5,1},{9,13},{13,9},{2,6},{6,2},{1... | collective-permute-start | bytes 1179656 | tf_op jit(solution)/shard_map/ppermute | solution.py:351
  39.4 17.8 %collective-permute-start.11 = (bf16[3,2,128,256]{3,2,1,0:T(8,128)(2,1)S(1)}, bf16[3,2,128,256]{3,2,1,0:T(8,128)(2,1)S(1)}, u32[]{:S(2)}, u32[]{:S(2)}) collective-permute-start(bf16[3,2,128,256]{3,2,1,0:T(8,128)(2,1)S(1)} %stage_pages.5), channel_id=1, source_target_pairs={{0,12},{4,8},{8,4},{12,0},{1,13},{5,9},{9,5},{13,1},{2,14},{6,10},... | collective-permute-start | bytes 1179656 | tf_op jit(solution)/shard_map/ppermute | solution.py:351

commit v3 on v2

--- a/solution.py
+++ b/solution.py
@@ -93,9 +93,9 @@
         pltpu.make_async_copy(messages[j], messages[j], sems.at[j]).wait()
 
 
-def stage_pages_kernel(dims, partners, plan, table, pool, _, *refs):
+def stage_pages_kernel(dims, partners, plan, table, pool, *refs):
     groups, own_cap, move_cap, _ = dims
-    outs, sems = refs[: len(partners)], refs[len(partners)]
+    *outs, sems = refs[-len(partners) - 1 :]
     page = pool.shape[2]
     for i, j in enumerate(partners):
         for k in range(move_cap):
@@ -161,7 +161,7 @@
     return parts[0]
 
 
-def query_kernel(dims, n_parts, told, b_ref, *refs):
+def query_kernel(dims, n_parts, told, b_ref, _, *refs):
     groups, own_cap, _, stores = dims
     partials, messages = refs[:n_parts], refs[n_parts : n_parts + groups]
     outs, x = refs[n_parts + groups : n_parts + 2 * groups], refs[n_parts + 2 * groups]
@@ -416,19 +416,19 @@
         got[j] = swap(messages[j], "req", j)
     got = [got[j] for j in range(groups)]
 
-    def stage_pages(partners, after):
+    def stage_pages(partners, *after):
         return pl.pallas_call(
             functools.partial(stage_pages_kernel, dims, partners),
             out_shape=[shape((move_cap, 2, context, kv_width), bf16)] * len(partners),
-            in_specs=[IN_SMEM] * 2 + [IN_PLACE] * 2,
+            in_specs=[IN_SMEM] * 2 + [IN_PLACE] * (1 + len(after)),
             out_specs=[IN_PLACE] * len(partners),
             scratch_shapes=[pltpu.SemaphoreType.DMA((len(partners),))],
             compiler_params=PARAMS,
             name="stage_pages",
             cost_estimate=lasts(0.1),
-        )(plan, table, pool, after)
-
-    first_pages = stage_pages(early, got[1])
+        )(plan, table, pool, *after)
+
+    first_pages = stage_pages(early, got[half])
     pages = {j: swap(x, "req", j) for j, x in zip(early, first_pages)}
 
     partial, told = pl.pallas_call(
@@ -451,22 +451,19 @@
     )(cached_len, a_store.reshape(stores * rank, width), first_pages[0], *got)
     partials = [partial] + [swap(partial, "mp", j) for j in range(1, shards)]
 
+    other_pages = stage_pages(late + middle)
     queries = pl.pallas_call(
         functools.partial(query_kernel, dims, shards),
         out_shape=[shape((own_cap * depth, LANES), bf16)] * groups,
-        in_specs=[IN_SMEM] + [IN_VMEM] * (1 + shards + groups),
+        in_specs=[IN_SMEM, IN_VMEM, IN_PLACE] + [IN_VMEM] * (shards + groups),
         out_specs=[IN_VMEM] * groups,
         scratch_shapes=[pltpu.VMEM((number * depth, LANES), f32)],
         compiler_params=PARAMS,
         name="queries",
         cost_estimate=lasts(0.1),
-    )(told, b_store.reshape(stores * rank, width), *partials, *got)
+    )(told, b_store.reshape(stores * rank, width), other_pages[0], *partials, *got)
     queries = [queries[0]] + [swap(queries[j], "req", j) for j in range(1, groups)]
-    after = queries[1]
-    for partners in (middle, late):
-        staged = stage_pages(partners, after)
-        pages.update((j, swap(x, "req", j)) for j, x in zip(partners, staged))
-        after = staged[0]
+    pages.update((j, swap(x, "req", j)) for j, x in zip(late + middle, other_pages))
 
     attended, cache, sorted_queries = pl.pallas_call(
         functools.partial(early_kernel, dims, early),

time: 60.1 us -> 58.2 us (0.968)
  starting transfers between devices: 27.2 us -> 17.9 us
  waiting for transfers between devices: 7.89 us -> 16.6 us
  Pallas kernels: 23.7 us -> 22.3 us
    ppermute x12, starting transfers between devices: 27.2 us -> 17.9 us  [swap(): lax.ppermute(x, axis, [(i, i ^ j) for i in range(lax.axis_size(axis))])]
    ppermute x12, waiting for transfers between devices: 7.89 us -> 16.6 us  [swap(): lax.ppermute(x, axis, [(i, i ^ j) for i in range(lax.axis_size(axis))])]
    pallas_call x3 -> x2, Pallas kernels: 5.14 us -> 3.59 us  [stage_pages(): pl.pallas_call(functools.partial(stage_pages_kernel, dims, partners), out...]
  transfers between devices with their start and end apart: 12 -> 12, of which waited for: 5 -> 5; matrix products, arithmetic and copies ran while one was open for 0% -> 0% of each run, Pallas kernels for 32% -> 30%
where the time goes in v3:
time: 58.2 us; the launch traced here: 57.7 us
  Pallas kernels  22.3 us (38%)
  starting transfers between devices  17.9 us (31%)
  waiting for transfers between devices  16.6 us (29%)
  between operations  0.76 us (1%)
    ppermute x12, starting transfers between devices, swap(): lax.ppermute(x, axis, [(i, i ^ j) for i in range(lax.axis_size(axis))])  17.9 us
    ppermute x12, waiting for transfers between devices, swap(): lax.ppermute(x, axis, [(i, i ^ j) for i in range(lax.axis_size(axis))])  16.6 us
    pallas_call x1, Pallas kernels, per_device(): pl.pallas_call(functools.partial(early_kernel, dims, early), out_shape=[s...  8.73 us
    pallas_call x2, Pallas kernels, per_device(): pl.pallas_call(functools.partial(late_kernel, dims, partners), out_shape=...  4.62 us
    pallas_call x2, Pallas kernels, stage_pages(): pl.pallas_call(functools.partial(stage_pages_kernel, dims, partners), out...  3.59 us
    pallas_call x1, Pallas kernels, per_device(): pl.pallas_call(functools.partial(stage_rows_kernel, dims), out_shape=[mes...  2.54 us
    pallas_call x1, Pallas kernels, per_device(): pl.pallas_call(functools.partial(rank_kernel, dims), out_shape=[shape((2...  2 us
  transfers between devices with their start and end apart: 12, of which 5 were waited for; matrix products, arithmetic and copies ran while one was open for 0% of the time, Pallas kernels for 30%

profile of v3, /device:TPU:0, one launch (start us, length us, event | category | flops | bytes accessed | tf_op | source)
XLA Modules:
  0.0 57.7 jit_solution(839784547554344096)
XLA Ops:
  0.6 2.5 %stage_rows.1 = (bf16[272,128]{1,0:T(8,128)(2,1)S(1)}, bf16[272,128]{1,0:T(8,128)(2,1)S(1)}, bf16[272,128]{1,0:T(8,128)(2,1)S(1)}, bf16[272,128]{1,0:T(8,128)(2,1)S(1)}, s32[28]{0:T(128)S(1)}) custom-call(s32[16]{0:T(128)} %adapter_of.1, s32[8]{0:T(128)} %adapter_home.1, s32[16]{0:T(128)} %new_group.1, s32[16]{0:T(128)} %cached_len.3, ...), custom_call_target="tpu_custom_call" | custom-call | flops 1000000000 | bytes 3000000 | tf_op jit(solution)/shard_map/stage_rows/pallas_call | solution.py:394
  3.2 0.0 copy-start.3
  3.2 4.1 %collective-permute-start = (bf16[272,128]{1,0:T(8,128)(2,1)S(1)}, bf16[272,128]{1,0:T(8,128)(2,1)S(1)}, u32[]{:S(2)}, u32[]{:S(2)}) collective-permute-start(bf16[272,128]{1,0:T(8,128)(2,1)S(1)} %get-tuple-element.23), channel_id=1, source_target_pairs={{0,8},{4,12},{8,0},{12,4},{1,9},{5,13},{9,1},{13,5},{2,10},{6,14},... | collective-permute-start | bytes 208904 | tf_op jit(solution)/shard_map/ppermute | solution.py:351
  7.3 1.6 %collective-permute-start.1 = (bf16[272,128]{1,0:T(8,128)(2,1)S(1)}, bf16[272,128]{1,0:T(8,128)(2,1)S(1)}, u32[]{:S(2)}, u32[]{:S(2)}) collective-permute-start(bf16[272,128]{1,0:T(8,128)(2,1)S(1)} %get-tuple-element.25), channel_id=1, source_target_pairs={{0,4},{4,0},{8,12},{12,8},{1,5},{5,1},{9,13},{13,9},{2,6},{6,2},{1... | collective-permute-start | bytes 208904 | tf_op jit(solution)/shard_map/ppermute | solution.py:351
  8.9 1.6 %collective-permute-done.refs_0_.refs_2_.refs_6_ = bf16[272,128]{1,0:T(8,128)(2,1)S(1)} collective-permute-done((bf16[272,128]{1,0:T(8,128)(2,1)S(1)}, bf16[272,128]{1,0:T(8,128)(2,1)S(1)}, u32[]{:S(2)}, u32[]{:S(2)}) %collective-permute-start) | collective-permute-done | bytes 69664 | tf_op jit(solution)/shard_map/ppermute | solution.py:351
  10.5 1.7 %stage_pages.2._ = bf16[3,2,128,256]{3,2,1,0:T(8,128)(2,1)S(1)} custom-call(s32[28]{0:T(128)S(1)} %get-tuple-element.22.plan, s32[8,16]{1,0:T(8,128)} %bitcast.28, bf16[2,128,16,256]{3,2,1,0:T(8,128)(2,1)} %pool.5, bf16[272,128]{1,0:T(8,128)(2,1)S(1)} %collective-permute-done.refs_0_.refs_2_.refs_6_), custom_call_target="tpu_custom_call" | custom-call | flops 100000000 | bytes 300000 | tf_op jit(solution)/shard_map/stage_pages/pallas_call | solution.py:420
  12.2 2.7 %collective-permute-start.9 = (bf16[3,2,128,256]{3,2,1,0:T(8,128)(2,1)S(1)}, bf16[3,2,128,256]{3,2,1,0:T(8,128)(2,1)S(1)}, u32[]{:S(2)}, u32[]{:S(2)}) collective-permute-start(bf16[3,2,128,256]{3,2,1,0:T(8,128)(2,1)S(1)} %stage_pages.2._), channel_id=1, source_target_pairs={{0,8},{4,12},{8,0},{12,4},{1,9},{5,13},{9,1},{13,5},{2,10},{6,14},... | collective-permute-start | bytes 1179656 | tf_op jit(solution)/shard_map/ppermute | solution.py:351
  14.9 0.2 collective-permute-done.2.refs_3_.refs_7_
  15.1 2.0 %rank_products.1 = (f32[32,128]{1,0:T(8,128)S(1)}, s32[64]{0:T(128)S(1)}) custom-call(s32[16]{0:T(128)S(1)} %copy-done.3, bf16[128,2048]{1,0:T(8,128)(2,1)S(1)} %bitcast.24, bf16[3,2,128,256]{3,2,1,0:T(8,128)(2,1)S(1)} %stage_pages.2._, bf16[272,128]{1,0:T(8,128)(2,1)S(1)} %get-tuple-element.24.refs_0_.refs_4_, ...), custom_call_target="tpu_custom_call" | custom-call | flops 10000000000 | bytes 30000000 | tf_op jit(solution)/shard_map/rank_products/pallas_call | solution.py:434
  17.1 0.1 collective-permute-start.5
  17.2 1.6 %collective-permute-start.4 = (f32[32,128]{1,0:T(8,128)S(1)}, f32[32,128]{1,0:T(8,128)S(1)}, u32[]{:S(2)}, u32[]{:S(2)}) collective-permute-start(f32[32,128]{1,0:T(8,128)S(1)} %get-tuple-element.29.refs_0_), channel_id=1, source_target_pairs={{0,2},{1,3},{2,0},{3,1},{4,6},{5,7},{6,4},{7,5},{8,10},{9,11},{10,... | collective-permute-start | bytes 49160 | tf_op jit(solution)/shard_map/ppermute | solution.py:351
  18.8 0.3 collective-permute-start.3
  19.1 1.9 %stage_pages.3 = (bf16[3,2,128,256]{3,2,1,0:T(8,128)(2,1)S(1)}, bf16[3,2,128,256]{3,2,1,0:T(8,128)(2,1)S(1)}) custom-call(s32[28]{0:T(128)S(1)} %get-tuple-element.22.plan, s32[8,16]{1,0:T(8,128)} %bitcast.29, bf16[2,128,16,256]{3,2,1,0:T(8,128)(2,1)} %pool.5), custom_call_target="tpu_custom_call" | custom-call | flops 100000000 | bytes 300000 | tf_op jit(solution)/shard_map/stage_pages/pallas_call | solution.py:420
  20.9 0.1 collective-permute-done.4.refs_2_
  21.0 0.8 %queries.1 = (bf16[128,128]{1,0:T(8,128)(2,1)S(1)}, bf16[128,128]{1,0:T(8,128)(2,1)S(1)}, bf16[128,128]{1,0:T(8,128)(2,1)S(1)}, bf16[128,128]{1,0:T(8,128)(2,1)S(1)}) custom-call(s32[64]{0:T(128)S(1)} %get-tuple-element.27.told, bf16[128,2048]{1,0:T(8,128)(2,1)S(1)} %bitcast.23, bf16[3,2,128,256]{3,2,1,0:T(8,128)(2,1)S(1)} %get-tuple-element.28._, ...), custom_call_target="tpu_custom_call" | custom-call | flops 100000000 | bytes 300000 | tf_op jit(solution)/shard_map/queries/pallas_call | solution.py:455
  21.9 3.8 %collective-permute-start.6 = (bf16[128,128]{1,0:T(8,128)(2,1)S(1)}, bf16[128,128]{1,0:T(8,128)(2,1)S(1)}, u32[]{:S(2)}, u32[]{:S(2)}) collective-permute-start(bf16[128,128]{1,0:T(8,128)(2,1)S(1)} %get-tuple-element.31), channel_id=1, source_target_pairs={{0,4},{4,0},{8,12},{12,8},{1,5},{5,1},{9,13},{13,9},{2,6},{6,2},{1... | collective-permute-start | bytes 98312 | tf_op jit(solution)/shard_map/ppermute | solution.py:351
  25.6 0.0 collective-permute-start.7
  25.7 2.4 %collective-permute-start.8 = (bf16[128,128]{1,0:T(8,128)(2,1)S(1)}, bf16[128,128]{1,0:T(8,128)(2,1)S(1)}, u32[]{:S(2)}, u32[]{:S(2)}) collective-permute-start(bf16[128,128]{1,0:T(8,128)(2,1)S(1)} %get-tuple-element.33), channel_id=1, source_target_pairs={{0,12},{4,8},{8,4},{12,0},{1,13},{5,9},{9,5},{13,1},{2,14},{6,10},... | collective-permute-start | bytes 98312 | tf_op jit(solution)/shard_map/ppermute | solution.py:351
  28.1 1.4 %collective-permute-start.11 = (bf16[3,2,128,256]{3,2,1,0:T(8,128)(2,1)S(1)}, bf16[3,2,128,256]{3,2,1,0:T(8,128)(2,1)S(1)}, u32[]{:S(2)}, u32[]{:S(2)}) collective-permute-start(bf16[3,2,128,256]{3,2,1,0:T(8,128)(2,1)S(1)} %get-tuple-element.28._), channel_id=1, source_target_pairs={{0,12},{4,8},{8,4},{12,0},{1,13},{5,9},{9,5},{13,1},{2,14},{6,10},... | collective-permute-start | bytes 1179656 | tf_op jit(solution)/shard_map/ppermute | solution.py:351
  29.5 0.6 collective-permute-done.6.refs_1_
  30.1 14.2 %collective-permute-done.7.refs_2_ = bf16[128,128]{1,0:T(8,128)(2,1)S(1)} collective-permute-done((bf16[128,128]{1,0:T(8,128)(2,1)S(1)}, bf16[128,128]{1,0:T(8,128)(2,1)S(1)}, u32[]{:S(2)}, u32[]{:S(2)}) %collective-permute-start.7) | collective-permute-done | bytes 32800 | tf_op jit(solution)/shard_map/ppermute | solution.py:351
  44.3 8.7 %attend_early.1 = (bf16[16,32,128]{2,1,0:T(8,128)(2,1)}, bf16[2,16,128,256]{3,2,1,0:T(8,128)(2,1)}, bf16[16,32,128]{2,1,0:T(8,128)(2,1)S(1)}) custom-call(s32[28]{0:T(128)S(1)} %get-tuple-element.22.plan, s32[64]{0:T(128)S(1)} %get-tuple-element.27.told, s32[8,16]{1,0:T(8,128)} %bitcast.30, bf16[2,128,16,256]{3,2,1,0:T(8,128)(2,1)} %pool.5, ...), custom_call_target="tpu_custom_call" | custom-call | flops 60000002048 | bytes 180000000 | tf_op jit(solution)/shard_map/attend_early/pallas_call | solution.py:468
  53.0 2.3 %attend_arrived.2 = (bf16[16,32,128]{2,1,0:T(8,128)(2,1)}, bf16[2,16,128,256]{3,2,1,0:T(8,128)(2,1)}) custom-call(s32[64]{0:T(128)S(1)} %get-tuple-element.27.told, bf16[128,128]{1,0:T(8,128)(2,1)S(1)} %bitcast.26, bf16[16,32,128]{2,1,0:T(8,128)(2,1)S(1)} %get-tuple-element.34.queries, ...), custom_call_target="tpu_custom_call", output_to_operand_aliasing={{0}: (3, {}), {1}: (4, {})} | custom-call | flops 1000000000 | bytes 3000000 | tf_op jit(solution)/shard_map/attend_arrived/pallas_call | solution.py:490
  55.3 2.3 %attend_arrived.3 = (bf16[16,32,128]{2,1,0:T(8,128)(2,1)}, bf16[2,16,128,256]{3,2,1,0:T(8,128)(2,1)}) custom-call(s32[64]{0:T(128)S(1)} %get-tuple-element.27.told, bf16[128,128]{1,0:T(8,128)(2,1)S(1)} %bitcast.27, bf16[16,32,128]{2,1,0:T(8,128)(2,1)S(1)} %get-tuple-element.34.queries, ...), custom_call_target="tpu_custom_call", output_to_operand_aliasing={{0}: (3, {}), {1}: (4, {})} | custom-call | flops 1000000000 | bytes 3000000 | tf_op jit(solution)/shard_map/attend_arrived/pallas_call | solution.py:490
  (16 shorter events, 0.0 us)
Async XLA Ops:
  3.2 11.9 %copy-start.1 = (bf16[2,64,2048]{2,1,0:T(8,128)(2,1)S(1)}, bf16[2,64,2048]{2,1,0:T(8,128)(2,1)}, u32[]{:S(2)}) copy-start(bf16[2,64,2048]{2,1,0:T(8,128)(2,1)} %param.16) | copy-start | bytes 1572868
  3.2 11.9 %copy-start.3 = (s32[16]{0:T(128)S(1)}, s32[16]{0:T(128)}, u32[]{:S(2)}) copy-start(s32[16]{0:T(128)} %cached_len.3) | copy-start | bytes 196
  3.2 7.3 %collective-permute-start = (bf16[272,128]{1,0:T(8,128)(2,1)S(1)}, bf16[272,128]{1,0:T(8,128)(2,1)S(1)}, u32[]{:S(2)}, u32[]{:S(2)}) collective-permute-start(bf16[272,128]{1,0:T(8,128)(2,1)S(1)} %get-tuple-element.23), channel_id=1, source_target_pairs={{0,8},{4,12},{8,0},{12,4},{1,9},{5,13},{9,1},{13,5},{2,10},{6,14},... | collective-permute-start | bytes 208904 | tf_op jit(solution)/shard_map/ppermute | solution.py:351
  7.3 7.6 %collective-permute-start.1 = (bf16[272,128]{1,0:T(8,128)(2,1)S(1)}, bf16[272,128]{1,0:T(8,128)(2,1)S(1)}, u32[]{:S(2)}, u32[]{:S(2)}) collective-permute-start(bf16[272,128]{1,0:T(8,128)(2,1)S(1)} %get-tuple-element.25), channel_id=1, source_target_pairs={{0,4},{4,0},{8,12},{12,8},{1,5},{5,1},{9,13},{13,9},{2,6},{6,2},{1... | collective-permute-start | bytes 208904 | tf_op jit(solution)/shard_map/ppermute | solution.py:351
  8.9 6.2 %collective-permute-start.2 = (bf16[272,128]{1,0:T(8,128)(2,1)S(1)}, bf16[272,128]{1,0:T(8,128)(2,1)S(1)}, u32[]{:S(2)}, u32[]{:S(2)}) collective-permute-start(bf16[272,128]{1,0:T(8,128)(2,1)S(1)} %get-tuple-element.26), channel_id=1, source_target_pairs={{0,12},{4,8},{8,4},{12,0},{1,13},{5,9},{9,5},{13,1},{2,14},{6,10},... | collective-permute-start | bytes 208904 | tf_op jit(solution)/shard_map/ppermute | solution.py:351
  12.2 32.1 %collective-permute-start.9 = (bf16[3,2,128,256]{3,2,1,0:T(8,128)(2,1)S(1)}, bf16[3,2,128,256]{3,2,1,0:T(8,128)(2,1)S(1)}, u32[]{:S(2)}, u32[]{:S(2)}) collective-permute-start(bf16[3,2,128,256]{3,2,1,0:T(8,128)(2,1)S(1)} %stage_pages.2._), channel_id=1, source_target_pairs={{0,8},{4,12},{8,0},{12,4},{1,9},{5,13},{9,1},{13,5},{2,10},{6,14},... | collective-permute-start | bytes 1179656 | tf_op jit(solution)/shard_map/ppermute | solution.py:351
  17.1 3.9 %copy-start = (bf16[2,64,2048]{2,1,0:T(8,128)(2,1)S(1)}, bf16[2,64,2048]{2,1,0:T(8,128)(2,1)}, u32[]{:S(2)}) copy-start(bf16[2,64,2048]{2,1,0:T(8,128)(2,1)} %param.17) | copy-start | bytes 1572868
  17.1 27.2 %copy-start.2 = (bf16[16,2,2,256]{3,2,1,0:T(2,128)(2,1)S(1)}, bf16[16,2,2,256]{3,2,1,0:T(2,128)(2,1)}, u32[]{:S(2)}) copy-start(bf16[16,2,2,256]{3,2,1,0:T(2,128)(2,1)} %param.13) | copy-start | bytes 98308
  17.1 3.8 %collective-permute-start.5 = (f32[32,128]{1,0:T(8,128)S(1)}, f32[32,128]{1,0:T(8,128)S(1)}, u32[]{:S(2)}, u32[]{:S(2)}) collective-permute-start(f32[32,128]{1,0:T(8,128)S(1)} %get-tuple-element.29.refs_0_), channel_id=1, source_target_pairs={{0,3},{1,2},{2,1},{3,0},{4,7},{5,6},{6,5},{7,4},{8,11},{9,10},{10,... | collective-permute-start | bytes 49160 | tf_op jit(solution)/shard_map/ppermute | solution.py:351
  17.2 3.8 %collective-permute-start.4 = (f32[32,128]{1,0:T(8,128)S(1)}, f32[32,128]{1,0:T(8,128)S(1)}, u32[]{:S(2)}, u32[]{:S(2)}) collective-permute-start(f32[32,128]{1,0:T(8,128)S(1)} %get-tuple-element.29.refs_0_), channel_id=1, source_target_pairs={{0,2},{1,3},{2,0},{3,1},{4,6},{5,7},{6,4},{7,5},{8,10},{9,11},{10,... | collective-permute-start | bytes 49160 | tf_op jit(solution)/shard_map/ppermute | solution.py:351
  18.8 2.3 %collective-permute-start.3 = (f32[32,128]{1,0:T(8,128)S(1)}, f32[32,128]{1,0:T(8,128)S(1)}, u32[]{:S(2)}, u32[]{:S(2)}) collective-permute-start(f32[32,128]{1,0:T(8,128)S(1)} %get-tuple-element.29.refs_0_), channel_id=1, source_target_pairs={{0,1},{1,0},{2,3},{3,2},{4,5},{5,4},{6,7},{7,6},{8,9},{9,8},{10,11... | collective-permute-start | bytes 49160 | tf_op jit(solution)/shard_map/ppermute | solution.py:351
  21.9 8.2 %collective-permute-start.6 = (bf16[128,128]{1,0:T(8,128)(2,1)S(1)}, bf16[128,128]{1,0:T(8,128)(2,1)S(1)}, u32[]{:S(2)}, u32[]{:S(2)}) collective-permute-start(bf16[128,128]{1,0:T(8,128)(2,1)S(1)} %get-tuple-element.31), channel_id=1, source_target_pairs={{0,4},{4,0},{8,12},{12,8},{1,5},{5,1},{9,13},{13,9},{2,6},{6,2},{1... | collective-permute-start | bytes 98312 | tf_op jit(solution)/shard_map/ppermute | solution.py:351
  25.6 18.6 %collective-permute-start.7 = (bf16[128,128]{1,0:T(8,128)(2,1)S(1)}, bf16[128,128]{1,0:T(8,128)(2,1)S(1)}, u32[]{:S(2)}, u32[]{:S(2)}) collective-permute-start(bf16[128,128]{1,0:T(8,128)(2,1)S(1)} %get-tuple-element.32), channel_id=1, source_target_pairs={{0,8},{4,12},{8,0},{12,4},{1,9},{5,13},{9,1},{13,5},{2,10},{6,14},... | collective-permute-start | bytes 98312 | tf_op jit(solution)/shard_map/ppermute | solution.py:351
  25.7 18.6 %collective-permute-start.8 = (bf16[128,128]{1,0:T(8,128)(2,1)S(1)}, bf16[128,128]{1,0:T(8,128)(2,1)S(1)}, u32[]{:S(2)}, u32[]{:S(2)}) collective-permute-start(bf16[128,128]{1,0:T(8,128)(2,1)S(1)} %get-tuple-element.33), channel_id=1, source_target_pairs={{0,12},{4,8},{8,4},{12,0},{1,13},{5,9},{9,5},{13,1},{2,14},{6,10},... | collective-permute-start | bytes 98312 | tf_op jit(solution)/shard_map/ppermute | solution.py:351
  28.1 27.2 %collective-permute-start.11 = (bf16[3,2,128,256]{3,2,1,0:T(8,128)(2,1)S(1)}, bf16[3,2,128,256]{3,2,1,0:T(8,128)(2,1)S(1)}, u32[]{:S(2)}, u32[]{:S(2)}) collective-permute-start(bf16[3,2,128,256]{3,2,1,0:T(8,128)(2,1)S(1)} %get-tuple-element.28._), channel_id=1, source_target_pairs={{0,12},{4,8},{8,4},{12,0},{1,13},{5,9},{9,5},{13,1},{2,14},{6,10},... | collective-permute-start | bytes 1179656 | tf_op jit(solution)/shard_map/ppermute | solution.py:351
  30.1 23.0 %collective-permute-start.10 = (bf16[3,2,128,256]{3,2,1,0:T(8,128)(2,1)S(1)}, bf16[3,2,128,256]{3,2,1,0:T(8,128)(2,1)S(1)}, u32[]{:S(2)}, u32[]{:S(2)}) collective-permute-start(bf16[3,2,128,256]{3,2,1,0:T(8,128)(2,1)S(1)} %get-tuple-element.37), channel_id=1, source_target_pairs={{0,4},{4,0},{8,12},{12,8},{1,5},{5,1},{9,13},{13,9},{2,6},{6,2},{1... | collective-permute-start | bytes 1179656 | tf_op jit(solution)/shard_map/ppermute | solution.py:351

commit v4 on v3

--- a/solution.py
+++ b/solution.py
@@ -201,14 +201,10 @@
     ]
 
 
-def attend(query, keys, values, fresh, length, slot):
-    depth = query.shape[0]
-    context, width = keys.shape
-    heads = width // HEAD
-    per = depth // heads
-    scale = HEAD**-0.5
+def by_head(query, heads):
+    per = query.shape[0] // heads
     blank = jnp.zeros((per, HEAD), query.dtype)
-    spread = jnp.concatenate(
+    return jnp.concatenate(
         [
             jnp.concatenate(
                 [query[h * per : (h + 1) * per] if i == h else blank for i in range(heads)], axis=1
@@ -217,124 +213,156 @@
         ],
         axis=0,
     )
-    all_keys = jnp.concatenate([keys, fresh[0]], axis=0)
-    all_values = jnp.concatenate([values, fresh[1]], axis=0)
-    scores = lax.dot_general(
-        spread, all_keys, (((1,), (1,)), ((), ())), preferred_element_type=jnp.float32
-    )
-    column = lax.broadcasted_iota(jnp.int32, scores.shape, 1)
-    step = lax.broadcasted_iota(jnp.int32, scores.shape, 0) % 2
-    fresh_at = column - context - 2 * slot
-    visible = (column < length) | ((fresh_at >= 0) & (fresh_at <= step))
-    scores = jnp.where(visible, scores * scale, NEG_FILL)
+
+
+def attend(queries, keys, values, fresh, lengths, slots):
+    depth = queries[0].shape[0]
+    context, width = keys[0].shape
+    heads = width // HEAD
+    per = depth // heads
+    scale = HEAD**-0.5
+    scores = []
+    for query, key, length, slot in zip(queries, keys, lengths, slots):
+        product = lax.dot_general(
+            by_head(query, heads),
+            jnp.concatenate([key, fresh[0]], axis=0),
+            (((1,), (1,)), ((), ())),
+            preferred_element_type=jnp.float32,
+        )
+        column = lax.broadcasted_iota(jnp.int32, product.shape, 1)
+        step = lax.broadcasted_iota(jnp.int32, product.shape, 0) % 2
+        fresh_at = column - context - 2 * slot
+        visible = (column < length) | ((fresh_at >= 0) & (fresh_at <= step))
+        scores.append(jnp.where(visible, product * scale, NEG_FILL))
+    scores = jnp.concatenate(scores, axis=0)
     weights = jnp.exp(scores - jnp.max(scores, axis=1, keepdims=True))
-    chance = (weights / jnp.sum(weights, axis=1, keepdims=True)).astype(jnp.bfloat16)
-    out = jnp.dot(chance, all_values, preferred_element_type=jnp.float32)
-    out = jnp.concatenate(
-        [out[h * per : (h + 1) * per, h * HEAD : (h + 1) * HEAD] for h in range(heads)], axis=0
-    )
-    return out.astype(jnp.bfloat16)
-
-
-def early_kernel(dims, partners, plan, told, table, pool, new_kv, *refs):
-    groups, own_cap, move_cap, _ = dims
-    queries, refs = refs[:groups], refs[groups:]
-    pages, refs = refs[: len(partners)], refs[len(partners) :]
-    attended, cache, sorted_queries, kv, x, kv_sems, query_sems, out_sems = refs
-    count, depth, _ = attended.shape
+    chances = (weights / jnp.sum(weights, axis=1, keepdims=True)).astype(jnp.bfloat16)
+    results = []
+    for n, value in enumerate(values):
+        out = jnp.dot(
+            chances[n * depth : (n + 1) * depth],
+            jnp.concatenate([value, fresh[1]], axis=0),
+            preferred_element_type=jnp.float32,
+        )
+        out = jnp.concatenate(
+            [out[h * per : (h + 1) * per, h * HEAD : (h + 1) * HEAD] for h in range(heads)], axis=0
+        )
+        results.append(out.astype(jnp.bfloat16))
+    return results
+
+
+def place_kernel(dims, told, table, pool, _, cache, kv, kv_sems, out_sems):
+    groups = dims[0]
+    count = kv.shape[1]
     page = pool.shape[2]
-
-    def here(source):
-        known = source == 0
-        for j in partners:
-            known = known | (source == j)
-        return known
-
     for r in range(count):
-        source = told[groups + r]
-
-        @pl.when(source == 0)
+
+        @pl.when(told[groups + r] == 0)
         def _(r=r):
             for p in range(table.shape[0]):
                 pltpu.make_async_copy(
                     pool.at[:, table[p, r]], kv.at[:, r, pl.ds(p * page, page)], kv_sems.at[r]
                 ).start()
 
-        for i, j in enumerate(partners):
-
-            @pl.when(source == j)
-            def _(r=r, i=i):
-                pltpu.make_async_copy(
-                    pages[i].at[told[groups + count + r]], kv.at[:, r], kv_sems.at[r]
-                ).start()
-
-    for j in range(groups):
-        for k in range(own_cap):
-            slot = plan[j * own_cap + k]
-
-            @pl.when(slot >= 0)
-            def _(j=j, k=k, slot=slot):
-                pltpu.make_async_copy(
-                    queries[j].at[pl.ds(k * depth, depth)],
-                    sorted_queries.at[slot],
-                    query_sems.at[slot],
-                ).start()
-
-    fresh = fresh_rows(new_kv, x, kv.shape[3] // HEAD)
     for r in range(count):
-        pltpu.make_async_copy(sorted_queries.at[r], sorted_queries.at[r], query_sems.at[r]).wait()
-
-        @pl.when(here(told[groups + r]))
+
+        @pl.when(told[groups + r] == 0)
         def _(r=r):
             pltpu.make_async_copy(kv.at[:, r], kv.at[:, r], kv_sems.at[r]).wait()
             pltpu.make_async_copy(kv.at[:, r], cache.at[:, r], out_sems.at[r]).start()
 
     for r in range(count):
-        attended[r] = attend(
-            sorted_queries[r], kv[0, r], kv[1, r], fresh, told[groups + 2 * count + r], r
-        )
-    for r in range(count):
-
-        @pl.when(here(told[groups + r]))
+
+        @pl.when(told[groups + r] == 0)
         def _(r=r):
             pltpu.make_async_copy(kv.at[:, r], cache.at[:, r], out_sems.at[r]).wait()
 
 
+def arrivals(dims, partners, told, count, pages):
+    groups, _, move_cap, _ = dims
+    blocks, slots = [], []
+    for i, j in enumerate(partners):
+        for k in range(move_cap):
+            blocks.append(pages[i].at[k])
+            slots.append(told[groups + 3 * count + j * move_cap + k])
+    return blocks, slots, [jnp.maximum(slot, 0) for slot in slots]
+
+
+def early_kernel(dims, partners, plan, told, kv, new_kv, cache_in, *refs):
+    groups, own_cap, _, _ = dims
+    queries, refs = refs[:groups], refs[groups:]
+    pages, refs = refs[: len(partners)], refs[len(partners) :]
+    attended, sorted_queries, cache, x, page_sems = refs
+    count, depth, _ = attended.shape
+    blocks, slots, places = arrivals(dims, partners, told, count, pages)
+    copies = [
+        pltpu.make_async_copy(block, cache.at[:, at], page_sems.at[n])
+        for n, (block, at) in enumerate(zip(blocks, places))
+    ]
+    for slot, copy in zip(slots, copies):
+        pl.when(slot >= 0)(copy.start)
+    for j in range(groups):
+        for k in range(own_cap):
+            slot = plan[j * own_cap + k]
+
+            @pl.when(slot >= 0)
+            def _(j=j, k=k, slot=slot):
+                sorted_queries[slot] = queries[j][k * depth : (k + 1) * depth, :]
+
+    every = list(range(count))
+    results = attend(
+        [sorted_queries[at] for at in every + places],
+        [kv[0, r] for r in every] + [block[0] for block in blocks],
+        [kv[1, r] for r in every] + [block[1] for block in blocks],
+        fresh_rows(new_kv, x, kv.shape[3] // HEAD),
+        [told[groups + 2 * count + at] for at in every + places],
+        every + places,
+    )
+    for r in every:
+        attended[r] = results[r]
+    for n, (slot, at) in enumerate(zip(slots, places)):
+
+        @pl.when(slot >= 0)
+        def _(n=n, at=at):
+            attended[at] = results[count + n]
+
+    for slot, copy in zip(slots, copies):
+        pl.when(slot >= 0)(copy.wait)
+
+
 def late_kernel(dims, partners, told, new_kv, queries, attended_in, cache_in, *refs):
-    groups, _, move_cap, _ = dims
+    groups = dims[0]
     pages, refs = refs[: len(partners)], refs[len(partners) :]
     attended, cache, results, x, page_sems, out_sems = refs
     count = queries.shape[0]
-    kv_width = cache.shape[3]
-    copies = []
-    for i, j in enumerate(partners):
-        for k in range(move_cap):
-            slot = told[groups + 3 * count + j * move_cap + k]
-            at = jnp.maximum(slot, 0)
-            n = i * move_cap + k
-            copies.append(
-                (
-                    slot,
-                    at,
-                    pltpu.make_async_copy(pages[i].at[k], cache.at[:, at], page_sems.at[n]),
-                    pltpu.make_async_copy(results.at[n], attended.at[at], out_sems.at[n]),
-                )
-            )
-            pl.when(slot >= 0)(copies[-1][2].start)
-    fresh = fresh_rows(new_kv, x, kv_width // HEAD)
-    for n, (slot, at, _, _) in enumerate(copies):
-        i, k = divmod(n, move_cap)
-        results[n] = attend(
-            queries[at], pages[i][k, 0], pages[i][k, 1], fresh, told[groups + 2 * count + at], at
+    blocks, slots, places = arrivals(dims, partners, told, count, pages)
+    copies = [
+        (
+            pltpu.make_async_copy(block, cache.at[:, at], page_sems.at[n]),
+            pltpu.make_async_copy(results.at[n], attended.at[at], out_sems.at[n]),
         )
-    for slot, _, _, copy in copies:
+        for n, (block, at) in enumerate(zip(blocks, places))
+    ]
+    for slot, (copy, _) in zip(slots, copies):
         pl.when(slot >= 0)(copy.start)
-    for slot, _, page_copy, copy in copies:
+    outs = attend(
+        [queries[at] for at in places],
+        [block[0] for block in blocks],
+        [block[1] for block in blocks],
+        fresh_rows(new_kv, x, cache.shape[3] // HEAD),
+        [told[groups + 2 * count + at] for at in places],
+        places,
+    )
+    for n, out in enumerate(outs):
+        results[n] = out
+    for slot, (_, copy) in zip(slots, copies):
+        pl.when(slot >= 0)(copy.start)
+    for slot, pair in zip(slots, copies):
 
         @pl.when(slot >= 0)
-        def _(page_copy=page_copy, copy=copy):
-            page_copy.wait()
-            copy.wait()
+        def _(pair=pair):
+            for copy in pair:
+                copy.wait()
 
 
 def lasts(microseconds):
@@ -377,9 +405,8 @@
     depth = width // LANES * steps
     number = groups * own_cap
     half = max(groups // 2, 1)
-    late = [groups - 1]
-    early = [half] if half not in late else []
-    middle = [j for j in range(1, groups) if j not in early + late]
+    early = [half]
+    late = [j for j in range(1, groups) if j != half]
     hidden, frozen = to_tiles(hidden_in), to_tiles(frozen_query_rows)
     table, pool = in_hbm(page_table.T, kv_pool)
     fresh = (
@@ -428,8 +455,8 @@
             cost_estimate=lasts(0.1),
         )(plan, table, pool, *after)
 
-    first_pages = stage_pages(early, got[half])
-    pages = {j: swap(x, "req", j) for j, x in zip(early, first_pages)}
+    staged = stage_pages(early, got[half])
+    pages = {j: swap(x, "req", j) for j, x in zip(early, staged)}
 
     partial, told = pl.pallas_call(
         functools.partial(rank_kernel, dims),
@@ -448,10 +475,10 @@
         compiler_params=PARAMS,
         name="rank_products",
         cost_estimate=lasts(10),
-    )(cached_len, a_store.reshape(stores * rank, width), first_pages[0], *got)
+    )(cached_len, a_store.reshape(stores * rank, width), staged[-1], *got)
     partials = [partial] + [swap(partial, "mp", j) for j in range(1, shards)]
 
-    other_pages = stage_pages(late + middle)
+    last_pages = stage_pages(late)
     queries = pl.pallas_call(
         functools.partial(query_kernel, dims, shards),
         out_shape=[shape((own_cap * depth, LANES), bf16)] * groups,
@@ -461,32 +488,35 @@
         compiler_params=PARAMS,
         name="queries",
         cost_estimate=lasts(0.1),
-    )(told, b_store.reshape(stores * rank, width), other_pages[0], *partials, *got)
+    )(told, b_store.reshape(stores * rank, width), last_pages[0], *partials, *got)
     queries = [queries[0]] + [swap(queries[j], "req", j) for j in range(1, groups)]
-    pages.update((j, swap(x, "req", j)) for j, x in zip(late + middle, other_pages))
-
-    attended, cache, sorted_queries = pl.pallas_call(
+    pages.update((j, swap(x, "req", j)) for j, x in zip(late, last_pages))
+
+    cache, kv = pl.pallas_call(
+        functools.partial(place_kernel, dims),
+        out_shape=[shape((2, count, context, kv_width), bf16)] * 2,
+        in_specs=[IN_SMEM] * 2 + [IN_PLACE] * 2,
+        out_specs=[IN_PLACE] * 2,
+        scratch_shapes=[pltpu.SemaphoreType.DMA((count,))] * 2,
+        compiler_params=PARAMS,
+        name="place_pages",
+        cost_estimate=lasts(0.1),
+    )(told, table, pool, queries[0])
+    attended, sorted_queries, cache = pl.pallas_call(
         functools.partial(early_kernel, dims, early),
-        out_shape=[
-            shape((count, depth, LANES), bf16),
-            shape((2, count, context, kv_width), bf16),
-            shape((count, depth, LANES), bf16),
-        ],
-        in_specs=[IN_SMEM] * 3 + [IN_PLACE, IN_VMEM] + [IN_PLACE] * (groups + len(early)),
-        out_specs=[IN_VMEM, IN_PLACE, IN_VMEM],
+        out_shape=[shape((count, depth, LANES), bf16)] * 2 + [shape(cache.shape, bf16)],
+        in_specs=[IN_SMEM] * 2 + [IN_VMEM] * 2 + [IN_PLACE] + [IN_VMEM] * (groups + len(early)),
+        out_specs=[IN_VMEM] * 2 + [IN_PLACE],
+        input_output_aliases={4: 2},
         scratch_shapes=[
-            pltpu.VMEM((2, count, context, kv_width), bf16),
             pltpu.VMEM(fresh.shape, f32),
-            pltpu.SemaphoreType.DMA((count,)),
-            pltpu.SemaphoreType.DMA((count,)),
-            pltpu.SemaphoreType.DMA((count,)),
+            pltpu.SemaphoreType.DMA((len(early) * move_cap,)),
         ],
         compiler_params=PARAMS,
         name="attend_early",
         cost_estimate=lasts(60),
-    )(plan, told, table, pool, fresh, *queries, *[pages[j] for j in early])
-
-    for partners in (middle, late):
+    )(plan, told, kv, fresh, cache, *queries, *[pages[j] for j in early])
+    for partners in (late,):
         attended, cache = pl.pallas_call(
             functools.partial(late_kernel, dims, partners),
             out_shape=[shape(attended.shape, bf16), shape(cache.shape, bf16)],

time: 58.2 us -> 52.9 us (0.909)
  Pallas kernels: 22.3 us -> 15.9 us
  starting transfers between devices: 17.9 us -> 18.5 us
    pallas_call x1, Pallas kernels: 8.73 us -> 2.27 us  [per_device(): pl.pallas_call(functools.partial(early_kernel, dims, early), out_shape=[s...]
    pallas_call x0 -> x1, Pallas kernels: none -> 2.83 us  [per_device(): pl.pallas_call(functools.partial(place_kernel, dims), out_shape=[shape((2...]
    pallas_call x2 -> x1, Pallas kernels: 4.62 us -> 1.82 us  [per_device(): pl.pallas_call(functools.partial(late_kernel, dims, partners), out_shape=...]
    ppermute x12, starting transfers between devices: 17.9 us -> 18.5 us  [swap(): lax.ppermute(x, axis, [(i, i ^ j) for i in range(lax.axis_size(axis))])]
  transfers between devices with their start and end apart: 12 -> 12, of which waited for: 5 -> 6; matrix products, arithmetic and copies ran while one was open for 0% -> 0% of each run, Pallas kernels for 30% -> 22%
where the time goes in v4:
time: 52.9 us; the launch traced here: 52.3 us
  starting transfers between devices  18.5 us (35%)
  waiting for transfers between devices  17.1 us (32%)
  Pallas kernels  15.9 us (30%)
  between operations  0.76 us (1%)
    ppermute x12, starting transfers between devices, swap(): lax.ppermute(x, axis, [(i, i ^ j) for i in range(lax.axis_size(axis))])  18.5 us
    ppermute x12, waiting for transfers between devices, swap(): lax.ppermute(x, axis, [(i, i ^ j) for i in range(lax.axis_size(axis))])  17.1 us
    pallas_call x2, Pallas kernels, stage_pages(): pl.pallas_call(functools.partial(stage_pages_kernel, dims, partners), out...  3.59 us
    pallas_call x1, Pallas kernels, per_device(): pl.pallas_call(functools.partial(place_kernel, dims), out_shape=[shape((2...  2.83 us
    pallas_call x1, Pallas kernels, per_device(): pl.pallas_call(functools.partial(stage_rows_kernel, dims), out_shape=[mes...  2.54 us
    pallas_call x1, Pallas kernels, per_device(): pl.pallas_call(functools.partial(early_kernel, dims, early), out_shape=[s...  2.27 us
    pallas_call x1, Pallas kernels, per_device(): pl.pallas_call(functools.partial(rank_kernel, dims), out_shape=[shape((2...  2.01 us
    pallas_call x1, Pallas kernels, per_device(): pl.pallas_call(functools.partial(late_kernel, dims, partners), out_shape=...  1.82 us
  transfers between devices with their start and end apart: 12, of which 6 were waited for; matrix products, arithmetic and copies ran while one was open for 0% of the time, Pallas kernels for 22%

profile of v4, /device:TPU:0, one launch (start us, length us, event | category | flops | bytes accessed | tf_op | source)
XLA Modules:
  0.0 52.3 jit_solution(9771487744582196699)
XLA Ops:
  0.6 2.5 %stage_rows.1 = (bf16[272,128]{1,0:T(8,128)(2,1)S(1)}, bf16[272,128]{1,0:T(8,128)(2,1)S(1)}, bf16[272,128]{1,0:T(8,128)(2,1)S(1)}, bf16[272,128]{1,0:T(8,128)(2,1)S(1)}, s32[28]{0:T(128)S(1)}) custom-call(s32[16]{0:T(128)} %adapter_of.1, s32[8]{0:T(128)} %adapter_home.1, s32[16]{0:T(128)} %new_group.1, s32[16]{0:T(128)} %cached_len.3, ...), custom_call_target="tpu_custom_call" | custom-call | flops 1000000000 | bytes 3000000 | tf_op jit(solution)/shard_map/stage_rows/pallas_call | solution.py:421
  3.2 4.1 %collective-permute-start = (bf16[272,128]{1,0:T(8,128)(2,1)S(1)}, bf16[272,128]{1,0:T(8,128)(2,1)S(1)}, u32[]{:S(2)}, u32[]{:S(2)}) collective-permute-start(bf16[272,128]{1,0:T(8,128)(2,1)S(1)} %get-tuple-element.23), channel_id=1, source_target_pairs={{0,8},{4,12},{8,0},{12,4},{1,9},{5,13},{9,1},{13,5},{2,10},{6,14},... | collective-permute-start | bytes 208904 | tf_op jit(solution)/shard_map/ppermute | solution.py:379
  7.3 1.6 %collective-permute-start.1 = (bf16[272,128]{1,0:T(8,128)(2,1)S(1)}, bf16[272,128]{1,0:T(8,128)(2,1)S(1)}, u32[]{:S(2)}, u32[]{:S(2)}) collective-permute-start(bf16[272,128]{1,0:T(8,128)(2,1)S(1)} %get-tuple-element.25), channel_id=1, source_target_pairs={{0,4},{4,0},{8,12},{12,8},{1,5},{5,1},{9,13},{13,9},{2,6},{6,2},{1... | collective-permute-start | bytes 208904 | tf_op jit(solution)/shard_map/ppermute | solution.py:379
  8.9 1.6 %collective-permute-done.refs_0_.refs_2_.refs_6_ = bf16[272,128]{1,0:T(8,128)(2,1)S(1)} collective-permute-done((bf16[272,128]{1,0:T(8,128)(2,1)S(1)}, bf16[272,128]{1,0:T(8,128)(2,1)S(1)}, u32[]{:S(2)}, u32[]{:S(2)}) %collective-permute-start) | collective-permute-done | bytes 69664 | tf_op jit(solution)/shard_map/ppermute | solution.py:379
  10.5 1.7 %stage_pages.2._ = bf16[3,2,128,256]{3,2,1,0:T(8,128)(2,1)S(1)} custom-call(s32[28]{0:T(128)S(1)} %get-tuple-element.22.plan, s32[8,16]{1,0:T(8,128)} %bitcast.27, bf16[2,128,16,256]{3,2,1,0:T(8,128)(2,1)} %pool.5, bf16[272,128]{1,0:T(8,128)(2,1)S(1)} %collective-permute-done.refs_0_.refs_2_.refs_6_), custom_call_target="tpu_custom_call" | custom-call | flops 100000000 | bytes 300000 | tf_op jit(solution)/shard_map/stage_pages/pallas_call | solution.py:447
  12.2 2.7 %collective-permute-start.9 = (bf16[3,2,128,256]{3,2,1,0:T(8,128)(2,1)S(1)}, bf16[3,2,128,256]{3,2,1,0:T(8,128)(2,1)S(1)}, u32[]{:S(2)}, u32[]{:S(2)}) collective-permute-start(bf16[3,2,128,256]{3,2,1,0:T(8,128)(2,1)S(1)} %stage_pages.2._), channel_id=1, source_target_pairs={{0,8},{4,12},{8,0},{12,4},{1,9},{5,13},{9,1},{13,5},{2,10},{6,14},... | collective-permute-start | bytes 1179656 | tf_op jit(solution)/shard_map/ppermute | solution.py:379
  14.9 0.2 collective-permute-done.2.refs_3_.refs_7_
  15.1 2.0 %rank_products.1 = (f32[32,128]{1,0:T(8,128)S(1)}, s32[64]{0:T(128)S(1)}) custom-call(s32[16]{0:T(128)S(1)} %copy-done.3, bf16[128,2048]{1,0:T(8,128)(2,1)S(1)} %bitcast.24, bf16[3,2,128,256]{3,2,1,0:T(8,128)(2,1)S(1)} %stage_pages.2._, bf16[272,128]{1,0:T(8,128)(2,1)S(1)} %get-tuple-element.24.refs_0_.refs_4_, ...), custom_call_target="tpu_custom_call" | custom-call | flops 10000000000 | bytes 30000000 | tf_op jit(solution)/shard_map/rank_products/pallas_call | solution.py:461
  17.1 0.1 collective-permute-start.5
  17.2 1.6 %collective-permute-start.4 = (f32[32,128]{1,0:T(8,128)S(1)}, f32[32,128]{1,0:T(8,128)S(1)}, u32[]{:S(2)}, u32[]{:S(2)}) collective-permute-start(f32[32,128]{1,0:T(8,128)S(1)} %get-tuple-element.29.refs_0_), channel_id=1, source_target_pairs={{0,2},{1,3},{2,0},{3,1},{4,6},{5,7},{6,4},{7,5},{8,10},{9,11},{10,... | collective-permute-start | bytes 49160 | tf_op jit(solution)/shard_map/ppermute | solution.py:379
  18.8 0.3 collective-permute-start.3
  19.1 1.9 %stage_pages.3 = (bf16[3,2,128,256]{3,2,1,0:T(8,128)(2,1)S(1)}, bf16[3,2,128,256]{3,2,1,0:T(8,128)(2,1)S(1)}) custom-call(s32[28]{0:T(128)S(1)} %get-tuple-element.22.plan, s32[8,16]{1,0:T(8,128)} %bitcast.28, bf16[2,128,16,256]{3,2,1,0:T(8,128)(2,1)} %pool.5), custom_call_target="tpu_custom_call" | custom-call | flops 100000000 | bytes 300000 | tf_op jit(solution)/shard_map/stage_pages/pallas_call | solution.py:447
  21.0 0.1 collective-permute-done.4.refs_2_
  21.0 0.8 %queries.1 = (bf16[128,128]{1,0:T(8,128)(2,1)S(1)}, bf16[128,128]{1,0:T(8,128)(2,1)S(1)}, bf16[128,128]{1,0:T(8,128)(2,1)S(1)}, bf16[128,128]{1,0:T(8,128)(2,1)S(1)}) custom-call(s32[64]{0:T(128)S(1)} %get-tuple-element.27.told, bf16[128,2048]{1,0:T(8,128)(2,1)S(1)} %bitcast.23, bf16[3,2,128,256]{3,2,1,0:T(8,128)(2,1)S(1)} %get-tuple-element.28._, ...), custom_call_target="tpu_custom_call" | custom-call | flops 100000000 | bytes 300000 | tf_op jit(solution)/shard_map/queries/pallas_call | solution.py:482
  21.9 3.8 %collective-permute-start.6 = (bf16[128,128]{1,0:T(8,128)(2,1)S(1)}, bf16[128,128]{1,0:T(8,128)(2,1)S(1)}, u32[]{:S(2)}, u32[]{:S(2)}) collective-permute-start(bf16[128,128]{1,0:T(8,128)(2,1)S(1)} %get-tuple-element.33), channel_id=1, source_target_pairs={{0,4},{4,0},{8,12},{12,8},{1,5},{5,1},{9,13},{13,9},{2,6},{6,2},{1... | collective-permute-start | bytes 98312 | tf_op jit(solution)/shard_map/ppermute | solution.py:379
  25.7 2.4 %collective-permute-start.8 = (bf16[128,128]{1,0:T(8,128)(2,1)S(1)}, bf16[128,128]{1,0:T(8,128)(2,1)S(1)}, u32[]{:S(2)}, u32[]{:S(2)}) collective-permute-start(bf16[128,128]{1,0:T(8,128)(2,1)S(1)} %get-tuple-element.35), channel_id=1, source_target_pairs={{0,12},{4,8},{8,4},{12,0},{1,13},{5,9},{9,5},{13,1},{2,14},{6,10},... | collective-permute-start | bytes 98312 | tf_op jit(solution)/shard_map/ppermute | solution.py:379
  28.1 1.0 %collective-permute-start.10 = (bf16[3,2,128,256]{3,2,1,0:T(8,128)(2,1)S(1)}, bf16[3,2,128,256]{3,2,1,0:T(8,128)(2,1)S(1)}, u32[]{:S(2)}, u32[]{:S(2)}) collective-permute-start(bf16[3,2,128,256]{3,2,1,0:T(8,128)(2,1)S(1)} %get-tuple-element.28._), channel_id=1, source_target_pairs={{0,4},{4,0},{8,12},{12,8},{1,5},{5,1},{9,13},{13,9},{2,6},{6,2},{1... | collective-permute-start | bytes 1179656 | tf_op jit(solution)/shard_map/ppermute | solution.py:379
  29.1 2.8 %place_pages.1 = (bf16[2,16,128,256]{3,2,1,0:T(8,128)(2,1)}, bf16[2,16,128,256]{3,2,1,0:T(8,128)(2,1)S(1)}) custom-call(s32[64]{0:T(128)S(1)} %get-tuple-element.27.told, s32[8,16]{1,0:T(8,128)} %bitcast.29, bf16[2,128,16,256]{3,2,1,0:T(8,128)(2,1)} %pool.5, bf16[128,128]{1,0:T(8,128)(2,1)S(1)} %get-tuple-element.30._.refs_0_), custom_call_target="tpu_custom_call" | custom-call | flops 100000000 | bytes 300000 | tf_op jit(solution)/shard_map/place_pages/pallas_call | solution.py:495
  32.0 1.0 %collective-permute-start.11 = (bf16[3,2,128,256]{3,2,1,0:T(8,128)(2,1)S(1)}, bf16[3,2,128,256]{3,2,1,0:T(8,128)(2,1)S(1)}, u32[]{:S(2)}, u32[]{:S(2)}) collective-permute-start(bf16[3,2,128,256]{3,2,1,0:T(8,128)(2,1)S(1)} %get-tuple-element.39), channel_id=1, source_target_pairs={{0,12},{4,8},{8,4},{12,0},{1,13},{5,9},{9,5},{13,1},{2,14},{6,10},... | collective-permute-start | bytes 1179656 | tf_op jit(solution)/shard_map/ppermute | solution.py:379
  33.0 1.1 %collective-permute-done.7.refs_2_ = bf16[128,128]{1,0:T(8,128)(2,1)S(1)} collective-permute-done((bf16[128,128]{1,0:T(8,128)(2,1)S(1)}, bf16[128,128]{1,0:T(8,128)(2,1)S(1)}, u32[]{:S(2)}, u32[]{:S(2)}) %collective-permute-start.7) | collective-permute-done | bytes 32800 | tf_op jit(solution)/shard_map/ppermute | solution.py:379
  34.1 2.3 %attend_early.1 = (bf16[16,32,128]{2,1,0:T(8,128)(2,1)}, bf16[16,32,128]{2,1,0:T(8,128)(2,1)S(1)}, bf16[2,16,128,256]{3,2,1,0:T(8,128)(2,1)}) custom-call(s32[28]{0:T(128)S(1)} %get-tuple-element.22.plan, s32[64]{0:T(128)S(1)} %get-tuple-element.27.told, bf16[2,16,128,256]{3,2,1,0:T(8,128)(2,1)S(1)} %get-tuple-element.31.kv, ...), custom_call_target="tpu_custom_call", output_to_operand_aliasing={{2}: (4, {})} | custom-call | flops 60000002048 | bytes 180000000 | tf_op jit(solution)/shard_map/attend_early/pallas_call | solution.py:505
  36.4 11.8 %collective-permute-done.11.refs_1_ = bf16[3,2,128,256]{3,2,1,0:T(8,128)(2,1)S(1)} collective-permute-done((bf16[3,2,128,256]{3,2,1,0:T(8,128)(2,1)S(1)}, bf16[3,2,128,256]{3,2,1,0:T(8,128)(2,1)S(1)}, u32[]{:S(2)}, u32[]{:S(2)}) %collective-permute-start.11) | collective-permute-done | bytes 393248 | tf_op jit(solution)/shard_map/ppermute | solution.py:379
  48.1 2.4 %collective-permute-done.10.refs_0_ = bf16[3,2,128,256]{3,2,1,0:T(8,128)(2,1)S(1)} collective-permute-done((bf16[3,2,128,256]{3,2,1,0:T(8,128)(2,1)S(1)}, bf16[3,2,128,256]{3,2,1,0:T(8,128)(2,1)S(1)}, u32[]{:S(2)}, u32[]{:S(2)}) %collective-permute-start.10) | collective-permute-done | bytes 393248 | tf_op jit(solution)/shard_map/ppermute | solution.py:379
  50.5 1.8 %attend_arrived.1 = (bf16[16,32,128]{2,1,0:T(8,128)(2,1)}, bf16[2,16,128,256]{3,2,1,0:T(8,128)(2,1)}) custom-call(s32[64]{0:T(128)S(1)} %get-tuple-element.27.told, bf16[128,128]{1,0:T(8,128)(2,1)S(1)} %bitcast.26, bf16[16,32,128]{2,1,0:T(8,128)(2,1)S(1)} %get-tuple-element.36.queries, ...), custom_call_target="tpu_custom_call", output_to_operand_aliasing={{0}: (3, {}), {1}: (4, {})} | custom-call | flops 1000000000 | bytes 3000000 | tf_op jit(solution)/shard_map/attend_arrived/pallas_call | solution.py:520
  (16 shorter events, 0.1 us)
Async XLA Ops:
  3.2 11.9 %copy-start.1 = (bf16[2,64,2048]{2,1,0:T(8,128)(2,1)S(1)}, bf16[2,64,2048]{2,1,0:T(8,128)(2,1)}, u32[]{:S(2)}) copy-start(bf16[2,64,2048]{2,1,0:T(8,128)(2,1)} %param.16) | copy-start | bytes 1572868
  3.2 11.9 %copy-start.3 = (s32[16]{0:T(128)S(1)}, s32[16]{0:T(128)}, u32[]{:S(2)}) copy-start(s32[16]{0:T(128)} %cached_len.3) | copy-start | bytes 196
  3.2 7.3 %collective-permute-start = (bf16[272,128]{1,0:T(8,128)(2,1)S(1)}, bf16[272,128]{1,0:T(8,128)(2,1)S(1)}, u32[]{:S(2)}, u32[]{:S(2)}) collective-permute-start(bf16[272,128]{1,0:T(8,128)(2,1)S(1)} %get-tuple-element.23), channel_id=1, source_target_pairs={{0,8},{4,12},{8,0},{12,4},{1,9},{5,13},{9,1},{13,5},{2,10},{6,14},... | collective-permute-start | bytes 208904 | tf_op jit(solution)/shard_map/ppermute | solution.py:379
  7.3 7.6 %collective-permute-start.1 = (bf16[272,128]{1,0:T(8,128)(2,1)S(1)}, bf16[272,128]{1,0:T(8,128)(2,1)S(1)}, u32[]{:S(2)}, u32[]{:S(2)}) collective-permute-start(bf16[272,128]{1,0:T(8,128)(2,1)S(1)} %get-tuple-element.25), channel_id=1, source_target_pairs={{0,4},{4,0},{8,12},{12,8},{1,5},{5,1},{9,13},{13,9},{2,6},{6,2},{1... | collective-permute-start | bytes 208904 | tf_op jit(solution)/shard_map/ppermute | solution.py:379
  8.9 6.2 %collective-permute-start.2 = (bf16[272,128]{1,0:T(8,128)(2,1)S(1)}, bf16[272,128]{1,0:T(8,128)(2,1)S(1)}, u32[]{:S(2)}, u32[]{:S(2)}) collective-permute-start(bf16[272,128]{1,0:T(8,128)(2,1)S(1)} %get-tuple-element.26), channel_id=1, source_target_pairs={{0,12},{4,8},{8,4},{12,0},{1,13},{5,9},{9,5},{13,1},{2,14},{6,10},... | collective-permute-start | bytes 208904 | tf_op jit(solution)/shard_map/ppermute | solution.py:379
  12.2 21.9 %collective-permute-start.9 = (bf16[3,2,128,256]{3,2,1,0:T(8,128)(2,1)S(1)}, bf16[3,2,128,256]{3,2,1,0:T(8,128)(2,1)S(1)}, u32[]{:S(2)}, u32[]{:S(2)}) collective-permute-start(bf16[3,2,128,256]{3,2,1,0:T(8,128)(2,1)S(1)} %stage_pages.2._), channel_id=1, source_target_pairs={{0,8},{4,12},{8,0},{12,4},{1,9},{5,13},{9,1},{13,5},{2,10},{6,14},... | collective-permute-start | bytes 1179656 | tf_op jit(solution)/shard_map/ppermute | solution.py:379
  17.1 3.9 %copy-start = (bf16[2,64,2048]{2,1,0:T(8,128)(2,1)S(1)}, bf16[2,64,2048]{2,1,0:T(8,128)(2,1)}, u32[]{:S(2)}) copy-start(bf16[2,64,2048]{2,1,0:T(8,128)(2,1)} %param.17) | copy-start | bytes 1572868
  17.1 3.8 %collective-permute-start.5 = (f32[32,128]{1,0:T(8,128)S(1)}, f32[32,128]{1,0:T(8,128)S(1)}, u32[]{:S(2)}, u32[]{:S(2)}) collective-permute-start(f32[32,128]{1,0:T(8,128)S(1)} %get-tuple-element.29.refs_0_), channel_id=1, source_target_pairs={{0,3},{1,2},{2,1},{3,0},{4,7},{5,6},{6,5},{7,4},{8,11},{9,10},{10,... | collective-permute-start | bytes 49160 | tf_op jit(solution)/shard_map/ppermute | solution.py:379
  17.2 3.8 %collective-permute-start.4 = (f32[32,128]{1,0:T(8,128)S(1)}, f32[32,128]{1,0:T(8,128)S(1)}, u32[]{:S(2)}, u32[]{:S(2)}) collective-permute-start(f32[32,128]{1,0:T(8,128)S(1)} %get-tuple-element.29.refs_0_), channel_id=1, source_target_pairs={{0,2},{1,3},{2,0},{3,1},{4,6},{5,7},{6,4},{7,5},{8,10},{9,11},{10,... | collective-permute-start | bytes 49160 | tf_op jit(solution)/shard_map/ppermute | solution.py:379
  18.8 2.3 %collective-permute-start.3 = (f32[32,128]{1,0:T(8,128)S(1)}, f32[32,128]{1,0:T(8,128)S(1)}, u32[]{:S(2)}, u32[]{:S(2)}) collective-permute-start(f32[32,128]{1,0:T(8,128)S(1)} %get-tuple-element.29.refs_0_), channel_id=1, source_target_pairs={{0,1},{1,0},{2,3},{3,2},{4,5},{5,4},{6,7},{7,6},{8,9},{9,8},{10,11... | collective-permute-start | bytes 49160 | tf_op jit(solution)/shard_map/ppermute | solution.py:379
  20.9 13.1 %copy-start.2 = (bf16[16,2,2,256]{3,2,1,0:T(2,128)(2,1)S(1)}, bf16[16,2,2,256]{3,2,1,0:T(2,128)(2,1)}, u32[]{:S(2)}) copy-start(bf16[16,2,2,256]{3,2,1,0:T(2,128)(2,1)} %param.13) | copy-start | bytes 98308
  21.9 10.1 %collective-permute-start.6 = (bf16[128,128]{1,0:T(8,128)(2,1)S(1)}, bf16[128,128]{1,0:T(8,128)(2,1)S(1)}, u32[]{:S(2)}, u32[]{:S(2)}) collective-permute-start(bf16[128,128]{1,0:T(8,128)(2,1)S(1)} %get-tuple-element.33), channel_id=1, source_target_pairs={{0,4},{4,0},{8,12},{12,8},{1,5},{5,1},{9,13},{13,9},{2,6},{6,2},{1... | collective-permute-start | bytes 98312 | tf_op jit(solution)/shard_map/ppermute | solution.py:379
  25.6 8.4 %collective-permute-start.7 = (bf16[128,128]{1,0:T(8,128)(2,1)S(1)}, bf16[128,128]{1,0:T(8,128)(2,1)S(1)}, u32[]{:S(2)}, u32[]{:S(2)}) collective-permute-start(bf16[128,128]{1,0:T(8,128)(2,1)S(1)} %get-tuple-element.34), channel_id=1, source_target_pairs={{0,8},{4,12},{8,0},{12,4},{1,9},{5,13},{9,1},{13,5},{2,10},{6,14},... | collective-permute-start | bytes 98312 | tf_op jit(solution)/shard_map/ppermute | solution.py:379
  25.7 8.4 %collective-permute-start.8 = (bf16[128,128]{1,0:T(8,128)(2,1)S(1)}, bf16[128,128]{1,0:T(8,128)(2,1)S(1)}, u32[]{:S(2)}, u32[]{:S(2)}) collective-permute-start(bf16[128,128]{1,0:T(8,128)(2,1)S(1)} %get-tuple-element.35), channel_id=1, source_target_pairs={{0,12},{4,8},{8,4},{12,0},{1,13},{5,9},{9,5},{13,1},{2,14},{6,10},... | collective-permute-start | bytes 98312 | tf_op jit(solution)/shard_map/ppermute | solution.py:379
  28.1 22.4 %collective-permute-start.10 = (bf16[3,2,128,256]{3,2,1,0:T(8,128)(2,1)S(1)}, bf16[3,2,128,256]{3,2,1,0:T(8,128)(2,1)S(1)}, u32[]{:S(2)}, u32[]{:S(2)}) collective-permute-start(bf16[3,2,128,256]{3,2,1,0:T(8,128)(2,1)S(1)} %get-tuple-element.28._), channel_id=1, source_target_pairs={{0,4},{4,0},{8,12},{12,8},{1,5},{5,1},{9,13},{13,9},{2,6},{6,2},{1... | collective-permute-start | bytes 1179656 | tf_op jit(solution)/shard_map/ppermute | solution.py:379
  32.0 16.1 %collective-permute-start.11 = (bf16[3,2,128,256]{3,2,1,0:T(8,128)(2,1)S(1)}, bf16[3,2,128,256]{3,2,1,0:T(8,128)(2,1)S(1)}, u32[]{:S(2)}, u32[]{:S(2)}) collective-permute-start(bf16[3,2,128,256]{3,2,1,0:T(8,128)(2,1)S(1)} %get-tuple-element.39), channel_id=1, source_target_pairs={{0,12},{4,8},{8,4},{12,0},{1,13},{5,9},{9,5},{13,1},{2,14},{6,10},... | collective-permute-start | bytes 1179656 | tf_op jit(solution)/shard_map/ppermute | solution.py:379

commit v5 on v4

--- a/solution.py
+++ b/solution.py
@@ -35,16 +35,16 @@
 def stage_rows_kernel(dims, adapter_of, adapter_home, new_group, cached_len, hidden, frozen, *refs):
     groups, own_cap, move_cap, stores = dims
     messages, plan = refs[:groups], refs[groups]
-    counts, picks, meta, *held, held_sems, sems = refs[groups + 1 :]
+    counts, picks, *held, held_sems = refs[groups + 1 :]
     count, depth, _ = hidden.shape
-    lists = (adapter_home, adapter_of, new_group, cached_len)
+    lists = (adapter_home, adapter_of, new_group, cached_len, hidden, frozen)
     copies = [
         pltpu.make_async_copy(source, target, held_sems.at[i])
         for i, (source, target) in enumerate(zip(lists, held))
     ]
     for copy in copies:
         copy.start()
-    adapter_home, adapter_of, new_group, cached_len = held
+    adapter_home, adapter_of, new_group, cached_len, hidden, frozen = held
     me = lax.axis_index("req")
     for i in range(groups * (own_cap + move_cap)):
         plan[i] = -1
@@ -52,7 +52,7 @@
         counts[j] = 0
         counts[groups + j] = 0
         picks[j] = 0
-    for copy in copies:
+    for copy in copies[:4]:
         copy.wait()
     for r in range(count):
         store = adapter_home[adapter_of[r]]
@@ -71,33 +71,51 @@
 
     lane = lax.broadcasted_iota(jnp.int32, (TILE, LANES), 1)
     for j in range(groups):
-        for k in range(own_cap):
-            source = jnp.maximum(plan[j * own_cap + k], 0)
-            for part, rows in enumerate((hidden, frozen)):
-                pltpu.make_async_copy(
-                    rows.at[source],
-                    messages[j].at[pl.ds((part * own_cap + k) * depth, depth)],
-                    sems.at[j],
-                ).start()
         told = jnp.where(lane == 0, picks[j], 0)
         for k in range(move_cap):
-            slot = plan[(groups * own_cap) + j * move_cap + k]
+            slot = plan[groups * own_cap + j * move_cap + k]
             length = cached_len[jnp.maximum(slot, 0)]
             told = jnp.where(lane == 1 + k, slot, told)
             told = jnp.where(lane == 1 + move_cap + k, length, told)
-        meta[j] = told.astype(jnp.float32).astype(jnp.bfloat16)
-        pltpu.make_async_copy(
-            meta.at[j], messages[j].at[pl.ds(2 * own_cap * depth, TILE)], sems.at[j]
-        ).start()
-    for j in range(groups):
-        pltpu.make_async_copy(messages[j], messages[j], sems.at[j]).wait()
-
-
-def stage_pages_kernel(dims, partners, plan, table, pool, *refs):
+        messages[j][2 * own_cap * depth :, :] = told.astype(jnp.float32).astype(jnp.bfloat16)
+    for part, rows in enumerate((hidden, frozen)):
+        copies[4 + part].wait()
+        for j in range(groups):
+            for k in range(own_cap):
+                source = jnp.maximum(plan[j * own_cap + k], 0)
+                at = (part * own_cap + k) * depth
+                messages[j][at : at + depth, :] = rows[source]
+
+
+def page_routes(groups):
+    half = groups // 2
+
+    def across(j):
+        return tuple(g ^ j for g in range(groups))
+
+    between = [across(j) for j in range(1, groups - 1) if j != half]
+    return between + [across(half)], [across(groups - 1)] if groups > 2 else []
+
+
+def partner(route, me, arriving):
+    if arriving:
+        route = [route.index(g) if g in route else -1 for g in range(len(route))]
+    codes = [g ^ other if other >= 0 else 0 for g, other in enumerate(route)]
+    if len(set(codes)) == 1:
+        return codes[0]
+    chosen = 0
+    for g, code in enumerate(codes):
+        chosen = jnp.where(me == g, code, chosen)
+    return chosen
+
+
+def stage_pages_kernel(dims, routes, plan, table, pool, *refs):
     groups, own_cap, move_cap, _ = dims
-    *outs, sems = refs[-len(partners) - 1 :]
+    *outs, sems = refs[-len(routes) - 1 :]
     page = pool.shape[2]
-    for i, j in enumerate(partners):
+    me = lax.axis_index("req")
+    for i, route in enumerate(routes):
+        j = partner(route, me, False)
         for k in range(move_cap):
             source = jnp.maximum(plan[groups * own_cap + j * move_cap + k], 0)
             for p in range(table.shape[0]):
@@ -106,13 +124,13 @@
                     outs[i].at[k, :, pl.ds(p * page, page)],
                     sems.at[i],
                 ).start()
-    for i in range(len(partners)):
+    for i in range(len(routes)):
         pltpu.make_async_copy(outs[i], outs[i], sems.at[i]).wait()
 
 
-def rank_kernel(dims, cached_len, a_ref, _, *refs):
+def rank_kernel(dims, order, cached_len, a_ref, _, *refs):
     groups, own_cap, move_cap, _ = dims
-    messages = refs[:groups]
+    messages = [refs[order.index(j)] for j in range(groups)]
     partial, told = refs[groups : groups + 2]
     x, meta, meta_scalar, sem = refs[groups + 2 :]
     width = a_ref.shape[1]
@@ -251,7 +269,8 @@
     return results
 
 
-def place_kernel(dims, told, table, pool, _, cache, kv, kv_sems, out_sems):
+def place_kernel(dims, told, table, pool, *refs):
+    cache, kv, kv_sems, out_sems = refs[-4:]
     groups = dims[0]
     count = kv.shape[1]
     page = pool.shape[2]
@@ -278,23 +297,25 @@
             pltpu.make_async_copy(kv.at[:, r], cache.at[:, r], out_sems.at[r]).wait()
 
 
-def arrivals(dims, partners, told, count, pages):
+def arrivals(dims, routes, told, count, pages):
     groups, _, move_cap, _ = dims
+    me = lax.axis_index("req")
     blocks, slots = [], []
-    for i, j in enumerate(partners):
+    for i, route in enumerate(routes):
+        j = partner(route, me, True)
         for k in range(move_cap):
             blocks.append(pages[i].at[k])
             slots.append(told[groups + 3 * count + j * move_cap + k])
     return blocks, slots, [jnp.maximum(slot, 0) for slot in slots]
 
 
-def early_kernel(dims, partners, plan, told, kv, new_kv, cache_in, *refs):
+def early_kernel(dims, routes, plan, told, kv, new_kv, cache_in, *refs):
     groups, own_cap, _, _ = dims
     queries, refs = refs[:groups], refs[groups:]
-    pages, refs = refs[: len(partners)], refs[len(partners) :]
+    pages, refs = refs[: len(routes)], refs[len(routes) :]
     attended, sorted_queries, cache, x, page_sems = refs
     count, depth, _ = attended.shape
-    blocks, slots, places = arrivals(dims, partners, told, count, pages)
+    blocks, slots, places = arrivals(dims, routes, told, count, pages)
     copies = [
         pltpu.make_async_copy(block, cache.at[:, at], page_sems.at[n])
         for n, (block, at) in enumerate(zip(blocks, places))
@@ -330,12 +351,12 @@
         pl.when(slot >= 0)(copy.wait)
 
 
-def late_kernel(dims, partners, told, new_kv, queries, attended_in, cache_in, *refs):
+def late_kernel(dims, routes, told, new_kv, queries, attended_in, cache_in, *refs):
     groups = dims[0]
-    pages, refs = refs[: len(partners)], refs[len(partners) :]
+    pages, refs = refs[: len(routes)], refs[len(routes) :]
     attended, cache, results, x, page_sems, out_sems = refs
     count = queries.shape[0]
-    blocks, slots, places = arrivals(dims, partners, told, count, pages)
+    blocks, slots, places = arrivals(dims, routes, told, count, pages)
     copies = [
         (
             pltpu.make_async_copy(block, cache.at[:, at], page_sems.at[n]),
@@ -405,8 +426,7 @@
     depth = width // LANES * steps
     number = groups * own_cap
     half = max(groups // 2, 1)
-    early = [half]
-    late = [j for j in range(1, groups) if j != half]
+    first, last = page_routes(groups)
     hidden, frozen = to_tiles(hidden_in), to_tiles(frozen_query_rows)
     table, pool = in_hbm(page_table.T, kv_pool)
     fresh = (
@@ -422,44 +442,51 @@
         functools.partial(stage_rows_kernel, dims),
         out_shape=[message] * groups + [shape((groups * (own_cap + move_cap),), i32)],
         in_specs=[IN_PLACE] * 6,
-        out_specs=[IN_PLACE] * groups + [IN_SMEM],
+        out_specs=[IN_VMEM] * groups + [IN_SMEM],
         scratch_shapes=[
             pltpu.SMEM((2 * groups,), i32),
             pltpu.SMEM((groups,), i32),
-            pltpu.VMEM((groups, TILE, LANES), bf16),
             *[
                 pltpu.SMEM(held.shape, i32)
                 for held in (adapter_home, adapter_of, new_group, cached_len)
             ],
-            pltpu.SemaphoreType.DMA((4,)),
-            pltpu.SemaphoreType.DMA((groups,)),
+            pltpu.VMEM(hidden.shape, bf16),
+            pltpu.VMEM(frozen.shape, bf16),
+            pltpu.SemaphoreType.DMA((6,)),
         ],
         compiler_params=PARAMS,
         name="stage_rows",
         cost_estimate=lasts(1),
     )(*in_hbm(adapter_of, adapter_home, new_group, cached_len, hidden, frozen))
     got = {0: messages[0]}
-    for j in range(1, groups):
+    order = [half] + [j for j in range(1, groups) if j != half] + [0]
+    for j in order[:-1]:
         got[j] = swap(messages[j], "req", j)
     got = [got[j] for j in range(groups)]
 
-    def stage_pages(partners, *after):
+    def stage_pages(routes, *after):
         return pl.pallas_call(
-            functools.partial(stage_pages_kernel, dims, partners),
-            out_shape=[shape((move_cap, 2, context, kv_width), bf16)] * len(partners),
+            functools.partial(stage_pages_kernel, dims, routes),
+            out_shape=[shape((move_cap, 2, context, kv_width), bf16)] * len(routes),
             in_specs=[IN_SMEM] * 2 + [IN_PLACE] * (1 + len(after)),
-            out_specs=[IN_PLACE] * len(partners),
-            scratch_shapes=[pltpu.SemaphoreType.DMA((len(partners),))],
+            out_specs=[IN_PLACE] * len(routes),
+            scratch_shapes=[pltpu.SemaphoreType.DMA((len(routes),))],
             compiler_params=PARAMS,
             name="stage_pages",
             cost_estimate=lasts(0.1),
         )(plan, table, pool, *after)
 
-    staged = stage_pages(early, got[half])
-    pages = {j: swap(x, "req", j) for j, x in zip(early, staged)}
+    def send_pages(routes, staged):
+        for route, x in zip(routes, staged):
+            pairs = [(g, other) for g, other in enumerate(route) if other >= 0]
+            pages[route] = lax.ppermute(x, "req", pairs)
+
+    pages = {}
+    first_pages = stage_pages(first) if first else [hidden]
+    send_pages(first, first_pages)
 
     partial, told = pl.pallas_call(
-        functools.partial(rank_kernel, dims),
+        functools.partial(rank_kernel, dims, order),
         out_shape=[
             shape((2 * number, stores * rank), f32),
             shape((groups + 3 * count + groups * move_cap,), i32),
@@ -475,10 +502,10 @@
         compiler_params=PARAMS,
         name="rank_products",
         cost_estimate=lasts(10),
-    )(cached_len, a_store.reshape(stores * rank, width), staged[-1], *got)
+    )(cached_len, a_store.reshape(stores * rank, width), first_pages[-1], *[got[j] for j in order])
     partials = [partial] + [swap(partial, "mp", j) for j in range(1, shards)]
 
-    last_pages = stage_pages(late)
+    last_pages = stage_pages(last, partial)
     queries = pl.pallas_call(
         functools.partial(query_kernel, dims, shards),
         out_shape=[shape((own_cap * depth, LANES), bf16)] * groups,
@@ -488,51 +515,51 @@
         compiler_params=PARAMS,
         name="queries",
         cost_estimate=lasts(0.1),
-    )(told, b_store.reshape(stores * rank, width), last_pages[0], *partials, *got)
+    )(told, b_store.reshape(stores * rank, width), last_pages[-1], *partials, *got)
     queries = [queries[0]] + [swap(queries[j], "req", j) for j in range(1, groups)]
-    pages.update((j, swap(x, "req", j)) for j, x in zip(late, last_pages))
+    send_pages(last, last_pages)
 
     cache, kv = pl.pallas_call(
         functools.partial(place_kernel, dims),
         out_shape=[shape((2, count, context, kv_width), bf16)] * 2,
-        in_specs=[IN_SMEM] * 2 + [IN_PLACE] * 2,
+        in_specs=[IN_SMEM] * 2 + [IN_PLACE] * (1 + len(first[:-1])),
         out_specs=[IN_PLACE] * 2,
         scratch_shapes=[pltpu.SemaphoreType.DMA((count,))] * 2,
         compiler_params=PARAMS,
         name="place_pages",
         cost_estimate=lasts(0.1),
-    )(told, table, pool, queries[0])
+    )(told, table, pool, *[pages[route] for route in first[:-1]])
     attended, sorted_queries, cache = pl.pallas_call(
-        functools.partial(early_kernel, dims, early),
+        functools.partial(early_kernel, dims, first),
         out_shape=[shape((count, depth, LANES), bf16)] * 2 + [shape(cache.shape, bf16)],
-        in_specs=[IN_SMEM] * 2 + [IN_VMEM] * 2 + [IN_PLACE] + [IN_VMEM] * (groups + len(early)),
+        in_specs=[IN_SMEM] * 2 + [IN_VMEM] * 2 + [IN_PLACE] + [IN_VMEM] * (groups + len(first)),
         out_specs=[IN_VMEM] * 2 + [IN_PLACE],
         input_output_aliases={4: 2},
         scratch_shapes=[
             pltpu.VMEM(fresh.shape, f32),
-            pltpu.SemaphoreType.DMA((len(early) * move_cap,)),
+            pltpu.SemaphoreType.DMA((len(first) * move_cap,)),
         ],
         compiler_params=PARAMS,
         name="attend_early",
         cost_estimate=lasts(60),
-    )(plan, told, kv, fresh, cache, *queries, *[pages[j] for j in early])
-    for partners in (late,):
+    )(plan, told, kv, fresh, cache, *queries, *[pages[route] for route in first])
+    for routes in (last,):
         attended, cache = pl.pallas_call(
-            functools.partial(late_kernel, dims, partners),
+            functools.partial(late_kernel, dims, routes),
             out_shape=[shape(attended.shape, bf16), shape(cache.shape, bf16)],
-            in_specs=[IN_SMEM, IN_VMEM, IN_VMEM] + [IN_PLACE] * 2 + [IN_VMEM] * len(partners),
+            in_specs=[IN_SMEM, IN_VMEM, IN_VMEM] + [IN_PLACE] * 2 + [IN_VMEM] * len(routes),
             out_specs=[IN_PLACE, IN_PLACE],
             input_output_aliases={3: 0, 4: 1},
             scratch_shapes=[
-                pltpu.VMEM((len(partners) * move_cap, depth, LANES), bf16),
+                pltpu.VMEM((len(routes) * move_cap, depth, LANES), bf16),
                 pltpu.VMEM(fresh.shape, f32),
-                pltpu.SemaphoreType.DMA((len(partners) * move_cap,)),
-                pltpu.SemaphoreType.DMA((len(partners) * move_cap,)),
+                pltpu.SemaphoreType.DMA((len(routes) * move_cap,)),
+                pltpu.SemaphoreType.DMA((len(routes) * move_cap,)),
             ],
             compiler_params=PARAMS,
             name="attend_arrived",
             cost_estimate=lasts(1),
-        )(told, fresh, sorted_queries, attended, cache, *[pages[j] for j in partners])
+        )(told, fresh, sorted_queries, attended, cache, *[pages[route] for route in routes])
     return from_tiles(attended, steps), cache
 
 

time: 52.9 us -> 50.8 us (0.960)
  the two profiles are of different devices: /device:TPU:0 before, /device:TPU:8 now
where the time goes in v5:
time: 50.8 us; the launch traced here: 50.1 us
  waiting for transfers between devices  20.4 us (40%)
  Pallas kernels  15.2 us (30%)
  starting transfers between devices  13.7 us (27%)
  between operations  0.77 us (2%)
    ppermute x3, waiting for transfers between devices, send_pages(): pages[route] = lax.ppermute(x, 'req', pairs)  11.2 us
    ppermute x9, starting transfers between devices, swap(): lax.ppermute(x, axis, [(i, i ^ j) for i in range(lax.axis_size(axis))])  9.38 us
    ppermute x9, waiting for transfers between devices, swap(): lax.ppermute(x, axis, [(i, i ^ j) for i in range(lax.axis_size(axis))])  9.22 us
    ppermute x3, starting transfers between devices, send_pages(): pages[route] = lax.ppermute(x, 'req', pairs)  4.35 us
    pallas_call x2, Pallas kernels, stage_pages(): pl.pallas_call(functools.partial(stage_pages_kernel, dims, routes), out_s...  3.58 us
    pallas_call x1, Pallas kernels, per_device(): pl.pallas_call(functools.partial(place_kernel, dims), out_shape=[shape((2...  2.84 us
    pallas_call x1, Pallas kernels, per_device(): pl.pallas_call(functools.partial(early_kernel, dims, first), out_shape=[s...  2.44 us
    pallas_call x1, Pallas kernels, per_device(): pl.pallas_call(functools.partial(rank_kernel, dims, order), out_shape=[sh...  1.99 us
  transfers between devices with their start and end apart: 12, of which 5 were waited for; matrix products, arithmetic and copies ran while one was open for 0% of the time, Pallas kernels for 23%

profile of v5, /device:TPU:8, one launch (start us, length us, event | category | flops | bytes accessed | tf_op | source)
XLA Modules:
  0.0 50.1 jit_solution(14305700937451473022)
XLA Ops:
  0.7 1.8 %stage_rows.1 = (bf16[272,128]{1,0:T(8,128)(2,1)S(1)}, bf16[272,128]{1,0:T(8,128)(2,1)S(1)}, bf16[272,128]{1,0:T(8,128)(2,1)S(1)}, bf16[272,128]{1,0:T(8,128)(2,1)S(1)}, s32[28]{0:T(128)S(1)}) custom-call(s32[16]{0:T(128)} %adapter_of.1, s32[8]{0:T(128)} %adapter_home.1, s32[16]{0:T(128)} %new_group.1, s32[16]{0:T(128)} %cached_len.3, ...), custom_call_target="tpu_custom_call" | custom-call | flops 1000000000 | bytes 3000000 | tf_op jit(solution)/shard_map/stage_rows/pallas_call | solution.py:441
  2.4 2.7 %collective-permute-start = (bf16[272,128]{1,0:T(8,128)(2,1)S(1)}, bf16[272,128]{1,0:T(8,128)(2,1)S(1)}, u32[]{:S(2)}, u32[]{:S(2)}) collective-permute-start(bf16[272,128]{1,0:T(8,128)(2,1)S(1)} %get-tuple-element.24), channel_id=1, source_target_pairs={{0,8},{4,12},{8,0},{12,4},{1,9},{5,13},{9,1},{13,5},{2,10},{6,14},... | collective-permute-start | bytes 208904 | tf_op jit(solution)/shard_map/ppermute | solution.py:400
  5.1 0.4 collective-permute-start.1
  5.5 0.5 collective-permute-start.2
  6.0 1.9 %stage_pages.2 = (bf16[3,2,128,256]{3,2,1,0:T(8,128)(2,1)S(1)}, bf16[3,2,128,256]{3,2,1,0:T(8,128)(2,1)S(1)}) custom-call(s32[28]{0:T(128)S(1)} %get-tuple-element.22.plan, s32[8,16]{1,0:T(8,128)} %bitcast.27, bf16[2,128,16,256]{3,2,1,0:T(8,128)(2,1)} %pool.5), custom_call_target="tpu_custom_call" | custom-call | flops 100000000 | bytes 300000 | tf_op jit(solution)/shard_map/stage_pages/pallas_call | solution.py:468
  7.8 1.2 %collective-permute-start.3 = (bf16[3,2,128,256]{3,2,1,0:T(8,128)(2,1)S(1)}, bf16[3,2,128,256]{3,2,1,0:T(8,128)(2,1)S(1)}, u32[]{:S(2)}, u32[]{:S(2)}) collective-permute-start(bf16[3,2,128,256]{3,2,1,0:T(8,128)(2,1)S(1)} %get-tuple-element.29), channel_id=1, source_target_pairs={{0,4},{4,0},{8,12},{12,8},{1,5},{5,1},{9,13},{13,9},{2,6},{6,2},{1... | collective-permute-start | bytes 1179656 | tf_op jit(solution)/shard_map/ppermute | solution.py:482
  9.0 2.4 %collective-permute-start.10 = (bf16[3,2,128,256]{3,2,1,0:T(8,128)(2,1)S(1)}, bf16[3,2,128,256]{3,2,1,0:T(8,128)(2,1)S(1)}, u32[]{:S(2)}, u32[]{:S(2)}) collective-permute-start(bf16[3,2,128,256]{3,2,1,0:T(8,128)(2,1)S(1)} %get-tuple-element.23._), channel_id=1, source_target_pairs={{0,8},{4,12},{8,0},{12,4},{1,9},{5,13},{9,1},{13,5},{2,10},{6,14},... | collective-permute-start | bytes 1179656 | tf_op jit(solution)/shard_map/ppermute | solution.py:482
  11.5 2.0 %rank_products.1 = (f32[32,128]{1,0:T(8,128)S(1)}, s32[64]{0:T(128)S(1)}) custom-call(s32[16]{0:T(128)S(1)} %copy-done.3, bf16[128,2048]{1,0:T(8,128)(2,1)S(1)} %bitcast.24, bf16[3,2,128,256]{3,2,1,0:T(8,128)(2,1)S(1)} %get-tuple-element.23._, bf16[272,128]{1,0:T(8,128)(2,1)S(1)} %collective-permute-done.refs_0_.refs_6_, ...), custom_call_target="tpu_custom_call" | custom-call | flops 10000000000 | bytes 30000000 | tf_op jit(solution)/shard_map/rank_products/pallas_call | solution.py:488
  13.5 0.1 collective-permute-start.6
  13.6 1.6 %collective-permute-start.5 = (f32[32,128]{1,0:T(8,128)S(1)}, f32[32,128]{1,0:T(8,128)S(1)}, u32[]{:S(2)}, u32[]{:S(2)}) collective-permute-start(f32[32,128]{1,0:T(8,128)S(1)} %get-tuple-element.32.refs_0_), channel_id=1, source_target_pairs={{0,2},{1,3},{2,0},{3,1},{4,6},{5,7},{6,4},{7,5},{8,10},{9,11},{10,... | collective-permute-start | bytes 49160 | tf_op jit(solution)/shard_map/ppermute | solution.py:400
  15.2 0.3 collective-permute-start.4
  15.5 1.7 %stage_pages.3._ = bf16[3,2,128,256]{3,2,1,0:T(8,128)(2,1)S(1)} custom-call(s32[28]{0:T(128)S(1)} %get-tuple-element.22.plan, s32[8,16]{1,0:T(8,128)} %bitcast.28, bf16[2,128,16,256]{3,2,1,0:T(8,128)(2,1)} %pool.5, f32[32,128]{1,0:T(8,128)S(1)} %get-tuple-element.32.refs_0_), custom_call_target="tpu_custom_call" | custom-call | flops 100000000 | bytes 300000 | tf_op jit(solution)/shard_map/stage_pages/pallas_call | solution.py:468
  17.2 0.2 collective-permute-done.5.refs_2_
  17.4 0.8 %queries.1 = (bf16[128,128]{1,0:T(8,128)(2,1)S(1)}, bf16[128,128]{1,0:T(8,128)(2,1)S(1)}, bf16[128,128]{1,0:T(8,128)(2,1)S(1)}, bf16[128,128]{1,0:T(8,128)(2,1)S(1)}) custom-call(s32[64]{0:T(128)S(1)} %get-tuple-element.28.told, bf16[128,2048]{1,0:T(8,128)(2,1)S(1)} %bitcast.23, bf16[3,2,128,256]{3,2,1,0:T(8,128)(2,1)S(1)} %stage_pages.3._, ...), custom_call_target="tpu_custom_call" | custom-call | flops 100000000 | bytes 300000 | tf_op jit(solution)/shard_map/queries/pallas_call | solution.py:509
  18.3 2.3 %collective-permute-start.7 = (bf16[128,128]{1,0:T(8,128)(2,1)S(1)}, bf16[128,128]{1,0:T(8,128)(2,1)S(1)}, u32[]{:S(2)}, u32[]{:S(2)}) collective-permute-start(bf16[128,128]{1,0:T(8,128)(2,1)S(1)} %get-tuple-element.34), channel_id=1, source_target_pairs={{0,4},{4,0},{8,12},{12,8},{1,5},{5,1},{9,13},{13,9},{2,6},{6,2},{1... | collective-permute-start | bytes 98312 | tf_op jit(solution)/shard_map/ppermute | solution.py:400
  20.6 1.6 %collective-permute-start.8 = (bf16[128,128]{1,0:T(8,128)(2,1)S(1)}, bf16[128,128]{1,0:T(8,128)(2,1)S(1)}, u32[]{:S(2)}, u32[]{:S(2)}) collective-permute-start(bf16[128,128]{1,0:T(8,128)(2,1)S(1)} %get-tuple-element.35), channel_id=1, source_target_pairs={{0,8},{4,12},{8,0},{12,4},{1,9},{5,13},{9,1},{13,5},{2,10},{6,14},... | collective-permute-start | bytes 98312 | tf_op jit(solution)/shard_map/ppermute | solution.py:400
  22.2 5.2 %collective-permute-done.3.refs_0_.refs_4_ = bf16[3,2,128,256]{3,2,1,0:T(8,128)(2,1)S(1)} collective-permute-done((bf16[3,2,128,256]{3,2,1,0:T(8,128)(2,1)S(1)}, bf16[3,2,128,256]{3,2,1,0:T(8,128)(2,1)S(1)}, u32[]{:S(2)}, u32[]{:S(2)}) %collective-permute-start.3) | collective-permute-done | bytes 393248 | tf_op jit(solution)/shard_map/ppermute | solution.py:482
  27.4 0.7 %collective-permute-start.11 = (bf16[3,2,128,256]{3,2,1,0:T(8,128)(2,1)S(1)}, bf16[3,2,128,256]{3,2,1,0:T(8,128)(2,1)S(1)}, u32[]{:S(2)}, u32[]{:S(2)}) collective-permute-start(bf16[3,2,128,256]{3,2,1,0:T(8,128)(2,1)S(1)} %stage_pages.3._), channel_id=1, source_target_pairs={{0,12},{4,8},{8,4},{12,0},{1,13},{5,9},{9,5},{13,1},{2,14},{6,10},... | collective-permute-start | bytes 1179656 | tf_op jit(solution)/shard_map/ppermute | solution.py:482
  28.1 2.8 %place_pages.1 = (bf16[2,16,128,256]{3,2,1,0:T(8,128)(2,1)}, bf16[2,16,128,256]{3,2,1,0:T(8,128)(2,1)S(1)}) custom-call(s32[64]{0:T(128)S(1)} %get-tuple-element.28.told, s32[8,16]{1,0:T(8,128)} %bitcast.29, bf16[2,128,16,256]{3,2,1,0:T(8,128)(2,1)} %pool.5, bf16[3,2,128,256]{3,2,1,0:T(8,128)(2,1)S(1)} %collective-permute-done.3.refs_0_.refs_4_), custom_call_target="tpu_custom_call" | custom-call | flops 100000000 | bytes 300000 | tf_op jit(solution)/shard_map/place_pages/pallas_call | solution.py:522
  31.0 8.2 %collective-permute-done.8.refs_2_ = bf16[128,128]{1,0:T(8,128)(2,1)S(1)} collective-permute-done((bf16[128,128]{1,0:T(8,128)(2,1)S(1)}, bf16[128,128]{1,0:T(8,128)(2,1)S(1)}, u32[]{:S(2)}, u32[]{:S(2)}) %collective-permute-start.8) | collective-permute-done | bytes 32800 | tf_op jit(solution)/shard_map/ppermute | solution.py:400
  39.2 0.7 %collective-permute-done.9.refs_3_ = bf16[128,128]{1,0:T(8,128)(2,1)S(1)} collective-permute-done((bf16[128,128]{1,0:T(8,128)(2,1)S(1)}, bf16[128,128]{1,0:T(8,128)(2,1)S(1)}, u32[]{:S(2)}, u32[]{:S(2)}) %collective-permute-start.9) | collective-permute-done | bytes 32800 | tf_op jit(solution)/shard_map/ppermute | solution.py:400
  39.9 2.4 %attend_early.1 = (bf16[16,32,128]{2,1,0:T(8,128)(2,1)}, bf16[16,32,128]{2,1,0:T(8,128)(2,1)S(1)}, bf16[2,16,128,256]{3,2,1,0:T(8,128)(2,1)}) custom-call(s32[28]{0:T(128)S(1)} %get-tuple-element.22.plan, s32[64]{0:T(128)S(1)} %get-tuple-element.28.told, bf16[2,16,128,256]{3,2,1,0:T(8,128)(2,1)S(1)} %get-tuple-element.30.kv, ...), custom_call_target="tpu_custom_call", output_to_operand_aliasing={{2}: (4, {})} | custom-call | flops 60000002048 | bytes 180000000 | tf_op jit(solution)/shard_map/attend_early/pallas_call | solution.py:532
  42.4 6.0 %collective-permute-done.11.refs_0_ = bf16[3,2,128,256]{3,2,1,0:T(8,128)(2,1)S(1)} collective-permute-done((bf16[3,2,128,256]{3,2,1,0:T(8,128)(2,1)S(1)}, bf16[3,2,128,256]{3,2,1,0:T(8,128)(2,1)S(1)}, u32[]{:S(2)}, u32[]{:S(2)}) %collective-permute-start.11) | collective-permute-done | bytes 393248 | tf_op jit(solution)/shard_map/ppermute | solution.py:482
  48.4 1.7 %attend_arrived.1 = (bf16[16,32,128]{2,1,0:T(8,128)(2,1)}, bf16[2,16,128,256]{3,2,1,0:T(8,128)(2,1)}) custom-call(s32[64]{0:T(128)S(1)} %get-tuple-element.28.told, bf16[128,128]{1,0:T(8,128)(2,1)S(1)} %bitcast.26, bf16[16,32,128]{2,1,0:T(8,128)(2,1)S(1)} %get-tuple-element.37.queries, ...), custom_call_target="tpu_custom_call", output_to_operand_aliasing={{0}: (3, {}), {1}: (4, {})} | custom-call | flops 1000000000 | bytes 3000000 | tf_op jit(solution)/shard_map/attend_arrived/pallas_call | solution.py:547
  (16 shorter events, 0.0 us)
Async XLA Ops:
  0.6 10.9 %copy-start.1 = (bf16[2,64,2048]{2,1,0:T(8,128)(2,1)S(1)}, bf16[2,64,2048]{2,1,0:T(8,128)(2,1)}, u32[]{:S(2)}) copy-start(bf16[2,64,2048]{2,1,0:T(8,128)(2,1)} %param.16) | copy-start | bytes 1572868
  0.6 10.9 %copy-start.3 = (s32[16]{0:T(128)S(1)}, s32[16]{0:T(128)}, u32[]{:S(2)}) copy-start(s32[16]{0:T(128)} %cached_len.3) | copy-start | bytes 196
  2.4 9.1 %collective-permute-start = (bf16[272,128]{1,0:T(8,128)(2,1)S(1)}, bf16[272,128]{1,0:T(8,128)(2,1)S(1)}, u32[]{:S(2)}, u32[]{:S(2)}) collective-permute-start(bf16[272,128]{1,0:T(8,128)(2,1)S(1)} %get-tuple-element.24), channel_id=1, source_target_pairs={{0,8},{4,12},{8,0},{12,4},{1,9},{5,13},{9,1},{13,5},{2,10},{6,14},... | collective-permute-start | bytes 208904 | tf_op jit(solution)/shard_map/ppermute | solution.py:400
  5.1 6.4 %collective-permute-start.1 = (bf16[272,128]{1,0:T(8,128)(2,1)S(1)}, bf16[272,128]{1,0:T(8,128)(2,1)S(1)}, u32[]{:S(2)}, u32[]{:S(2)}) collective-permute-start(bf16[272,128]{1,0:T(8,128)(2,1)S(1)} %get-tuple-element.25), channel_id=1, source_target_pairs={{0,4},{4,0},{8,12},{12,8},{1,5},{5,1},{9,13},{13,9},{2,6},{6,2},{1... | collective-permute-start | bytes 208904 | tf_op jit(solution)/shard_map/ppermute | solution.py:400
  5.5 6.0 %collective-permute-start.2 = (bf16[272,128]{1,0:T(8,128)(2,1)S(1)}, bf16[272,128]{1,0:T(8,128)(2,1)S(1)}, u32[]{:S(2)}, u32[]{:S(2)}) collective-permute-start(bf16[272,128]{1,0:T(8,128)(2,1)S(1)} %get-tuple-element.26), channel_id=1, source_target_pairs={{0,12},{4,8},{8,4},{12,0},{1,13},{5,9},{9,5},{13,1},{2,14},{6,10},... | collective-permute-start | bytes 208904 | tf_op jit(solution)/shard_map/ppermute | solution.py:400
  7.8 19.5 %collective-permute-start.3 = (bf16[3,2,128,256]{3,2,1,0:T(8,128)(2,1)S(1)}, bf16[3,2,128,256]{3,2,1,0:T(8,128)(2,1)S(1)}, u32[]{:S(2)}, u32[]{:S(2)}) collective-permute-start(bf16[3,2,128,256]{3,2,1,0:T(8,128)(2,1)S(1)} %get-tuple-element.29), channel_id=1, source_target_pairs={{0,4},{4,0},{8,12},{12,8},{1,5},{5,1},{9,13},{13,9},{2,6},{6,2},{1... | collective-permute-start | bytes 1179656 | tf_op jit(solution)/shard_map/ppermute | solution.py:482
  9.0 30.9 %collective-permute-start.10 = (bf16[3,2,128,256]{3,2,1,0:T(8,128)(2,1)S(1)}, bf16[3,2,128,256]{3,2,1,0:T(8,128)(2,1)S(1)}, u32[]{:S(2)}, u32[]{:S(2)}) collective-permute-start(bf16[3,2,128,256]{3,2,1,0:T(8,128)(2,1)S(1)} %get-tuple-element.23._), channel_id=1, source_target_pairs={{0,8},{4,12},{8,0},{12,4},{1,9},{5,13},{9,1},{13,5},{2,10},{6,14},... | collective-permute-start | bytes 1179656 | tf_op jit(solution)/shard_map/ppermute | solution.py:482
  13.5 3.9 %copy-start = (bf16[2,64,2048]{2,1,0:T(8,128)(2,1)S(1)}, bf16[2,64,2048]{2,1,0:T(8,128)(2,1)}, u32[]{:S(2)}) copy-start(bf16[2,64,2048]{2,1,0:T(8,128)(2,1)} %param.17) | copy-start | bytes 1572868
  13.5 3.7 %collective-permute-start.6 = (f32[32,128]{1,0:T(8,128)S(1)}, f32[32,128]{1,0:T(8,128)S(1)}, u32[]{:S(2)}, u32[]{:S(2)}) collective-permute-start(f32[32,128]{1,0:T(8,128)S(1)} %get-tuple-element.32.refs_0_), channel_id=1, source_target_pairs={{0,3},{1,2},{2,1},{3,0},{4,7},{5,6},{6,5},{7,4},{8,11},{9,10},{10,... | collective-permute-start | bytes 49160 | tf_op jit(solution)/shard_map/ppermute | solution.py:400
  13.6 3.8 %collective-permute-start.5 = (f32[32,128]{1,0:T(8,128)S(1)}, f32[32,128]{1,0:T(8,128)S(1)}, u32[]{:S(2)}, u32[]{:S(2)}) collective-permute-start(f32[32,128]{1,0:T(8,128)S(1)} %get-tuple-element.32.refs_0_), channel_id=1, source_target_pairs={{0,2},{1,3},{2,0},{3,1},{4,6},{5,7},{6,4},{7,5},{8,10},{9,11},{10,... | collective-permute-start | bytes 49160 | tf_op jit(solution)/shard_map/ppermute | solution.py:400
  15.2 2.3 %collective-permute-start.4 = (f32[32,128]{1,0:T(8,128)S(1)}, f32[32,128]{1,0:T(8,128)S(1)}, u32[]{:S(2)}, u32[]{:S(2)}) collective-permute-start(f32[32,128]{1,0:T(8,128)S(1)} %get-tuple-element.32.refs_0_), channel_id=1, source_target_pairs={{0,1},{1,0},{2,3},{3,2},{4,5},{5,4},{6,7},{7,6},{8,9},{9,8},{10,11... | collective-permute-start | bytes 49160 | tf_op jit(solution)/shard_map/ppermute | solution.py:400
  17.2 22.8 %copy-start.2 = (bf16[16,2,2,256]{3,2,1,0:T(2,128)(2,1)S(1)}, bf16[16,2,2,256]{3,2,1,0:T(2,128)(2,1)}, u32[]{:S(2)}) copy-start(bf16[16,2,2,256]{3,2,1,0:T(2,128)(2,1)} %param.13) | copy-start | bytes 98308
  18.3 12.7 %collective-permute-start.7 = (bf16[128,128]{1,0:T(8,128)(2,1)S(1)}, bf16[128,128]{1,0:T(8,128)(2,1)S(1)}, u32[]{:S(2)}, u32[]{:S(2)}) collective-permute-start(bf16[128,128]{1,0:T(8,128)(2,1)S(1)} %get-tuple-element.34), channel_id=1, source_target_pairs={{0,4},{4,0},{8,12},{12,8},{1,5},{5,1},{9,13},{13,9},{2,6},{6,2},{1... | collective-permute-start | bytes 98312 | tf_op jit(solution)/shard_map/ppermute | solution.py:400
  20.6 18.6 %collective-permute-start.8 = (bf16[128,128]{1,0:T(8,128)(2,1)S(1)}, bf16[128,128]{1,0:T(8,128)(2,1)S(1)}, u32[]{:S(2)}, u32[]{:S(2)}) collective-permute-start(bf16[128,128]{1,0:T(8,128)(2,1)S(1)} %get-tuple-element.35), channel_id=1, source_target_pairs={{0,8},{4,12},{8,0},{12,4},{1,9},{5,13},{9,1},{13,5},{2,10},{6,14},... | collective-permute-start | bytes 98312 | tf_op jit(solution)/shard_map/ppermute | solution.py:400
  22.2 17.8 %collective-permute-start.9 = (bf16[128,128]{1,0:T(8,128)(2,1)S(1)}, bf16[128,128]{1,0:T(8,128)(2,1)S(1)}, u32[]{:S(2)}, u32[]{:S(2)}) collective-permute-start(bf16[128,128]{1,0:T(8,128)(2,1)S(1)} %get-tuple-element.36), channel_id=1, source_target_pairs={{0,12},{4,8},{8,4},{12,0},{1,13},{5,9},{9,5},{13,1},{2,14},{6,10},... | collective-permute-start | bytes 98312 | tf_op jit(solution)/shard_map/ppermute | solution.py:400
  27.4 21.0 %collective-permute-start.11 = (bf16[3,2,128,256]{3,2,1,0:T(8,128)(2,1)S(1)}, bf16[3,2,128,256]{3,2,1,0:T(8,128)(2,1)S(1)}, u32[]{:S(2)}, u32[]{:S(2)}) collective-permute-start(bf16[3,2,128,256]{3,2,1,0:T(8,128)(2,1)S(1)} %stage_pages.3._), channel_id=1, source_target_pairs={{0,12},{4,8},{8,4},{12,0},{1,13},{5,9},{9,5},{13,1},{2,14},{6,10},... | collective-permute-start | bytes 1179656 | tf_op jit(solution)/shard_map/ppermute | solution.py:482

commit v6 on v5

--- a/solution.py
+++ b/solution.py
@@ -233,25 +233,27 @@
     )
 
 
-def attend(queries, keys, values, fresh, lengths, slots):
+def visible(depth, context, count, length, slot):
+    column = lax.broadcasted_iota(jnp.int32, (depth, context + 2 * count), 1)
+    step = lax.broadcasted_iota(jnp.int32, (depth, context + 2 * count), 0) % 2
+    fresh_at = column - context - 2 * slot
+    return (column < length) | ((fresh_at >= 0) & (fresh_at <= step))
+
+
+def attend(queries, keys, values, fresh, masks):
     depth = queries[0].shape[0]
-    context, width = keys[0].shape
-    heads = width // HEAD
+    heads = keys[0].shape[1] // HEAD
     per = depth // heads
     scale = HEAD**-0.5
     scores = []
-    for query, key, length, slot in zip(queries, keys, lengths, slots):
+    for query, key, mask in zip(queries, keys, masks):
         product = lax.dot_general(
             by_head(query, heads),
             jnp.concatenate([key, fresh[0]], axis=0),
             (((1,), (1,)), ((), ())),
             preferred_element_type=jnp.float32,
         )
-        column = lax.broadcasted_iota(jnp.int32, product.shape, 1)
-        step = lax.broadcasted_iota(jnp.int32, product.shape, 0) % 2
-        fresh_at = column - context - 2 * slot
-        visible = (column < length) | ((fresh_at >= 0) & (fresh_at <= step))
-        scores.append(jnp.where(visible, product * scale, NEG_FILL))
+        scores.append(jnp.where(mask, product * scale, NEG_FILL))
     scores = jnp.concatenate(scores, axis=0)
     weights = jnp.exp(scores - jnp.max(scores, axis=1, keepdims=True))
     chances = (weights / jnp.sum(weights, axis=1, keepdims=True)).astype(jnp.bfloat16)
@@ -297,25 +299,26 @@
             pltpu.make_async_copy(kv.at[:, r], cache.at[:, r], out_sems.at[r]).wait()
 
 
-def arrivals(dims, routes, told, count, pages):
+def arrivals(dims, routes, told, count):
     groups, _, move_cap, _ = dims
     me = lax.axis_index("req")
-    blocks, slots = [], []
-    for i, route in enumerate(routes):
+    slots = []
+    for route in routes:
         j = partner(route, me, True)
-        for k in range(move_cap):
-            blocks.append(pages[i].at[k])
-            slots.append(told[groups + 3 * count + j * move_cap + k])
-    return blocks, slots, [jnp.maximum(slot, 0) for slot in slots]
-
-
-def early_kernel(dims, routes, plan, told, kv, new_kv, cache_in, *refs):
-    groups, own_cap, _, _ = dims
+        slots += [told[groups + 3 * count + j * move_cap + k] for k in range(move_cap)]
+    return slots, [jnp.maximum(slot, 0) for slot in slots]
+
+
+def early_kernel(dims, routes, later, plan, told, kv, new_kv, cache_in, *refs):
+    groups, own_cap, move_cap, _ = dims
     queries, refs = refs[:groups], refs[groups:]
     pages, refs = refs[: len(routes)], refs[len(routes) :]
-    attended, sorted_queries, cache, x, page_sems = refs
+    attended, cache, late_queries, late_masks, new_keys, new_values = refs[:6]
+    sorted_queries, x, page_sems = refs[6:]
     count, depth, _ = attended.shape
-    blocks, slots, places = arrivals(dims, routes, told, count, pages)
+    _, _, context, width = kv.shape
+    blocks = [ref.at[k] for ref in pages for k in range(move_cap)]
+    slots, places = arrivals(dims, routes, told, count)
     copies = [
         pltpu.make_async_copy(block, cache.at[:, at], page_sems.at[n])
         for n, (block, at) in enumerate(zip(blocks, places))
@@ -330,14 +333,17 @@
             def _(j=j, k=k, slot=slot):
                 sorted_queries[slot] = queries[j][k * depth : (k + 1) * depth, :]
 
+    def mask(at):
+        return visible(depth, context, count, told[groups + 2 * count + at], at)
+
     every = list(range(count))
+    fresh = fresh_rows(new_kv, x, width // HEAD)
     results = attend(
         [sorted_queries[at] for at in every + places],
         [kv[0, r] for r in every] + [block[0] for block in blocks],
         [kv[1, r] for r in every] + [block[1] for block in blocks],
-        fresh_rows(new_kv, x, kv.shape[3] // HEAD),
-        [told[groups + 2 * count + at] for at in every + places],
-        every + places,
+        fresh,
+        [mask(at) for at in every + places],
     )
     for r in every:
         attended[r] = results[r]
@@ -347,16 +353,32 @@
         def _(n=n, at=at):
             attended[at] = results[count + n]
 
+    new_keys[...], new_values[...] = fresh
+    for n, at in enumerate(arrivals(dims, later, told, count)[1]):
+        late_queries[n] = sorted_queries[at]
+        late_masks[n] = jnp.where(mask(at), 1.0, 0.0)
     for slot, copy in zip(slots, copies):
         pl.when(slot >= 0)(copy.wait)
 
 
-def late_kernel(dims, routes, told, new_kv, queries, attended_in, cache_in, *refs):
-    groups = dims[0]
+def late_kernel(
+    dims, routes, told, queries, masks, new_keys, new_values, attended_in, cache_in, *refs
+):
     pages, refs = refs[: len(routes)], refs[len(routes) :]
-    attended, cache, results, x, page_sems, out_sems = refs
-    count = queries.shape[0]
-    blocks, slots, places = arrivals(dims, routes, told, count, pages)
+    attended, cache, slots_held, results, told_sem, page_sems, out_sems = refs
+    number, count = queries.shape[0], attended.shape[0]
+    blocks = [ref.at[k] for ref in pages for k in range(dims[2])]
+    told_copy = pltpu.make_async_copy(told, slots_held, told_sem)
+    told_copy.start()
+    outs = attend(
+        [queries[n] for n in range(number)],
+        [block[0] for block in blocks],
+        [block[1] for block in blocks],
+        (new_keys[...], new_values[...]),
+        [masks[n] > 0.5 for n in range(number)],
+    )
+    told_copy.wait()
+    slots, places = arrivals(dims, routes, slots_held, count)
     copies = [
         (
             pltpu.make_async_copy(block, cache.at[:, at], page_sems.at[n]),
@@ -366,14 +388,6 @@
     ]
     for slot, (copy, _) in zip(slots, copies):
         pl.when(slot >= 0)(copy.start)
-    outs = attend(
-        [queries[at] for at in places],
-        [block[0] for block in blocks],
-        [block[1] for block in blocks],
-        fresh_rows(new_kv, x, cache.shape[3] // HEAD),
-        [told[groups + 2 * count + at] for at in places],
-        places,
-    )
     for n, out in enumerate(outs):
         results[n] = out
     for slot, (_, copy) in zip(slots, copies):
@@ -529,13 +543,22 @@
         name="place_pages",
         cost_estimate=lasts(0.1),
     )(told, table, pool, *[pages[route] for route in first[:-1]])
-    attended, sorted_queries, cache = pl.pallas_call(
-        functools.partial(early_kernel, dims, first),
-        out_shape=[shape((count, depth, LANES), bf16)] * 2 + [shape(cache.shape, bf16)],
+    number_late = len(last) * move_cap
+    attended, cache, *for_last = pl.pallas_call(
+        functools.partial(early_kernel, dims, first, last),
+        out_shape=[
+            shape((count, depth, LANES), bf16),
+            shape(cache.shape, bf16),
+            shape((max(number_late, 1), depth, LANES), bf16),
+            shape((max(number_late, 1), depth, context + 2 * count), f32),
+            shape((2 * count, kv_width), bf16),
+            shape((2 * count, kv_width), bf16),
+        ],
         in_specs=[IN_SMEM] * 2 + [IN_VMEM] * 2 + [IN_PLACE] + [IN_VMEM] * (groups + len(first)),
-        out_specs=[IN_VMEM] * 2 + [IN_PLACE],
-        input_output_aliases={4: 2},
+        out_specs=[IN_VMEM, IN_PLACE] + [IN_VMEM] * 4,
+        input_output_aliases={4: 1},
         scratch_shapes=[
+            pltpu.VMEM((count, depth, LANES), bf16),
             pltpu.VMEM(fresh.shape, f32),
             pltpu.SemaphoreType.DMA((len(first) * move_cap,)),
         ],
@@ -543,23 +566,25 @@
         name="attend_early",
         cost_estimate=lasts(60),
     )(plan, told, kv, fresh, cache, *queries, *[pages[route] for route in first])
-    for routes in (last,):
+
+    if last:
         attended, cache = pl.pallas_call(
-            functools.partial(late_kernel, dims, routes),
+            functools.partial(late_kernel, dims, last),
             out_shape=[shape(attended.shape, bf16), shape(cache.shape, bf16)],
-            in_specs=[IN_SMEM, IN_VMEM, IN_VMEM] + [IN_PLACE] * 2 + [IN_VMEM] * len(routes),
+            in_specs=[IN_PLACE] + [IN_VMEM] * 4 + [IN_PLACE] * 2 + [IN_VMEM] * len(last),
             out_specs=[IN_PLACE, IN_PLACE],
-            input_output_aliases={3: 0, 4: 1},
+            input_output_aliases={5: 0, 6: 1},
             scratch_shapes=[
-                pltpu.VMEM((len(routes) * move_cap, depth, LANES), bf16),
-                pltpu.VMEM(fresh.shape, f32),
-                pltpu.SemaphoreType.DMA((len(routes) * move_cap,)),
-                pltpu.SemaphoreType.DMA((len(routes) * move_cap,)),
+                pltpu.SMEM(told.shape, i32),
+                pltpu.VMEM((number_late, depth, LANES), bf16),
+                pltpu.SemaphoreType.DMA,
+                pltpu.SemaphoreType.DMA((number_late,)),
+                pltpu.SemaphoreType.DMA((number_late,)),
             ],
             compiler_params=PARAMS,
             name="attend_arrived",
             cost_estimate=lasts(1),
-        )(told, fresh, sorted_queries, attended, cache, *[pages[route] for route in routes])
+        )(told, *for_last, attended, cache, *[pages[route] for route in last])
     return from_tiles(attended, steps), cache
 
 

time: 50.8 us -> 50.5 us (level)
  transfers between devices with their start and end apart: 12 -> 12, of which waited for: 5 -> 5; matrix products, arithmetic and copies ran while one was open for 0% -> 0% of each run, Pallas kernels for 23% -> 24%
where the time goes in v6:
time: 50.5 us; the launch traced here: 49.7 us
  waiting for transfers between devices  20.3 us (40%)
  Pallas kernels  14.9 us (30%)
  starting transfers between devices  13.7 us (27%)
  between operations  0.77 us (2%)
    ppermute x3, waiting for transfers between devices, send_pages(): pages[route] = lax.ppermute(x, 'req', pairs)  11.1 us
    ppermute x9, starting transfers between devices, swap(): lax.ppermute(x, axis, [(i, i ^ j) for i in range(lax.axis_size(axis))])  9.38 us
    ppermute x9, waiting for transfers between devices, swap(): lax.ppermute(x, axis, [(i, i ^ j) for i in range(lax.axis_size(axis))])  9.18 us
    ppermute x3, starting transfers between devices, send_pages(): pages[route] = lax.ppermute(x, 'req', pairs)  4.35 us
    pallas_call x2, Pallas kernels, stage_pages(): pl.pallas_call(functools.partial(stage_pages_kernel, dims, routes), out_s...  3.58 us
    pallas_call x1, Pallas kernels, per_device(): pl.pallas_call(functools.partial(place_kernel, dims), out_shape=[shape((2...  2.88 us
    pallas_call x1, Pallas kernels, per_device(): pl.pallas_call(functools.partial(early_kernel, dims, first, last), out_sh...  2.48 us
    pallas_call x1, Pallas kernels, per_device(): pl.pallas_call(functools.partial(rank_kernel, dims, order), out_shape=[sh...  1.99 us
  transfers between devices with their start and end apart: 12, of which 5 were waited for; matrix products, arithmetic and copies ran while one was open for 0% of the time, Pallas kernels for 24%

profile of v6, /device:TPU:8, one launch (start us, length us, event | category | flops | bytes accessed | tf_op | source)
XLA Modules:
  0.0 49.7 jit_solution(12750005839665219597)
XLA Ops:
  0.7 1.8 %stage_rows.1 = (bf16[272,128]{1,0:T(8,128)(2,1)S(1)}, bf16[272,128]{1,0:T(8,128)(2,1)S(1)}, bf16[272,128]{1,0:T(8,128)(2,1)S(1)}, bf16[272,128]{1,0:T(8,128)(2,1)S(1)}, s32[28]{0:T(128)S(1)}) custom-call(s32[16]{0:T(128)} %adapter_of.1, s32[8]{0:T(128)} %adapter_home.1, s32[16]{0:T(128)} %new_group.1, s32[16]{0:T(128)} %cached_len.3, ...), custom_call_target="tpu_custom_call" | custom-call | flops 1000000000 | bytes 3000000 | tf_op jit(solution)/shard_map/stage_rows/pallas_call | solution.py:455
  2.4 2.7 %collective-permute-start = (bf16[272,128]{1,0:T(8,128)(2,1)S(1)}, bf16[272,128]{1,0:T(8,128)(2,1)S(1)}, u32[]{:S(2)}, u32[]{:S(2)}) collective-permute-start(bf16[272,128]{1,0:T(8,128)(2,1)S(1)} %get-tuple-element.27), channel_id=1, source_target_pairs={{0,8},{4,12},{8,0},{12,4},{1,9},{5,13},{9,1},{13,5},{2,10},{6,14},... | collective-permute-start | bytes 208904 | tf_op jit(solution)/shard_map/ppermute | solution.py:414
  5.1 0.4 collective-permute-start.1
  5.5 0.5 collective-permute-start.2
  6.0 1.9 %stage_pages.2 = (bf16[3,2,128,256]{3,2,1,0:T(8,128)(2,1)S(1)}, bf16[3,2,128,256]{3,2,1,0:T(8,128)(2,1)S(1)}) custom-call(s32[28]{0:T(128)S(1)} %get-tuple-element.25.plan, s32[8,16]{1,0:T(8,128)} %bitcast.26, bf16[2,128,16,256]{3,2,1,0:T(8,128)(2,1)} %pool.5), custom_call_target="tpu_custom_call" | custom-call | flops 100000000 | bytes 300000 | tf_op jit(solution)/shard_map/stage_pages/pallas_call | solution.py:482
  7.8 1.2 %collective-permute-start.3 = (bf16[3,2,128,256]{3,2,1,0:T(8,128)(2,1)S(1)}, bf16[3,2,128,256]{3,2,1,0:T(8,128)(2,1)S(1)}, u32[]{:S(2)}, u32[]{:S(2)}) collective-permute-start(bf16[3,2,128,256]{3,2,1,0:T(8,128)(2,1)S(1)} %get-tuple-element.32), channel_id=1, source_target_pairs={{0,4},{4,0},{8,12},{12,8},{1,5},{5,1},{9,13},{13,9},{2,6},{6,2},{1... | collective-permute-start | bytes 1179656 | tf_op jit(solution)/shard_map/ppermute | solution.py:496
  9.0 2.4 %collective-permute-start.10 = (bf16[3,2,128,256]{3,2,1,0:T(8,128)(2,1)S(1)}, bf16[3,2,128,256]{3,2,1,0:T(8,128)(2,1)S(1)}, u32[]{:S(2)}, u32[]{:S(2)}) collective-permute-start(bf16[3,2,128,256]{3,2,1,0:T(8,128)(2,1)S(1)} %get-tuple-element.26._), channel_id=1, source_target_pairs={{0,8},{4,12},{8,0},{12,4},{1,9},{5,13},{9,1},{13,5},{2,10},{6,14},... | collective-permute-start | bytes 1179656 | tf_op jit(solution)/shard_map/ppermute | solution.py:496
  11.5 2.0 %rank_products.1 = (f32[32,128]{1,0:T(8,128)S(1)}, s32[64]{0:T(128)S(1)}) custom-call(s32[16]{0:T(128)S(1)} %copy-done.3, bf16[128,2048]{1,0:T(8,128)(2,1)S(1)} %bitcast.24, bf16[3,2,128,256]{3,2,1,0:T(8,128)(2,1)S(1)} %get-tuple-element.26._, bf16[272,128]{1,0:T(8,128)(2,1)S(1)} %collective-permute-done.refs_0_.refs_6_, ...), custom_call_target="tpu_custom_call" | custom-call | flops 10000000000 | bytes 30000000 | tf_op jit(solution)/shard_map/rank_products/pallas_call | solution.py:502
  13.5 0.1 collective-permute-start.6
  13.6 1.6 %collective-permute-start.5 = (f32[32,128]{1,0:T(8,128)S(1)}, f32[32,128]{1,0:T(8,128)S(1)}, u32[]{:S(2)}, u32[]{:S(2)}) collective-permute-start(f32[32,128]{1,0:T(8,128)S(1)} %get-tuple-element.35.refs_0_), channel_id=1, source_target_pairs={{0,2},{1,3},{2,0},{3,1},{4,6},{5,7},{6,4},{7,5},{8,10},{9,11},{10,... | collective-permute-start | bytes 49160 | tf_op jit(solution)/shard_map/ppermute | solution.py:414
  15.2 0.3 collective-permute-start.4
  15.5 1.7 %stage_pages.3._ = bf16[3,2,128,256]{3,2,1,0:T(8,128)(2,1)S(1)} custom-call(s32[28]{0:T(128)S(1)} %get-tuple-element.25.plan, s32[8,16]{1,0:T(8,128)} %bitcast.27, bf16[2,128,16,256]{3,2,1,0:T(8,128)(2,1)} %pool.5, f32[32,128]{1,0:T(8,128)S(1)} %get-tuple-element.35.refs_0_), custom_call_target="tpu_custom_call" | custom-call | flops 100000000 | bytes 300000 | tf_op jit(solution)/shard_map/stage_pages/pallas_call | solution.py:482
  17.2 0.2 collective-permute-done.5.refs_2_
  17.4 0.8 %queries.1 = (bf16[128,128]{1,0:T(8,128)(2,1)S(1)}, bf16[128,128]{1,0:T(8,128)(2,1)S(1)}, bf16[128,128]{1,0:T(8,128)(2,1)S(1)}, bf16[128,128]{1,0:T(8,128)(2,1)S(1)}) custom-call(s32[64]{0:T(128)S(1)} %get-tuple-element.31.told, bf16[128,2048]{1,0:T(8,128)(2,1)S(1)} %bitcast.23, bf16[3,2,128,256]{3,2,1,0:T(8,128)(2,1)S(1)} %stage_pages.3._, ...), custom_call_target="tpu_custom_call" | custom-call | flops 100000000 | bytes 300000 | tf_op jit(solution)/shard_map/queries/pallas_call | solution.py:523
  18.3 2.3 %collective-permute-start.7 = (bf16[128,128]{1,0:T(8,128)(2,1)S(1)}, bf16[128,128]{1,0:T(8,128)(2,1)S(1)}, u32[]{:S(2)}, u32[]{:S(2)}) collective-permute-start(bf16[128,128]{1,0:T(8,128)(2,1)S(1)} %get-tuple-element.37), channel_id=1, source_target_pairs={{0,4},{4,0},{8,12},{12,8},{1,5},{5,1},{9,13},{13,9},{2,6},{6,2},{1... | collective-permute-start | bytes 98312 | tf_op jit(solution)/shard_map/ppermute | solution.py:414
  20.6 1.6 %collective-permute-start.8 = (bf16[128,128]{1,0:T(8,128)(2,1)S(1)}, bf16[128,128]{1,0:T(8,128)(2,1)S(1)}, u32[]{:S(2)}, u32[]{:S(2)}) collective-permute-start(bf16[128,128]{1,0:T(8,128)(2,1)S(1)} %get-tuple-element.38), channel_id=1, source_target_pairs={{0,8},{4,12},{8,0},{12,4},{1,9},{5,13},{9,1},{13,5},{2,10},{6,14},... | collective-permute-start | bytes 98312 | tf_op jit(solution)/shard_map/ppermute | solution.py:414
  22.2 5.2 %collective-permute-done.3.refs_0_.refs_4_ = bf16[3,2,128,256]{3,2,1,0:T(8,128)(2,1)S(1)} collective-permute-done((bf16[3,2,128,256]{3,2,1,0:T(8,128)(2,1)S(1)}, bf16[3,2,128,256]{3,2,1,0:T(8,128)(2,1)S(1)}, u32[]{:S(2)}, u32[]{:S(2)}) %collective-permute-start.3) | collective-permute-done | bytes 393248 | tf_op jit(solution)/shard_map/ppermute | solution.py:496
  27.4 0.7 %collective-permute-start.11 = (bf16[3,2,128,256]{3,2,1,0:T(8,128)(2,1)S(1)}, bf16[3,2,128,256]{3,2,1,0:T(8,128)(2,1)S(1)}, u32[]{:S(2)}, u32[]{:S(2)}) collective-permute-start(bf16[3,2,128,256]{3,2,1,0:T(8,128)(2,1)S(1)} %stage_pages.3._), channel_id=1, source_target_pairs={{0,12},{4,8},{8,4},{12,0},{1,13},{5,9},{9,5},{13,1},{2,14},{6,10},... | collective-permute-start | bytes 1179656 | tf_op jit(solution)/shard_map/ppermute | solution.py:496
  28.1 2.9 %place_pages.1 = (bf16[2,16,128,256]{3,2,1,0:T(8,128)(2,1)}, bf16[2,16,128,256]{3,2,1,0:T(8,128)(2,1)S(1)}) custom-call(s32[64]{0:T(128)S(1)} %get-tuple-element.31.told, s32[8,16]{1,0:T(8,128)} %bitcast.28, bf16[2,128,16,256]{3,2,1,0:T(8,128)(2,1)} %pool.5, bf16[3,2,128,256]{3,2,1,0:T(8,128)(2,1)S(1)} %collective-permute-done.3.refs_0_.refs_4_), custom_call_target="tpu_custom_call" | custom-call | flops 100000000 | bytes 300000 | tf_op jit(solution)/shard_map/place_pages/pallas_call | solution.py:536
  31.0 8.2 %collective-permute-done.8.refs_2_ = bf16[128,128]{1,0:T(8,128)(2,1)S(1)} collective-permute-done((bf16[128,128]{1,0:T(8,128)(2,1)S(1)}, bf16[128,128]{1,0:T(8,128)(2,1)S(1)}, u32[]{:S(2)}, u32[]{:S(2)}) %collective-permute-start.8) | collective-permute-done | bytes 32800 | tf_op jit(solution)/shard_map/ppermute | solution.py:414
  39.2 0.7 %collective-permute-done.9.refs_3_ = bf16[128,128]{1,0:T(8,128)(2,1)S(1)} collective-permute-done((bf16[128,128]{1,0:T(8,128)(2,1)S(1)}, bf16[128,128]{1,0:T(8,128)(2,1)S(1)}, u32[]{:S(2)}, u32[]{:S(2)}) %collective-permute-start.9) | collective-permute-done | bytes 32800 | tf_op jit(solution)/shard_map/ppermute | solution.py:414
  39.9 2.5 %attend_early.1 = (bf16[16,32,128]{2,1,0:T(8,128)(2,1)}, bf16[2,16,128,256]{3,2,1,0:T(8,128)(2,1)}, bf16[3,32,128]{2,1,0:T(8,128)(2,1)S(1)}, f32[3,32,160]{2,1,0...) custom-call(s32[28]{0:T(128)S(1)} %get-tuple-element.25.plan, ...), custom_call_target="tpu_custom_call", output_to_operand_aliasing={{1}: (4, {})} | custom-call | flops 60000002048 | bytes 180000000 | tf_op jit(solution)/shard_map/attend_early/pallas_call | solution.py:547
  42.4 5.9 %collective-permute-done.11.refs_0_ = bf16[3,2,128,256]{3,2,1,0:T(8,128)(2,1)S(1)} collective-permute-done((bf16[3,2,128,256]{3,2,1,0:T(8,128)(2,1)S(1)}, bf16[3,2,128,256]{3,2,1,0:T(8,128)(2,1)S(1)}, u32[]{:S(2)}, u32[]{:S(2)}) %collective-permute-start.11) | collective-permute-done | bytes 393248 | tf_op jit(solution)/shard_map/ppermute | solution.py:496
  48.4 1.4 %attend_arrived.1 = (bf16[16,32,128]{2,1,0:T(8,128)(2,1)}, bf16[2,16,128,256]{3,2,1,0:T(8,128)(2,1)}) custom-call(s32[64]{0:T(128)S(1)} %get-tuple-element.31.told, bf16[3,32,128]{2,1,0:T(8,128)(2,1)S(1)} %get-tuple-element.40.queries, f32[3,32,160]{2,1,0:T(8,128)S(1)} %get-tuple-element.41.masks, ...), custom_call_target="tpu_custom_call", output_to_operand_aliasing={{0}: (5, {}), {1}: (6, {})} | custom-call | flops 1000000000 | bytes 3000000 | tf_op jit(solution)/shard_map/attend_arrived/pallas_call | solution.py:571
  (16 shorter events, 0.0 us)
Async XLA Ops:
  0.6 10.9 %copy-start.1 = (bf16[2,64,2048]{2,1,0:T(8,128)(2,1)S(1)}, bf16[2,64,2048]{2,1,0:T(8,128)(2,1)}, u32[]{:S(2)}) copy-start(bf16[2,64,2048]{2,1,0:T(8,128)(2,1)} %param.16) | copy-start | bytes 1572868
  0.6 10.9 %copy-start.3 = (s32[16]{0:T(128)S(1)}, s32[16]{0:T(128)}, u32[]{:S(2)}) copy-start(s32[16]{0:T(128)} %cached_len.3) | copy-start | bytes 196
  2.4 9.1 %collective-permute-start = (bf16[272,128]{1,0:T(8,128)(2,1)S(1)}, bf16[272,128]{1,0:T(8,128)(2,1)S(1)}, u32[]{:S(2)}, u32[]{:S(2)}) collective-permute-start(bf16[272,128]{1,0:T(8,128)(2,1)S(1)} %get-tuple-element.27), channel_id=1, source_target_pairs={{0,8},{4,12},{8,0},{12,4},{1,9},{5,13},{9,1},{13,5},{2,10},{6,14},... | collective-permute-start | bytes 208904 | tf_op jit(solution)/shard_map/ppermute | solution.py:414
  5.1 6.4 %collective-permute-start.1 = (bf16[272,128]{1,0:T(8,128)(2,1)S(1)}, bf16[272,128]{1,0:T(8,128)(2,1)S(1)}, u32[]{:S(2)}, u32[]{:S(2)}) collective-permute-start(bf16[272,128]{1,0:T(8,128)(2,1)S(1)} %get-tuple-element.28), channel_id=1, source_target_pairs={{0,4},{4,0},{8,12},{12,8},{1,5},{5,1},{9,13},{13,9},{2,6},{6,2},{1... | collective-permute-start | bytes 208904 | tf_op jit(solution)/shard_map/ppermute | solution.py:414
  5.5 6.0 %collective-permute-start.2 = (bf16[272,128]{1,0:T(8,128)(2,1)S(1)}, bf16[272,128]{1,0:T(8,128)(2,1)S(1)}, u32[]{:S(2)}, u32[]{:S(2)}) collective-permute-start(bf16[272,128]{1,0:T(8,128)(2,1)S(1)} %get-tuple-element.29), channel_id=1, source_target_pairs={{0,12},{4,8},{8,4},{12,0},{1,13},{5,9},{9,5},{13,1},{2,14},{6,10},... | collective-permute-start | bytes 208904 | tf_op jit(solution)/shard_map/ppermute | solution.py:414
  7.8 19.5 %collective-permute-start.3 = (bf16[3,2,128,256]{3,2,1,0:T(8,128)(2,1)S(1)}, bf16[3,2,128,256]{3,2,1,0:T(8,128)(2,1)S(1)}, u32[]{:S(2)}, u32[]{:S(2)}) collective-permute-start(bf16[3,2,128,256]{3,2,1,0:T(8,128)(2,1)S(1)} %get-tuple-element.32), channel_id=1, source_target_pairs={{0,4},{4,0},{8,12},{12,8},{1,5},{5,1},{9,13},{13,9},{2,6},{6,2},{1... | collective-permute-start | bytes 1179656 | tf_op jit(solution)/shard_map/ppermute | solution.py:496
  9.0 30.9 %collective-permute-start.10 = (bf16[3,2,128,256]{3,2,1,0:T(8,128)(2,1)S(1)}, bf16[3,2,128,256]{3,2,1,0:T(8,128)(2,1)S(1)}, u32[]{:S(2)}, u32[]{:S(2)}) collective-permute-start(bf16[3,2,128,256]{3,2,1,0:T(8,128)(2,1)S(1)} %get-tuple-element.26._), channel_id=1, source_target_pairs={{0,8},{4,12},{8,0},{12,4},{1,9},{5,13},{9,1},{13,5},{2,10},{6,14},... | collective-permute-start | bytes 1179656 | tf_op jit(solution)/shard_map/ppermute | solution.py:496
  13.5 3.9 %copy-start = (bf16[2,64,2048]{2,1,0:T(8,128)(2,1)S(1)}, bf16[2,64,2048]{2,1,0:T(8,128)(2,1)}, u32[]{:S(2)}) copy-start(bf16[2,64,2048]{2,1,0:T(8,128)(2,1)} %param.17) | copy-start | bytes 1572868
  13.5 3.7 %collective-permute-start.6 = (f32[32,128]{1,0:T(8,128)S(1)}, f32[32,128]{1,0:T(8,128)S(1)}, u32[]{:S(2)}, u32[]{:S(2)}) collective-permute-start(f32[32,128]{1,0:T(8,128)S(1)} %get-tuple-element.35.refs_0_), channel_id=1, source_target_pairs={{0,3},{1,2},{2,1},{3,0},{4,7},{5,6},{6,5},{7,4},{8,11},{9,10},{10,... | collective-permute-start | bytes 49160 | tf_op jit(solution)/shard_map/ppermute | solution.py:414
  13.6 3.8 %collective-permute-start.5 = (f32[32,128]{1,0:T(8,128)S(1)}, f32[32,128]{1,0:T(8,128)S(1)}, u32[]{:S(2)}, u32[]{:S(2)}) collective-permute-start(f32[32,128]{1,0:T(8,128)S(1)} %get-tuple-element.35.refs_0_), channel_id=1, source_target_pairs={{0,2},{1,3},{2,0},{3,1},{4,6},{5,7},{6,4},{7,5},{8,10},{9,11},{10,... | collective-permute-start | bytes 49160 | tf_op jit(solution)/shard_map/ppermute | solution.py:414
  15.2 2.3 %collective-permute-start.4 = (f32[32,128]{1,0:T(8,128)S(1)}, f32[32,128]{1,0:T(8,128)S(1)}, u32[]{:S(2)}, u32[]{:S(2)}) collective-permute-start(f32[32,128]{1,0:T(8,128)S(1)} %get-tuple-element.35.refs_0_), channel_id=1, source_target_pairs={{0,1},{1,0},{2,3},{3,2},{4,5},{5,4},{6,7},{7,6},{8,9},{9,8},{10,11... | collective-permute-start | bytes 49160 | tf_op jit(solution)/shard_map/ppermute | solution.py:414
  17.2 22.8 %copy-start.2 = (bf16[16,2,2,256]{3,2,1,0:T(2,128)(2,1)S(1)}, bf16[16,2,2,256]{3,2,1,0:T(2,128)(2,1)}, u32[]{:S(2)}) copy-start(bf16[16,2,2,256]{3,2,1,0:T(2,128)(2,1)} %param.13) | copy-start | bytes 98308
  18.3 12.7 %collective-permute-start.7 = (bf16[128,128]{1,0:T(8,128)(2,1)S(1)}, bf16[128,128]{1,0:T(8,128)(2,1)S(1)}, u32[]{:S(2)}, u32[]{:S(2)}) collective-permute-start(bf16[128,128]{1,0:T(8,128)(2,1)S(1)} %get-tuple-element.37), channel_id=1, source_target_pairs={{0,4},{4,0},{8,12},{12,8},{1,5},{5,1},{9,13},{13,9},{2,6},{6,2},{1... | collective-permute-start | bytes 98312 | tf_op jit(solution)/shard_map/ppermute | solution.py:414
  20.6 18.6 %collective-permute-start.8 = (bf16[128,128]{1,0:T(8,128)(2,1)S(1)}, bf16[128,128]{1,0:T(8,128)(2,1)S(1)}, u32[]{:S(2)}, u32[]{:S(2)}) collective-permute-start(bf16[128,128]{1,0:T(8,128)(2,1)S(1)} %get-tuple-element.38), channel_id=1, source_target_pairs={{0,8},{4,12},{8,0},{12,4},{1,9},{5,13},{9,1},{13,5},{2,10},{6,14},... | collective-permute-start | bytes 98312 | tf_op jit(solution)/shard_map/ppermute | solution.py:414
  22.2 17.8 %collective-permute-start.9 = (bf16[128,128]{1,0:T(8,128)(2,1)S(1)}, bf16[128,128]{1,0:T(8,128)(2,1)S(1)}, u32[]{:S(2)}, u32[]{:S(2)}) collective-permute-start(bf16[128,128]{1,0:T(8,128)(2,1)S(1)} %get-tuple-element.39), channel_id=1, source_target_pairs={{0,12},{4,8},{8,4},{12,0},{1,13},{5,9},{9,5},{13,1},{2,14},{6,10},... | collective-permute-start | bytes 98312 | tf_op jit(solution)/shard_map/ppermute | solution.py:414
  27.4 21.0 %collective-permute-start.11 = (bf16[3,2,128,256]{3,2,1,0:T(8,128)(2,1)S(1)}, bf16[3,2,128,256]{3,2,1,0:T(8,128)(2,1)S(1)}, u32[]{:S(2)}, u32[]{:S(2)}) collective-permute-start(bf16[3,2,128,256]{3,2,1,0:T(8,128)(2,1)S(1)} %stage_pages.3._), channel_id=1, source_target_pairs={{0,12},{4,8},{8,4},{12,0},{1,13},{5,9},{9,5},{13,1},{2,14},{6,10},... | collective-permute-start | bytes 1179656 | tf_op jit(solution)/shard_map/ppermute | solution.py:496

commit v7 on v6

--- a/solution.py
+++ b/solution.py
@@ -111,7 +111,7 @@
 
 def stage_pages_kernel(dims, routes, plan, table, pool, *refs):
     groups, own_cap, move_cap, _ = dims
-    *outs, sems = refs[-len(routes) - 1 :]
+    outs = refs[-len(routes) :]
     page = pool.shape[2]
     me = lax.axis_index("req")
     for i, route in enumerate(routes):
@@ -119,13 +119,9 @@
         for k in range(move_cap):
             source = jnp.maximum(plan[groups * own_cap + j * move_cap + k], 0)
             for p in range(table.shape[0]):
-                pltpu.make_async_copy(
-                    pool.at[:, table[p, source]],
-                    outs[i].at[k, :, pl.ds(p * page, page)],
-                    sems.at[i],
-                ).start()
-    for i in range(len(routes)):
-        pltpu.make_async_copy(outs[i], outs[i], sems.at[i]).wait()
+                number = table[p, source]
+                for half in range(2):
+                    outs[i][k, half, p * page : (p + 1) * page, :] = pool[half, number]
 
 
 def rank_kernel(dims, order, cached_len, a_ref, _, *refs):
@@ -482,13 +478,12 @@
         return pl.pallas_call(
             functools.partial(stage_pages_kernel, dims, routes),
             out_shape=[shape((move_cap, 2, context, kv_width), bf16)] * len(routes),
-            in_specs=[IN_SMEM] * 2 + [IN_PLACE] * (1 + len(after)),
-            out_specs=[IN_PLACE] * len(routes),
-            scratch_shapes=[pltpu.SemaphoreType.DMA((len(routes),))],
+            in_specs=[IN_SMEM] * 2 + [IN_VMEM] + [IN_PLACE] * len(after),
+            out_specs=[IN_VMEM] * len(routes),
             compiler_params=PARAMS,
             name="stage_pages",
             cost_estimate=lasts(0.1),
-        )(plan, table, pool, *after)
+        )(plan, page_table.T, kv_pool, *after)
 
     def send_pages(routes, staged):
         for route, x in zip(routes, staged):

time: 50.5 us -> 50 us (0.990)
  Pallas kernels: 14.9 us -> 12.7 us
  starting transfers between devices: 13.7 us -> 14.9 us
    ppermute x9, waiting for transfers between devices: 9.18 us -> 11.7 us  [swap(): lax.ppermute(x, axis, [(i, i ^ j) for i in range(lax.axis_size(axis))])]
    pallas_call x2, Pallas kernels: 3.58 us -> 1.32 us  [stage_pages(): pl.pallas_call(functools.partial(stage_pages_kernel, dims, routes), out_s...]
    ppermute x3, waiting for transfers between devices: 11.1 us -> 9.13 us  [send_pages(): pages[route] = lax.ppermute(x, 'req', pairs)]
    ppermute x9, starting transfers between devices: 9.38 us -> 9.97 us  [swap(): lax.ppermute(x, axis, [(i, i ^ j) for i in range(lax.axis_size(axis))])]
    ppermute x3, starting transfers between devices: 4.35 us -> 4.92 us  [send_pages(): pages[route] = lax.ppermute(x, 'req', pairs)]
  transfers between devices with their start and end apart: 12 -> 12, of which waited for: 5 -> 7; matrix products, arithmetic and copies ran while one was open for 0% -> 0% of each run, Pallas kernels for 24% -> 19%
where the time goes in v7:
time: 50 us; the launch traced here: 49.3 us
  waiting for transfers between devices  20.8 us (42%)
  starting transfers between devices  14.9 us (30%)
  Pallas kernels  12.7 us (25%)
  between operations  0.77 us (2%)
    ppermute x9, waiting for transfers between devices, swap(): lax.ppermute(x, axis, [(i, i ^ j) for i in range(lax.axis_size(axis))])  11.7 us
    ppermute x9, starting transfers between devices, swap(): lax.ppermute(x, axis, [(i, i ^ j) for i in range(lax.axis_size(axis))])  9.97 us
    ppermute x3, waiting for transfers between devices, send_pages(): pages[route] = lax.ppermute(x, 'req', pairs)  9.13 us
    ppermute x3, starting transfers between devices, send_pages(): pages[route] = lax.ppermute(x, 'req', pairs)  4.92 us
    pallas_call x1, Pallas kernels, per_device(): pl.pallas_call(functools.partial(place_kernel, dims), out_shape=[shape((2...  2.9 us
    pallas_call x1, Pallas kernels, per_device(): pl.pallas_call(functools.partial(early_kernel, dims, first, last), out_sh...  2.49 us
    pallas_call x1, Pallas kernels, per_device(): pl.pallas_call(functools.partial(rank_kernel, dims, order), out_shape=[sh...  2.01 us
    pallas_call x1, Pallas kernels, per_device(): pl.pallas_call(functools.partial(stage_rows_kernel, dims), out_shape=[mes...  1.78 us
  transfers between devices with their start and end apart: 12, of which 7 were waited for; matrix products, arithmetic and copies ran while one was open for 0% of the time, Pallas kernels for 19%

profile of v7, /device:TPU:8, one launch (start us, length us, event | category | flops | bytes accessed | tf_op | source)
XLA Modules:
  0.0 49.3 jit_solution(13410500847560239972)
XLA Ops:
  0.7 1.8 %stage_rows.1 = (bf16[272,128]{1,0:T(8,128)(2,1)S(1)}, bf16[272,128]{1,0:T(8,128)(2,1)S(1)}, bf16[272,128]{1,0:T(8,128)(2,1)S(1)}, bf16[272,128]{1,0:T(8,128)(2,1)S(1)}, s32[28]{0:T(128)S(1)}) custom-call(s32[16]{0:T(128)} %adapter_of.1, s32[8]{0:T(128)} %adapter_home.1, s32[16]{0:T(128)} %new_group.1, s32[16]{0:T(128)} %cached_len.3, ...), custom_call_target="tpu_custom_call" | custom-call | flops 1000000000 | bytes 3000000 | tf_op jit(solution)/shard_map/stage_rows/pallas_call | solution.py:451
  2.5 2.7 %collective-permute-start = (bf16[272,128]{1,0:T(8,128)(2,1)S(1)}, bf16[272,128]{1,0:T(8,128)(2,1)S(1)}, u32[]{:S(2)}, u32[]{:S(2)}) collective-permute-start(bf16[272,128]{1,0:T(8,128)(2,1)S(1)} %get-tuple-element.27), channel_id=1, source_target_pairs={{0,8},{4,12},{8,0},{12,4},{1,9},{5,13},{9,1},{13,5},{2,10},{6,14},... | collective-permute-start | bytes 208904 | tf_op jit(solution)/shard_map/ppermute | solution.py:410
  5.1 0.4 collective-permute-start.1
  5.6 0.5 collective-permute-start.2
  6.0 0.7 %stage_pages.2 = (bf16[3,2,128,256]{3,2,1,0:T(8,128)(2,1)S(1)}, bf16[3,2,128,256]{3,2,1,0:T(8,128)(2,1)S(1)}) custom-call(s32[28]{0:T(128)S(1)} %get-tuple-element.25.plan, s32[8,16]{1,0:T(8,128)S(1)} %bitcast.25, bf16[2,128,16,256]{3,2,1,0:T(8,128)(2,1)S(1)} %copy-done), custom_call_target="tpu_custom_call" | custom-call | flops 100000000 | bytes 300000 | tf_op jit(solution)/shard_map/stage_pages/pallas_call | solution.py:478
  6.7 1.2 %collective-permute-start.3 = (bf16[3,2,128,256]{3,2,1,0:T(8,128)(2,1)S(1)}, bf16[3,2,128,256]{3,2,1,0:T(8,128)(2,1)S(1)}, u32[]{:S(2)}, u32[]{:S(2)}) collective-permute-start(bf16[3,2,128,256]{3,2,1,0:T(8,128)(2,1)S(1)} %get-tuple-element.32), channel_id=1, source_target_pairs={{0,4},{4,0},{8,12},{12,8},{1,5},{5,1},{9,13},{13,9},{2,6},{6,2},{1... | collective-permute-start | bytes 1179656 | tf_op jit(solution)/shard_map/ppermute | solution.py:491
  7.9 2.4 %collective-permute-start.10 = (bf16[3,2,128,256]{3,2,1,0:T(8,128)(2,1)S(1)}, bf16[3,2,128,256]{3,2,1,0:T(8,128)(2,1)S(1)}, u32[]{:S(2)}, u32[]{:S(2)}) collective-permute-start(bf16[3,2,128,256]{3,2,1,0:T(8,128)(2,1)S(1)} %get-tuple-element.26._), channel_id=1, source_target_pairs={{0,8},{4,12},{8,0},{12,4},{1,9},{5,13},{9,1},{13,5},{2,10},{6,14},... | collective-permute-start | bytes 1179656 | tf_op jit(solution)/shard_map/ppermute | solution.py:491
  10.3 0.8 %collective-permute-done.2.refs_2_.refs_7_ = bf16[272,128]{1,0:T(8,128)(2,1)S(1)} collective-permute-done((bf16[272,128]{1,0:T(8,128)(2,1)S(1)}, bf16[272,128]{1,0:T(8,128)(2,1)S(1)}, u32[]{:S(2)}, u32[]{:S(2)}) %collective-permute-start.2) | collective-permute-done | bytes 69664 | tf_op jit(solution)/shard_map/ppermute | solution.py:410
  11.2 2.0 %rank_products.1 = (f32[32,128]{1,0:T(8,128)S(1)}, s32[64]{0:T(128)S(1)}) custom-call(s32[16]{0:T(128)S(1)} %copy-done.5, bf16[128,2048]{1,0:T(8,128)(2,1)S(1)} %bitcast.27, bf16[3,2,128,256]{3,2,1,0:T(8,128)(2,1)S(1)} %get-tuple-element.26._, bf16[272,128]{1,0:T(8,128)(2,1)S(1)} %collective-permute-done.refs_0_.refs_6_, ...), custom_call_target="tpu_custom_call" | custom-call | flops 10000000000 | bytes 30000000 | tf_op jit(solution)/shard_map/rank_products/pallas_call | solution.py:497
  13.3 1.6 %collective-permute-start.5 = (f32[32,128]{1,0:T(8,128)S(1)}, f32[32,128]{1,0:T(8,128)S(1)}, u32[]{:S(2)}, u32[]{:S(2)}) collective-permute-start(f32[32,128]{1,0:T(8,128)S(1)} %get-tuple-element.35.refs_0_), channel_id=1, source_target_pairs={{0,2},{1,3},{2,0},{3,1},{4,6},{5,7},{6,4},{7,5},{8,10},{9,11},{10,... | collective-permute-start | bytes 49160 | tf_op jit(solution)/shard_map/ppermute | solution.py:410
  15.1 0.6 %stage_pages.3._ = bf16[3,2,128,256]{3,2,1,0:T(8,128)(2,1)S(1)} custom-call(s32[28]{0:T(128)S(1)} %get-tuple-element.25.plan, s32[8,16]{1,0:T(8,128)S(1)} %bitcast.26, bf16[2,128,16,256]{3,2,1,0:T(8,128)(2,1)S(1)} %copy-done, f32[32,128]{1,0:T(8,128)S(1)} %get-tuple-element.35.refs_0_), custom_call_target="tpu_custom_call" | custom-call | flops 100000000 | bytes 300000 | tf_op jit(solution)/shard_map/stage_pages/pallas_call | solution.py:478
  15.8 0.8 %collective-permute-done.6.refs_3_ = f32[32,128]{1,0:T(8,128)S(1)} collective-permute-done((f32[32,128]{1,0:T(8,128)S(1)}, f32[32,128]{1,0:T(8,128)S(1)}, u32[]{:S(2)}, u32[]{:S(2)}) %collective-permute-start.6) | collective-permute-done | bytes 16416 | tf_op jit(solution)/shard_map/ppermute | solution.py:410
  16.6 0.5 %collective-permute-done.5.refs_2_ = f32[32,128]{1,0:T(8,128)S(1)} collective-permute-done((f32[32,128]{1,0:T(8,128)S(1)}, f32[32,128]{1,0:T(8,128)S(1)}, u32[]{:S(2)}, u32[]{:S(2)}) %collective-permute-start.5) | collective-permute-done | bytes 16416 | tf_op jit(solution)/shard_map/ppermute | solution.py:410
  17.1 0.8 %queries.1 = (bf16[128,128]{1,0:T(8,128)(2,1)S(1)}, bf16[128,128]{1,0:T(8,128)(2,1)S(1)}, bf16[128,128]{1,0:T(8,128)(2,1)S(1)}, bf16[128,128]{1,0:T(8,128)(2,1)S(1)}) custom-call(s32[64]{0:T(128)S(1)} %get-tuple-element.31.told, bf16[128,2048]{1,0:T(8,128)(2,1)S(1)} %bitcast.23, bf16[3,2,128,256]{3,2,1,0:T(8,128)(2,1)S(1)} %stage_pages.3._, ...), custom_call_target="tpu_custom_call" | custom-call | flops 100000000 | bytes 300000 | tf_op jit(solution)/shard_map/queries/pallas_call | solution.py:518
  18.0 2.9 %collective-permute-start.7 = (bf16[128,128]{1,0:T(8,128)(2,1)S(1)}, bf16[128,128]{1,0:T(8,128)(2,1)S(1)}, u32[]{:S(2)}, u32[]{:S(2)}) collective-permute-start(bf16[128,128]{1,0:T(8,128)(2,1)S(1)} %get-tuple-element.37), channel_id=1, source_target_pairs={{0,4},{4,0},{8,12},{12,8},{1,5},{5,1},{9,13},{13,9},{2,6},{6,2},{1... | collective-permute-start | bytes 98312 | tf_op jit(solution)/shard_map/ppermute | solution.py:410
  20.9 1.4 %collective-permute-start.8 = (bf16[128,128]{1,0:T(8,128)(2,1)S(1)}, bf16[128,128]{1,0:T(8,128)(2,1)S(1)}, u32[]{:S(2)}, u32[]{:S(2)}) collective-permute-start(bf16[128,128]{1,0:T(8,128)(2,1)S(1)} %get-tuple-element.38), channel_id=1, source_target_pairs={{0,8},{4,12},{8,0},{12,4},{1,9},{5,13},{9,1},{13,5},{2,10},{6,14},... | collective-permute-start | bytes 98312 | tf_op jit(solution)/shard_map/ppermute | solution.py:410
  22.5 3.5 %collective-permute-done.3.refs_0_.refs_4_ = bf16[3,2,128,256]{3,2,1,0:T(8,128)(2,1)S(1)} collective-permute-done((bf16[3,2,128,256]{3,2,1,0:T(8,128)(2,1)S(1)}, bf16[3,2,128,256]{3,2,1,0:T(8,128)(2,1)S(1)}, u32[]{:S(2)}, u32[]{:S(2)}) %collective-permute-start.3) | collective-permute-done | bytes 393248 | tf_op jit(solution)/shard_map/ppermute | solution.py:491
  26.0 1.3 %collective-permute-start.11 = (bf16[3,2,128,256]{3,2,1,0:T(8,128)(2,1)S(1)}, bf16[3,2,128,256]{3,2,1,0:T(8,128)(2,1)S(1)}, u32[]{:S(2)}, u32[]{:S(2)}) collective-permute-start(bf16[3,2,128,256]{3,2,1,0:T(8,128)(2,1)S(1)} %stage_pages.3._), channel_id=1, source_target_pairs={{0,12},{4,8},{8,4},{12,0},{1,13},{5,9},{9,5},{13,1},{2,14},{6,10},... | collective-permute-start | bytes 1179656 | tf_op jit(solution)/shard_map/ppermute | solution.py:491
  27.3 2.9 %place_pages.1 = (bf16[2,16,128,256]{3,2,1,0:T(8,128)(2,1)}, bf16[2,16,128,256]{3,2,1,0:T(8,128)(2,1)S(1)}) custom-call(s32[64]{0:T(128)S(1)} %get-tuple-element.31.told, s32[8,16]{1,0:T(8,128)} %bitcast.24, bf16[2,128,16,256]{3,2,1,0:T(8,128)(2,1)} %pool.5, bf16[3,2,128,256]{3,2,1,0:T(8,128)(2,1)S(1)} %collective-permute-done.3.refs_0_.refs_4_), custom_call_target="tpu_custom_call" | custom-call | flops 100000000 | bytes 300000 | tf_op jit(solution)/shard_map/place_pages/pallas_call | solution.py:531
  30.2 8.7 %collective-permute-done.8.refs_2_ = bf16[128,128]{1,0:T(8,128)(2,1)S(1)} collective-permute-done((bf16[128,128]{1,0:T(8,128)(2,1)S(1)}, bf16[128,128]{1,0:T(8,128)(2,1)S(1)}, u32[]{:S(2)}, u32[]{:S(2)}) %collective-permute-start.8) | collective-permute-done | bytes 32800 | tf_op jit(solution)/shard_map/ppermute | solution.py:410
  38.9 0.9 %collective-permute-done.9.refs_3_ = bf16[128,128]{1,0:T(8,128)(2,1)S(1)} collective-permute-done((bf16[128,128]{1,0:T(8,128)(2,1)S(1)}, bf16[128,128]{1,0:T(8,128)(2,1)S(1)}, u32[]{:S(2)}, u32[]{:S(2)}) %collective-permute-start.9) | collective-permute-done | bytes 32800 | tf_op jit(solution)/shard_map/ppermute | solution.py:410
  39.8 2.5 %attend_early.1 = (bf16[16,32,128]{2,1,0:T(8,128)(2,1)}, bf16[2,16,128,256]{3,2,1,0:T(8,128)(2,1)}, bf16[3,32,128]{2,1,0:T(8,128)(2,1)S(1)}, f32[3,32,160]{2,1,0...) custom-call(s32[28]{0:T(128)S(1)} %get-tuple-element.25.plan, ...), custom_call_target="tpu_custom_call", output_to_operand_aliasing={{1}: (4, {})} | custom-call | flops 60000002048 | bytes 180000000 | tf_op jit(solution)/shard_map/attend_early/pallas_call | solution.py:542
  42.3 5.6 %collective-permute-done.11.refs_0_ = bf16[3,2,128,256]{3,2,1,0:T(8,128)(2,1)S(1)} collective-permute-done((bf16[3,2,128,256]{3,2,1,0:T(8,128)(2,1)S(1)}, bf16[3,2,128,256]{3,2,1,0:T(8,128)(2,1)S(1)}, u32[]{:S(2)}, u32[]{:S(2)}) %collective-permute-start.11) | collective-permute-done | bytes 393248 | tf_op jit(solution)/shard_map/ppermute | solution.py:491
  47.9 1.4 %attend_arrived.1 = (bf16[16,32,128]{2,1,0:T(8,128)(2,1)}, bf16[2,16,128,256]{3,2,1,0:T(8,128)(2,1)}) custom-call(s32[64]{0:T(128)S(1)} %get-tuple-element.31.told, bf16[3,32,128]{2,1,0:T(8,128)(2,1)S(1)} %get-tuple-element.40.queries, f32[3,32,160]{2,1,0:T(8,128)S(1)} %get-tuple-element.41.masks, ...), custom_call_target="tpu_custom_call", output_to_operand_aliasing={{0}: (5, {}), {1}: (6, {})} | custom-call | flops 1000000000 | bytes 3000000 | tf_op jit(solution)/shard_map/attend_arrived/pallas_call | solution.py:566
  (20 shorter events, 0.6 us)
Async XLA Ops:
  0.6 5.4 %copy-start = (bf16[2,128,16,256]{3,2,1,0:T(8,128)(2,1)S(1)}, bf16[2,128,16,256]{3,2,1,0:T(8,128)(2,1)}, u32[]{:S(2)}) copy-start(bf16[2,128,16,256]{3,2,1,0:T(8,128)(2,1)} %pool.5) | copy-start | bytes 6291460
  0.6 5.4 %copy-start.2 = (s32[16,8]{0,1:T(8,128)S(1)}, s32[16,8]{0,1:T(8,128)}, u32[]{:S(2)}) copy-start(s32[16,8]{0,1:T(8,128)} %param.19) | copy-start | bytes 1540
  0.7 10.5 %copy-start.3 = (bf16[2,64,2048]{2,1,0:T(8,128)(2,1)S(1)}, bf16[2,64,2048]{2,1,0:T(8,128)(2,1)}, u32[]{:S(2)}) copy-start(bf16[2,64,2048]{2,1,0:T(8,128)(2,1)} %param.16) | copy-start | bytes 1572868
  0.7 10.5 %copy-start.5 = (s32[16]{0:T(128)S(1)}, s32[16]{0:T(128)}, u32[]{:S(2)}) copy-start(s32[16]{0:T(128)} %cached_len.3) | copy-start | bytes 196
  2.5 7.9 %collective-permute-start = (bf16[272,128]{1,0:T(8,128)(2,1)S(1)}, bf16[272,128]{1,0:T(8,128)(2,1)S(1)}, u32[]{:S(2)}, u32[]{:S(2)}) collective-permute-start(bf16[272,128]{1,0:T(8,128)(2,1)S(1)} %get-tuple-element.27), channel_id=1, source_target_pairs={{0,8},{4,12},{8,0},{12,4},{1,9},{5,13},{9,1},{13,5},{2,10},{6,14},... | collective-permute-start | bytes 208904 | tf_op jit(solution)/shard_map/ppermute | solution.py:410
  5.1 5.2 %collective-permute-start.1 = (bf16[272,128]{1,0:T(8,128)(2,1)S(1)}, bf16[272,128]{1,0:T(8,128)(2,1)S(1)}, u32[]{:S(2)}, u32[]{:S(2)}) collective-permute-start(bf16[272,128]{1,0:T(8,128)(2,1)S(1)} %get-tuple-element.28), channel_id=1, source_target_pairs={{0,4},{4,0},{8,12},{12,8},{1,5},{5,1},{9,13},{13,9},{2,6},{6,2},{1... | collective-permute-start | bytes 208904 | tf_op jit(solution)/shard_map/ppermute | solution.py:410
  5.6 5.6 %collective-permute-start.2 = (bf16[272,128]{1,0:T(8,128)(2,1)S(1)}, bf16[272,128]{1,0:T(8,128)(2,1)S(1)}, u32[]{:S(2)}, u32[]{:S(2)}) collective-permute-start(bf16[272,128]{1,0:T(8,128)(2,1)S(1)} %get-tuple-element.29), channel_id=1, source_target_pairs={{0,12},{4,8},{8,4},{12,0},{1,13},{5,9},{9,5},{13,1},{2,14},{6,10},... | collective-permute-start | bytes 208904 | tf_op jit(solution)/shard_map/ppermute | solution.py:410
  6.7 19.3 %collective-permute-start.3 = (bf16[3,2,128,256]{3,2,1,0:T(8,128)(2,1)S(1)}, bf16[3,2,128,256]{3,2,1,0:T(8,128)(2,1)S(1)}, u32[]{:S(2)}, u32[]{:S(2)}) collective-permute-start(bf16[3,2,128,256]{3,2,1,0:T(8,128)(2,1)S(1)} %get-tuple-element.32), channel_id=1, source_target_pairs={{0,4},{4,0},{8,12},{12,8},{1,5},{5,1},{9,13},{13,9},{2,6},{6,2},{1... | collective-permute-start | bytes 1179656 | tf_op jit(solution)/shard_map/ppermute | solution.py:491
  7.9 31.9 %collective-permute-start.10 = (bf16[3,2,128,256]{3,2,1,0:T(8,128)(2,1)S(1)}, bf16[3,2,128,256]{3,2,1,0:T(8,128)(2,1)S(1)}, u32[]{:S(2)}, u32[]{:S(2)}) collective-permute-start(bf16[3,2,128,256]{3,2,1,0:T(8,128)(2,1)S(1)} %get-tuple-element.26._), channel_id=1, source_target_pairs={{0,8},{4,12},{8,0},{12,4},{1,9},{5,13},{9,1},{13,5},{2,10},{6,14},... | collective-permute-start | bytes 1179656 | tf_op jit(solution)/shard_map/ppermute | solution.py:491
  13.2 3.9 %copy-start.1 = (bf16[2,64,2048]{2,1,0:T(8,128)(2,1)S(1)}, bf16[2,64,2048]{2,1,0:T(8,128)(2,1)}, u32[]{:S(2)}) copy-start(bf16[2,64,2048]{2,1,0:T(8,128)(2,1)} %param.17) | copy-start | bytes 1572868
  13.2 3.4 %collective-permute-start.6 = (f32[32,128]{1,0:T(8,128)S(1)}, f32[32,128]{1,0:T(8,128)S(1)}, u32[]{:S(2)}, u32[]{:S(2)}) collective-permute-start(f32[32,128]{1,0:T(8,128)S(1)} %get-tuple-element.35.refs_0_), channel_id=1, source_target_pairs={{0,3},{1,2},{2,1},{3,0},{4,7},{5,6},{6,5},{7,4},{8,11},{9,10},{10,... | collective-permute-start | bytes 49160 | tf_op jit(solution)/shard_map/ppermute | solution.py:410
  13.3 3.8 %collective-permute-start.5 = (f32[32,128]{1,0:T(8,128)S(1)}, f32[32,128]{1,0:T(8,128)S(1)}, u32[]{:S(2)}, u32[]{:S(2)}) collective-permute-start(f32[32,128]{1,0:T(8,128)S(1)} %get-tuple-element.35.refs_0_), channel_id=1, source_target_pairs={{0,2},{1,3},{2,0},{3,1},{4,6},{5,7},{6,4},{7,5},{8,10},{9,11},{10,... | collective-permute-start | bytes 49160 | tf_op jit(solution)/shard_map/ppermute | solution.py:410
  14.8 2.3 %collective-permute-start.4 = (f32[32,128]{1,0:T(8,128)S(1)}, f32[32,128]{1,0:T(8,128)S(1)}, u32[]{:S(2)}, u32[]{:S(2)}) collective-permute-start(f32[32,128]{1,0:T(8,128)S(1)} %get-tuple-element.35.refs_0_), channel_id=1, source_target_pairs={{0,1},{1,0},{2,3},{3,2},{4,5},{5,4},{6,7},{7,6},{8,9},{9,8},{10,11... | collective-permute-start | bytes 49160 | tf_op jit(solution)/shard_map/ppermute | solution.py:410
  15.8 24.0 %copy-start.4 = (bf16[16,2,2,256]{3,2,1,0:T(2,128)(2,1)S(1)}, bf16[16,2,2,256]{3,2,1,0:T(2,128)(2,1)}, u32[]{:S(2)}) copy-start(bf16[16,2,2,256]{3,2,1,0:T(2,128)(2,1)} %param.13) | copy-start | bytes 98308
  18.0 12.2 %collective-permute-start.7 = (bf16[128,128]{1,0:T(8,128)(2,1)S(1)}, bf16[128,128]{1,0:T(8,128)(2,1)S(1)}, u32[]{:S(2)}, u32[]{:S(2)}) collective-permute-start(bf16[128,128]{1,0:T(8,128)(2,1)S(1)} %get-tuple-element.37), channel_id=1, source_target_pairs={{0,4},{4,0},{8,12},{12,8},{1,5},{5,1},{9,13},{13,9},{2,6},{6,2},{1... | collective-permute-start | bytes 98312 | tf_op jit(solution)/shard_map/ppermute | solution.py:410
  20.9 18.0 %collective-permute-start.8 = (bf16[128,128]{1,0:T(8,128)(2,1)S(1)}, bf16[128,128]{1,0:T(8,128)(2,1)S(1)}, u32[]{:S(2)}, u32[]{:S(2)}) collective-permute-start(bf16[128,128]{1,0:T(8,128)(2,1)S(1)} %get-tuple-element.38), channel_id=1, source_target_pairs={{0,8},{4,12},{8,0},{12,4},{1,9},{5,13},{9,1},{13,5},{2,10},{6,14},... | collective-permute-start | bytes 98312 | tf_op jit(solution)/shard_map/ppermute | solution.py:410
  22.2 17.6 %collective-permute-start.9 = (bf16[128,128]{1,0:T(8,128)(2,1)S(1)}, bf16[128,128]{1,0:T(8,128)(2,1)S(1)}, u32[]{:S(2)}, u32[]{:S(2)}) collective-permute-start(bf16[128,128]{1,0:T(8,128)(2,1)S(1)} %get-tuple-element.39), channel_id=1, source_target_pairs={{0,12},{4,8},{8,4},{12,0},{1,13},{5,9},{9,5},{13,1},{2,14},{6,10},... | collective-permute-start | bytes 98312 | tf_op jit(solution)/shard_map/ppermute | solution.py:410
  26.0 21.9 %collective-permute-start.11 = (bf16[3,2,128,256]{3,2,1,0:T(8,128)(2,1)S(1)}, bf16[3,2,128,256]{3,2,1,0:T(8,128)(2,1)S(1)}, u32[]{:S(2)}, u32[]{:S(2)}) collective-permute-start(bf16[3,2,128,256]{3,2,1,0:T(8,128)(2,1)S(1)} %stage_pages.3._), channel_id=1, source_target_pairs={{0,12},{4,8},{8,4},{12,0},{1,13},{5,9},{9,5},{13,1},{2,14},{6,10},... | collective-permute-start | bytes 1179656 | tf_op jit(solution)/shard_map/ppermute | solution.py:491

commit v8 on v7

--- a/solution.py
+++ b/solution.py
@@ -469,7 +469,8 @@
         cost_estimate=lasts(1),
     )(*in_hbm(adapter_of, adapter_home, new_group, cached_len, hidden, frozen))
     got = {0: messages[0]}
-    order = [half] + [j for j in range(1, groups) if j != half] + [0]
+    between = [j for j in range(1, groups - 1) if j != half]
+    order = list(dict.fromkeys([groups - 1, *between, half, 0]))
     for j in order[:-1]:
         got[j] = swap(messages[j], "req", j)
     got = [got[j] for j in range(groups)]
@@ -531,13 +532,13 @@
     cache, kv = pl.pallas_call(
         functools.partial(place_kernel, dims),
         out_shape=[shape((2, count, context, kv_width), bf16)] * 2,
-        in_specs=[IN_SMEM] * 2 + [IN_PLACE] * (1 + len(first[:-1])),
+        in_specs=[IN_SMEM] * 2 + [IN_PLACE] * 2,
         out_specs=[IN_PLACE] * 2,
         scratch_shapes=[pltpu.SemaphoreType.DMA((count,))] * 2,
         compiler_params=PARAMS,
         name="place_pages",
         cost_estimate=lasts(0.1),
-    )(told, table, pool, *[pages[route] for route in first[:-1]])
+    )(told, table, pool, queries[1])
     number_late = len(last) * move_cap
     attended, cache, *for_last = pl.pallas_call(
         functools.partial(early_kernel, dims, first, last),

time: 50 us -> 49.7 us (level); the launches traced: 49.3 us -> 49.5 us
  waiting for transfers between devices: 20.8 us -> 23.2 us
  starting transfers between devices: 14.9 us -> 12.7 us
    ppermute x3, waiting for transfers between devices: 9.13 us -> 12.9 us  [send_pages(): pages[route] = lax.ppermute(x, 'req', pairs)]
    ppermute x3, starting transfers between devices: 4.92 us -> 3.1 us  [send_pages(): pages[route] = lax.ppermute(x, 'req', pairs)]
    ppermute x9, waiting for transfers between devices: 11.7 us -> 10.3 us  [swap(): lax.ppermute(x, axis, [(i, i ^ j) for i in range(lax.axis_size(axis))])]
  transfers between devices with their start and end apart: 12 -> 12, of which waited for: 7 -> 6; matrix products, arithmetic and copies ran while one was open for 0% -> 0% of each run, Pallas kernels for 19% -> 19%
where the time goes in v8:
time: 49.7 us; the launch traced here: 49.5 us
  waiting for transfers between devices  23.2 us (47%)
  Pallas kernels  12.7 us (26%)
  starting transfers between devices  12.7 us (26%)
  between operations  0.8 us (2%)
    ppermute x3, waiting for transfers between devices, send_pages(): pages[route] = lax.ppermute(x, 'req', pairs)  12.9 us
    ppermute x9, waiting for transfers between devices, swap(): lax.ppermute(x, axis, [(i, i ^ j) for i in range(lax.axis_size(axis))])  10.3 us
    ppermute x9, starting transfers between devices, swap(): lax.ppermute(x, axis, [(i, i ^ j) for i in range(lax.axis_size(axis))])  9.62 us
    ppermute x3, starting transfers between devices, send_pages(): pages[route] = lax.ppermute(x, 'req', pairs)  3.1 us
    pallas_call x1, Pallas kernels, per_device(): pl.pallas_call(functools.partial(place_kernel, dims), out_shape=[shape((2...  2.85 us
    pallas_call x1, Pallas kernels, per_device(): pl.pallas_call(functools.partial(early_kernel, dims, first, last), out_sh...  2.52 us
    pallas_call x1, Pallas kernels, per_device(): pl.pallas_call(functools.partial(rank_kernel, dims, order), out_shape=[sh...  2.01 us
    pallas_call x1, Pallas kernels, per_device(): pl.pallas_call(functools.partial(stage_rows_kernel, dims), out_shape=[mes...  1.78 us
  transfers between devices with their start and end apart: 12, of which 6 were waited for; matrix products, arithmetic and copies ran while one was open for 0% of the time, Pallas kernels for 19%

profile of v8, /device:TPU:8, one launch (start us, length us, event | category | flops | bytes accessed | tf_op | source)
XLA Modules:
  0.0 49.5 jit_solution(3288167973439902060)
XLA Ops:
  0.7 1.8 %stage_rows.1 = (bf16[272,128]{1,0:T(8,128)(2,1)S(1)}, bf16[272,128]{1,0:T(8,128)(2,1)S(1)}, bf16[272,128]{1,0:T(8,128)(2,1)S(1)}, bf16[272,128]{1,0:T(8,128)(2,1)S(1)}, s32[28]{0:T(128)S(1)}) custom-call(s32[16]{0:T(128)} %adapter_of.1, s32[8]{0:T(128)} %adapter_home.1, s32[16]{0:T(128)} %new_group.1, s32[16]{0:T(128)} %cached_len.3, ...), custom_call_target="tpu_custom_call" | custom-call | flops 1000000000 | bytes 3000000 | tf_op jit(solution)/shard_map/stage_rows/pallas_call | solution.py:451
  2.5 1.6 %collective-permute-start = (bf16[272,128]{1,0:T(8,128)(2,1)S(1)}, bf16[272,128]{1,0:T(8,128)(2,1)S(1)}, u32[]{:S(2)}, u32[]{:S(2)}) collective-permute-start(bf16[272,128]{1,0:T(8,128)(2,1)S(1)} %get-tuple-element.27), channel_id=1, source_target_pairs={{0,12},{4,8},{8,4},{12,0},{1,13},{5,9},{9,5},{13,1},{2,14},{6,10},... | collective-permute-start | bytes 208904 | tf_op jit(solution)/shard_map/ppermute | solution.py:410
  4.1 2.5 %collective-permute-start.1 = (bf16[272,128]{1,0:T(8,128)(2,1)S(1)}, bf16[272,128]{1,0:T(8,128)(2,1)S(1)}, u32[]{:S(2)}, u32[]{:S(2)}) collective-permute-start(bf16[272,128]{1,0:T(8,128)(2,1)S(1)} %get-tuple-element.28), channel_id=1, source_target_pairs={{0,4},{4,0},{8,12},{12,8},{1,5},{5,1},{9,13},{13,9},{2,6},{6,2},{1... | collective-permute-start | bytes 208904 | tf_op jit(solution)/shard_map/ppermute | solution.py:410
  6.6 0.7 %stage_pages.2 = (bf16[3,2,128,256]{3,2,1,0:T(8,128)(2,1)S(1)}, bf16[3,2,128,256]{3,2,1,0:T(8,128)(2,1)S(1)}) custom-call(s32[28]{0:T(128)S(1)} %get-tuple-element.25.plan, s32[8,16]{1,0:T(8,128)S(1)} %bitcast.25, bf16[2,128,16,256]{3,2,1,0:T(8,128)(2,1)S(1)} %copy-done), custom_call_target="tpu_custom_call" | custom-call | flops 100000000 | bytes 300000 | tf_op jit(solution)/shard_map/stage_pages/pallas_call | solution.py:479
  7.3 0.7 %collective-permute-start.9 = (bf16[3,2,128,256]{3,2,1,0:T(8,128)(2,1)S(1)}, bf16[3,2,128,256]{3,2,1,0:T(8,128)(2,1)S(1)}, u32[]{:S(2)}, u32[]{:S(2)}) collective-permute-start(bf16[3,2,128,256]{3,2,1,0:T(8,128)(2,1)S(1)} %get-tuple-element.39), channel_id=1, source_target_pairs={{0,4},{4,0},{8,12},{12,8},{1,5},{5,1},{9,13},{13,9},{2,6},{6,2},{1... | collective-permute-start | bytes 1179656 | tf_op jit(solution)/shard_map/ppermute | solution.py:492
  8.0 2.4 %collective-permute-start.10 = (bf16[3,2,128,256]{3,2,1,0:T(8,128)(2,1)S(1)}, bf16[3,2,128,256]{3,2,1,0:T(8,128)(2,1)S(1)}, u32[]{:S(2)}, u32[]{:S(2)}) collective-permute-start(bf16[3,2,128,256]{3,2,1,0:T(8,128)(2,1)S(1)} %get-tuple-element.26._), channel_id=1, source_target_pairs={{0,8},{4,12},{8,0},{12,4},{1,9},{5,13},{9,1},{13,5},{2,10},{6,14},... | collective-permute-start | bytes 1179656 | tf_op jit(solution)/shard_map/ppermute | solution.py:492
  10.4 0.7 %collective-permute-done.1.refs_1_.refs_5_ = bf16[272,128]{1,0:T(8,128)(2,1)S(1)} collective-permute-done((bf16[272,128]{1,0:T(8,128)(2,1)S(1)}, bf16[272,128]{1,0:T(8,128)(2,1)S(1)}, u32[]{:S(2)}, u32[]{:S(2)}) %collective-permute-start.1) | collective-permute-done | bytes 69664 | tf_op jit(solution)/shard_map/ppermute | solution.py:410
  11.1 1.4 %collective-permute-done.2.refs_2_.refs_6_ = bf16[272,128]{1,0:T(8,128)(2,1)S(1)} collective-permute-done((bf16[272,128]{1,0:T(8,128)(2,1)S(1)}, bf16[272,128]{1,0:T(8,128)(2,1)S(1)}, u32[]{:S(2)}, u32[]{:S(2)}) %collective-permute-start.2) | collective-permute-done | bytes 69664 | tf_op jit(solution)/shard_map/ppermute | solution.py:410
  12.6 2.0 %rank_products.1 = (f32[32,128]{1,0:T(8,128)S(1)}, s32[64]{0:T(128)S(1)}) custom-call(s32[16]{0:T(128)S(1)} %copy-done.5, bf16[128,2048]{1,0:T(8,128)(2,1)S(1)} %bitcast.27, bf16[3,2,128,256]{3,2,1,0:T(8,128)(2,1)S(1)} %get-tuple-element.26._, bf16[272,128]{1,0:T(8,128)(2,1)S(1)} %collective-permute-done.refs_0_.refs_7_, ...), custom_call_target="tpu_custom_call" | custom-call | flops 10000000000 | bytes 30000000 | tf_op jit(solution)/shard_map/rank_products/pallas_call | solution.py:498
  14.6 0.1 collective-permute-start.5
  14.7 1.6 %collective-permute-start.4 = (f32[32,128]{1,0:T(8,128)S(1)}, f32[32,128]{1,0:T(8,128)S(1)}, u32[]{:S(2)}, u32[]{:S(2)}) collective-permute-start(f32[32,128]{1,0:T(8,128)S(1)} %get-tuple-element.32.refs_0_), channel_id=1, source_target_pairs={{0,2},{1,3},{2,0},{3,1},{4,6},{5,7},{6,4},{7,5},{8,10},{9,11},{10,... | collective-permute-start | bytes 49160 | tf_op jit(solution)/shard_map/ppermute | solution.py:410
  16.2 0.3 collective-permute-start.3
  16.5 0.6 %stage_pages.3._ = bf16[3,2,128,256]{3,2,1,0:T(8,128)(2,1)S(1)} custom-call(s32[28]{0:T(128)S(1)} %get-tuple-element.25.plan, s32[8,16]{1,0:T(8,128)S(1)} %bitcast.26, bf16[2,128,16,256]{3,2,1,0:T(8,128)(2,1)S(1)} %copy-done, f32[32,128]{1,0:T(8,128)S(1)} %get-tuple-element.32.refs_0_), custom_call_target="tpu_custom_call" | custom-call | flops 100000000 | bytes 300000 | tf_op jit(solution)/shard_map/stage_pages/pallas_call | solution.py:479
  17.2 0.8 %collective-permute-done.5.refs_3_ = f32[32,128]{1,0:T(8,128)S(1)} collective-permute-done((f32[32,128]{1,0:T(8,128)S(1)}, f32[32,128]{1,0:T(8,128)S(1)}, u32[]{:S(2)}, u32[]{:S(2)}) %collective-permute-start.5) | collective-permute-done | bytes 16416 | tf_op jit(solution)/shard_map/ppermute | solution.py:410
  18.0 0.5 %collective-permute-done.4.refs_2_ = f32[32,128]{1,0:T(8,128)S(1)} collective-permute-done((f32[32,128]{1,0:T(8,128)S(1)}, f32[32,128]{1,0:T(8,128)S(1)}, u32[]{:S(2)}, u32[]{:S(2)}) %collective-permute-start.4) | collective-permute-done | bytes 16416 | tf_op jit(solution)/shard_map/ppermute | solution.py:410
  18.5 0.8 %queries.1 = (bf16[128,128]{1,0:T(8,128)(2,1)S(1)}, bf16[128,128]{1,0:T(8,128)(2,1)S(1)}, bf16[128,128]{1,0:T(8,128)(2,1)S(1)}, bf16[128,128]{1,0:T(8,128)(2,1)S(1)}) custom-call(s32[64]{0:T(128)S(1)} %get-tuple-element.31.told, bf16[128,2048]{1,0:T(8,128)(2,1)S(1)} %bitcast.23, bf16[3,2,128,256]{3,2,1,0:T(8,128)(2,1)S(1)} %stage_pages.3._, ...), custom_call_target="tpu_custom_call" | custom-call | flops 100000000 | bytes 300000 | tf_op jit(solution)/shard_map/queries/pallas_call | solution.py:519
  19.3 0.9 %collective-permute-start.6 = (bf16[128,128]{1,0:T(8,128)(2,1)S(1)}, bf16[128,128]{1,0:T(8,128)(2,1)S(1)}, u32[]{:S(2)}, u32[]{:S(2)}) collective-permute-start(bf16[128,128]{1,0:T(8,128)(2,1)S(1)} %get-tuple-element.33), channel_id=1, source_target_pairs={{0,4},{4,0},{8,12},{12,8},{1,5},{5,1},{9,13},{13,9},{2,6},{6,2},{1... | collective-permute-start | bytes 98312 | tf_op jit(solution)/shard_map/ppermute | solution.py:410
  20.2 2.2 %collective-permute-start.7 = (bf16[128,128]{1,0:T(8,128)(2,1)S(1)}, bf16[128,128]{1,0:T(8,128)(2,1)S(1)}, u32[]{:S(2)}, u32[]{:S(2)}) collective-permute-start(bf16[128,128]{1,0:T(8,128)(2,1)S(1)} %get-tuple-element.37), channel_id=1, source_target_pairs={{0,8},{4,12},{8,0},{12,4},{1,9},{5,13},{9,1},{13,5},{2,10},{6,14},... | collective-permute-start | bytes 98312 | tf_op jit(solution)/shard_map/ppermute | solution.py:410
  22.4 0.5 %collective-permute-start.8 = (bf16[128,128]{1,0:T(8,128)(2,1)S(1)}, bf16[128,128]{1,0:T(8,128)(2,1)S(1)}, u32[]{:S(2)}, u32[]{:S(2)}) collective-permute-start(bf16[128,128]{1,0:T(8,128)(2,1)S(1)} %get-tuple-element.38), channel_id=1, source_target_pairs={{0,12},{4,8},{8,4},{12,0},{1,13},{5,9},{9,5},{13,1},{2,14},{6,10},... | collective-permute-start | bytes 98312 | tf_op jit(solution)/shard_map/ppermute | solution.py:410
  22.9 6.8 %collective-permute-done.6.refs_0_.refs_1_ = bf16[128,128]{1,0:T(8,128)(2,1)S(1)} collective-permute-done((bf16[128,128]{1,0:T(8,128)(2,1)S(1)}, bf16[128,128]{1,0:T(8,128)(2,1)S(1)}, u32[]{:S(2)}, u32[]{:S(2)}) %collective-permute-start.6) | collective-permute-done | bytes 32800 | tf_op jit(solution)/shard_map/ppermute | solution.py:410
  29.8 2.9 %place_pages.1 = (bf16[2,16,128,256]{3,2,1,0:T(8,128)(2,1)}, bf16[2,16,128,256]{3,2,1,0:T(8,128)(2,1)S(1)}) custom-call(s32[64]{0:T(128)S(1)} %get-tuple-element.31.told, s32[8,16]{1,0:T(8,128)} %bitcast.24, bf16[2,128,16,256]{3,2,1,0:T(8,128)(2,1)} %pool.5, bf16[128,128]{1,0:T(8,128)(2,1)S(1)} %collective-permute-done.6.refs_0_.refs_1_), custom_call_target="tpu_custom_call" | custom-call | flops 100000000 | bytes 300000 | tf_op jit(solution)/shard_map/place_pages/pallas_call | solution.py:532
  32.7 2.5 %attend_early.1 = (bf16[16,32,128]{2,1,0:T(8,128)(2,1)}, bf16[2,16,128,256]{3,2,1,0:T(8,128)(2,1)}, bf16[3,32,128]{2,1,0:T(8,128)(2,1)S(1)}, f32[3,32,160]{2,1,0...) custom-call(s32[28]{0:T(128)S(1)} %get-tuple-element.25.plan, ...), custom_call_target="tpu_custom_call", output_to_operand_aliasing={{1}: (4, {})} | custom-call | flops 60000002048 | bytes 180000000 | tf_op jit(solution)/shard_map/attend_early/pallas_call | solution.py:543
  35.2 12.9 %collective-permute-done.11.refs_0_ = bf16[3,2,128,256]{3,2,1,0:T(8,128)(2,1)S(1)} collective-permute-done((bf16[3,2,128,256]{3,2,1,0:T(8,128)(2,1)S(1)}, bf16[3,2,128,256]{3,2,1,0:T(8,128)(2,1)S(1)}, u32[]{:S(2)}, u32[]{:S(2)}) %collective-permute-start.11) | collective-permute-done | bytes 393248 | tf_op jit(solution)/shard_map/ppermute | solution.py:492
  48.1 1.4 %attend_arrived.1 = (bf16[16,32,128]{2,1,0:T(8,128)(2,1)}, bf16[2,16,128,256]{3,2,1,0:T(8,128)(2,1)}) custom-call(s32[64]{0:T(128)S(1)} %get-tuple-element.31.told, bf16[3,32,128]{2,1,0:T(8,128)(2,1)S(1)} %get-tuple-element.40.queries, f32[3,32,160]{2,1,0:T(8,128)S(1)} %get-tuple-element.41.masks, ...), custom_call_target="tpu_custom_call", output_to_operand_aliasing={{0}: (5, {}), {1}: (6, {})} | custom-call | flops 1000000000 | bytes 3000000 | tf_op jit(solution)/shard_map/attend_arrived/pallas_call | solution.py:567
  (20 shorter events, 0.1 us)
Async XLA Ops:
  0.6 6.0 %copy-start = (bf16[2,128,16,256]{3,2,1,0:T(8,128)(2,1)S(1)}, bf16[2,128,16,256]{3,2,1,0:T(8,128)(2,1)}, u32[]{:S(2)}) copy-start(bf16[2,128,16,256]{3,2,1,0:T(8,128)(2,1)} %pool.5) | copy-start | bytes 6291460
  0.6 5.9 %copy-start.2 = (s32[16,8]{0,1:T(8,128)S(1)}, s32[16,8]{0,1:T(8,128)}, u32[]{:S(2)}) copy-start(s32[16,8]{0,1:T(8,128)} %param.19) | copy-start | bytes 1540
  0.7 11.9 %copy-start.3 = (bf16[2,64,2048]{2,1,0:T(8,128)(2,1)S(1)}, bf16[2,64,2048]{2,1,0:T(8,128)(2,1)}, u32[]{:S(2)}) copy-start(bf16[2,64,2048]{2,1,0:T(8,128)(2,1)} %param.16) | copy-start | bytes 1572868
  0.7 11.9 %copy-start.5 = (s32[16]{0:T(128)S(1)}, s32[16]{0:T(128)}, u32[]{:S(2)}) copy-start(s32[16]{0:T(128)} %cached_len.3) | copy-start | bytes 196
  2.5 7.9 %collective-permute-start = (bf16[272,128]{1,0:T(8,128)(2,1)S(1)}, bf16[272,128]{1,0:T(8,128)(2,1)S(1)}, u32[]{:S(2)}, u32[]{:S(2)}) collective-permute-start(bf16[272,128]{1,0:T(8,128)(2,1)S(1)} %get-tuple-element.27), channel_id=1, source_target_pairs={{0,12},{4,8},{8,4},{12,0},{1,13},{5,9},{9,5},{13,1},{2,14},{6,10},... | collective-permute-start | bytes 208904 | tf_op jit(solution)/shard_map/ppermute | solution.py:410
  4.1 7.0 %collective-permute-start.1 = (bf16[272,128]{1,0:T(8,128)(2,1)S(1)}, bf16[272,128]{1,0:T(8,128)(2,1)S(1)}, u32[]{:S(2)}, u32[]{:S(2)}) collective-permute-start(bf16[272,128]{1,0:T(8,128)(2,1)S(1)} %get-tuple-element.28), channel_id=1, source_target_pairs={{0,4},{4,0},{8,12},{12,8},{1,5},{5,1},{9,13},{13,9},{2,6},{6,2},{1... | collective-permute-start | bytes 208904 | tf_op jit(solution)/shard_map/ppermute | solution.py:410
  6.6 6.0 %collective-permute-start.2 = (bf16[272,128]{1,0:T(8,128)(2,1)S(1)}, bf16[272,128]{1,0:T(8,128)(2,1)S(1)}, u32[]{:S(2)}, u32[]{:S(2)}) collective-permute-start(bf16[272,128]{1,0:T(8,128)(2,1)S(1)} %get-tuple-element.29), channel_id=1, source_target_pairs={{0,8},{4,12},{8,0},{12,4},{1,9},{5,13},{9,1},{13,5},{2,10},{6,14},... | collective-permute-start | bytes 208904 | tf_op jit(solution)/shard_map/ppermute | solution.py:410
  7.3 25.4 %collective-permute-start.9 = (bf16[3,2,128,256]{3,2,1,0:T(8,128)(2,1)S(1)}, bf16[3,2,128,256]{3,2,1,0:T(8,128)(2,1)S(1)}, u32[]{:S(2)}, u32[]{:S(2)}) collective-permute-start(bf16[3,2,128,256]{3,2,1,0:T(8,128)(2,1)S(1)} %get-tuple-element.39), channel_id=1, source_target_pairs={{0,4},{4,0},{8,12},{12,8},{1,5},{5,1},{9,13},{13,9},{2,6},{6,2},{1... | collective-permute-start | bytes 1179656 | tf_op jit(solution)/shard_map/ppermute | solution.py:492
  8.0 24.7 %collective-permute-start.10 = (bf16[3,2,128,256]{3,2,1,0:T(8,128)(2,1)S(1)}, bf16[3,2,128,256]{3,2,1,0:T(8,128)(2,1)S(1)}, u32[]{:S(2)}, u32[]{:S(2)}) collective-permute-start(bf16[3,2,128,256]{3,2,1,0:T(8,128)(2,1)S(1)} %get-tuple-element.26._), channel_id=1, source_target_pairs={{0,8},{4,12},{8,0},{12,4},{1,9},{5,13},{9,1},{13,5},{2,10},{6,14},... | collective-permute-start | bytes 1179656 | tf_op jit(solution)/shard_map/ppermute | solution.py:492
  14.6 3.9 %copy-start.1 = (bf16[2,64,2048]{2,1,0:T(8,128)(2,1)S(1)}, bf16[2,64,2048]{2,1,0:T(8,128)(2,1)}, u32[]{:S(2)}) copy-start(bf16[2,64,2048]{2,1,0:T(8,128)(2,1)} %param.17) | copy-start | bytes 1572868
  14.6 3.4 %collective-permute-start.5 = (f32[32,128]{1,0:T(8,128)S(1)}, f32[32,128]{1,0:T(8,128)S(1)}, u32[]{:S(2)}, u32[]{:S(2)}) collective-permute-start(f32[32,128]{1,0:T(8,128)S(1)} %get-tuple-element.32.refs_0_), channel_id=1, source_target_pairs={{0,3},{1,2},{2,1},{3,0},{4,7},{5,6},{6,5},{7,4},{8,11},{9,10},{10,... | collective-permute-start | bytes 49160 | tf_op jit(solution)/shard_map/ppermute | solution.py:410
  14.7 3.8 %collective-permute-start.4 = (f32[32,128]{1,0:T(8,128)S(1)}, f32[32,128]{1,0:T(8,128)S(1)}, u32[]{:S(2)}, u32[]{:S(2)}) collective-permute-start(f32[32,128]{1,0:T(8,128)S(1)} %get-tuple-element.32.refs_0_), channel_id=1, source_target_pairs={{0,2},{1,3},{2,0},{3,1},{4,6},{5,7},{6,4},{7,5},{8,10},{9,11},{10,... | collective-permute-start | bytes 49160 | tf_op jit(solution)/shard_map/ppermute | solution.py:410
  16.2 2.3 %collective-permute-start.3 = (f32[32,128]{1,0:T(8,128)S(1)}, f32[32,128]{1,0:T(8,128)S(1)}, u32[]{:S(2)}, u32[]{:S(2)}) collective-permute-start(f32[32,128]{1,0:T(8,128)S(1)} %get-tuple-element.32.refs_0_), channel_id=1, source_target_pairs={{0,1},{1,0},{2,3},{3,2},{4,5},{5,4},{6,7},{7,6},{8,9},{9,8},{10,11... | collective-permute-start | bytes 49160 | tf_op jit(solution)/shard_map/ppermute | solution.py:410
  17.2 15.5 %copy-start.4 = (bf16[16,2,2,256]{3,2,1,0:T(2,128)(2,1)S(1)}, bf16[16,2,2,256]{3,2,1,0:T(2,128)(2,1)}, u32[]{:S(2)}) copy-start(bf16[16,2,2,256]{3,2,1,0:T(2,128)(2,1)} %param.13) | copy-start | bytes 98308
  19.3 10.4 %collective-permute-start.6 = (bf16[128,128]{1,0:T(8,128)(2,1)S(1)}, bf16[128,128]{1,0:T(8,128)(2,1)S(1)}, u32[]{:S(2)}, u32[]{:S(2)}) collective-permute-start(bf16[128,128]{1,0:T(8,128)(2,1)S(1)} %get-tuple-element.33), channel_id=1, source_target_pairs={{0,4},{4,0},{8,12},{12,8},{1,5},{5,1},{9,13},{13,9},{2,6},{6,2},{1... | collective-permute-start | bytes 98312 | tf_op jit(solution)/shard_map/ppermute | solution.py:410
  20.2 12.4 %collective-permute-start.7 = (bf16[128,128]{1,0:T(8,128)(2,1)S(1)}, bf16[128,128]{1,0:T(8,128)(2,1)S(1)}, u32[]{:S(2)}, u32[]{:S(2)}) collective-permute-start(bf16[128,128]{1,0:T(8,128)(2,1)S(1)} %get-tuple-element.37), channel_id=1, source_target_pairs={{0,8},{4,12},{8,0},{12,4},{1,9},{5,13},{9,1},{13,5},{2,10},{6,14},... | collective-permute-start | bytes 98312 | tf_op jit(solution)/shard_map/ppermute | solution.py:410
  22.4 10.2 %collective-permute-start.8 = (bf16[128,128]{1,0:T(8,128)(2,1)S(1)}, bf16[128,128]{1,0:T(8,128)(2,1)S(1)}, u32[]{:S(2)}, u32[]{:S(2)}) collective-permute-start(bf16[128,128]{1,0:T(8,128)(2,1)S(1)} %get-tuple-element.38), channel_id=1, source_target_pairs={{0,12},{4,8},{8,4},{12,0},{1,13},{5,9},{9,5},{13,1},{2,14},{6,10},... | collective-permute-start | bytes 98312 | tf_op jit(solution)/shard_map/ppermute | solution.py:410
  29.8 18.3 %collective-permute-start.11 = (bf16[3,2,128,256]{3,2,1,0:T(8,128)(2,1)S(1)}, bf16[3,2,128,256]{3,2,1,0:T(8,128)(2,1)S(1)}, u32[]{:S(2)}, u32[]{:S(2)}) collective-permute-start(bf16[3,2,128,256]{3,2,1,0:T(8,128)(2,1)S(1)} %stage_pages.3._), channel_id=1, source_target_pairs={{0,12},{4,8},{8,4},{12,0},{1,13},{5,9},{9,5},{13,1},{2,14},{6,10},... | collective-permute-start | bytes 1179656 | tf_op jit(solution)/shard_map/ppermute | solution.py:492

commit v9 on v8

--- a/solution.py
+++ b/solution.py
@@ -34,8 +34,8 @@
 
 def stage_rows_kernel(dims, adapter_of, adapter_home, new_group, cached_len, hidden, frozen, *refs):
     groups, own_cap, move_cap, stores = dims
-    messages, plan = refs[:groups], refs[groups]
-    counts, picks, *held, held_sems = refs[groups + 1 :]
+    messages, plan_out = refs[:groups], refs[groups]
+    plan, counts, picks, *held, held_sems = refs[groups + 1 :]
     count, depth, _ = hidden.shape
     lists = (adapter_home, adapter_of, new_group, cached_len, hidden, frozen)
     copies = [
@@ -69,6 +69,8 @@
             plan[groups * own_cap + to * move_cap + at] = r
             counts[groups + to] = at + 1
 
+    plan_copy = pltpu.make_async_copy(plan, plan_out, held_sems.at[6])
+    plan_copy.start()
     lane = lax.broadcasted_iota(jnp.int32, (TILE, LANES), 1)
     for j in range(groups):
         told = jnp.where(lane == 0, picks[j], 0)
@@ -85,6 +87,7 @@
                 source = jnp.maximum(plan[j * own_cap + k], 0)
                 at = (part * own_cap + k) * depth
                 messages[j][at : at + depth, :] = rows[source]
+    plan_copy.wait()
 
 
 def page_routes(groups):
@@ -452,8 +455,9 @@
         functools.partial(stage_rows_kernel, dims),
         out_shape=[message] * groups + [shape((groups * (own_cap + move_cap),), i32)],
         in_specs=[IN_PLACE] * 6,
-        out_specs=[IN_VMEM] * groups + [IN_SMEM],
+        out_specs=[IN_VMEM] * groups + [IN_PLACE],
         scratch_shapes=[
+            pltpu.SMEM((groups * (own_cap + move_cap),), i32),
             pltpu.SMEM((2 * groups,), i32),
             pltpu.SMEM((groups,), i32),
             *[
@@ -462,7 +466,7 @@
             ],
             pltpu.VMEM(hidden.shape, bf16),
             pltpu.VMEM(frozen.shape, bf16),
-            pltpu.SemaphoreType.DMA((6,)),
+            pltpu.SemaphoreType.DMA((7,)),
         ],
         compiler_params=PARAMS,
         name="stage_rows",
@@ -538,7 +542,7 @@
         compiler_params=PARAMS,
         name="place_pages",
         cost_estimate=lasts(0.1),
-    )(told, table, pool, queries[1])
+    )(told, page_table.T, kv_pool, queries[1])
     number_late = len(last) * move_cap
     attended, cache, *for_last = pl.pallas_call(
         functools.partial(early_kernel, dims, first, last),

time: 49.7 us -> 49.5 us (level)
  no operation moved by 1% of the time
where the time goes in v9:
time: 49.5 us; the launch traced here: 49.4 us
  waiting for transfers between devices  23.4 us (47%)
  starting transfers between devices  12.7 us (26%)
  Pallas kernels  12.5 us (25%)
  between operations  0.8 us (2%)
    ppermute x3, waiting for transfers between devices, send_pages(): pages[route] = lax.ppermute(x, 'req', pairs)  13 us
    ppermute x9, waiting for transfers between devices, swap(): lax.ppermute(x, axis, [(i, i ^ j) for i in range(lax.axis_size(axis))])  10.3 us
    ppermute x9, starting transfers between devices, swap(): lax.ppermute(x, axis, [(i, i ^ j) for i in range(lax.axis_size(axis))])  9.62 us
    ppermute x3, starting transfers between devices, send_pages(): pages[route] = lax.ppermute(x, 'req', pairs)  3.1 us
    pallas_call x1, Pallas kernels, per_device(): pl.pallas_call(functools.partial(place_kernel, dims), out_shape=[shape((2...  2.73 us
    pallas_call x1, Pallas kernels, per_device(): pl.pallas_call(functools.partial(early_kernel, dims, first, last), out_sh...  2.51 us
    pallas_call x1, Pallas kernels, per_device(): pl.pallas_call(functools.partial(rank_kernel, dims, order), out_shape=[sh...  2.01 us
    pallas_call x1, Pallas kernels, per_device(): pl.pallas_call(functools.partial(stage_rows_kernel, dims), out_shape=[mes...  1.69 us
  transfers between devices with their start and end apart: 12, of which 6 were waited for; matrix products, arithmetic and copies ran while one was open for 0% of the time, Pallas kernels for 19%

profile of v9, /device:TPU:8, one launch (start us, length us, event | category | flops | bytes accessed | tf_op | source)
XLA Modules:
  0.0 49.4 jit_solution(933249503286301198)
XLA Ops:
  0.7 1.7 %stage_rows.1 = (bf16[272,128]{1,0:T(8,128)(2,1)S(1)}, bf16[272,128]{1,0:T(8,128)(2,1)S(1)}, bf16[272,128]{1,0:T(8,128)(2,1)S(1)}, bf16[272,128]{1,0:T(8,128)(2,1)S(1)}, s32[28]{0:T(128)S(1)}) custom-call(s32[16]{0:T(128)} %adapter_of.1, s32[8]{0:T(128)} %adapter_home.1, s32[16]{0:T(128)} %new_group.1, s32[16]{0:T(128)} %cached_len.3, ...), custom_call_target="tpu_custom_call" | custom-call | flops 1000000000 | bytes 3000000 | tf_op jit(solution)/shard_map/stage_rows/pallas_call | solution.py:454
  2.4 1.6 %collective-permute-start = (bf16[272,128]{1,0:T(8,128)(2,1)S(1)}, bf16[272,128]{1,0:T(8,128)(2,1)S(1)}, u32[]{:S(2)}, u32[]{:S(2)}) collective-permute-start(bf16[272,128]{1,0:T(8,128)(2,1)S(1)} %get-tuple-element.27), channel_id=1, source_target_pairs={{0,12},{4,8},{8,4},{12,0},{1,13},{5,9},{9,5},{13,1},{2,14},{6,10},... | collective-permute-start | bytes 208904 | tf_op jit(solution)/shard_map/ppermute | solution.py:413
  4.0 2.5 %collective-permute-start.1 = (bf16[272,128]{1,0:T(8,128)(2,1)S(1)}, bf16[272,128]{1,0:T(8,128)(2,1)S(1)}, u32[]{:S(2)}, u32[]{:S(2)}) collective-permute-start(bf16[272,128]{1,0:T(8,128)(2,1)S(1)} %get-tuple-element.28), channel_id=1, source_target_pairs={{0,4},{4,0},{8,12},{12,8},{1,5},{5,1},{9,13},{13,9},{2,6},{6,2},{1... | collective-permute-start | bytes 208904 | tf_op jit(solution)/shard_map/ppermute | solution.py:413
  6.5 0.7 %stage_pages.2 = (bf16[3,2,128,256]{3,2,1,0:T(8,128)(2,1)S(1)}, bf16[3,2,128,256]{3,2,1,0:T(8,128)(2,1)S(1)}) custom-call(s32[28]{0:T(128)S(1)} %get-tuple-element.25.plan, s32[8,16]{1,0:T(8,128)S(1)} %bitcast.24, bf16[2,128,16,256]{3,2,1,0:T(8,128)(2,1)S(1)} %copy-done), custom_call_target="tpu_custom_call" | custom-call | flops 100000000 | bytes 300000 | tf_op jit(solution)/shard_map/stage_pages/pallas_call | solution.py:483
  7.2 0.7 %collective-permute-start.9 = (bf16[3,2,128,256]{3,2,1,0:T(8,128)(2,1)S(1)}, bf16[3,2,128,256]{3,2,1,0:T(8,128)(2,1)S(1)}, u32[]{:S(2)}, u32[]{:S(2)}) collective-permute-start(bf16[3,2,128,256]{3,2,1,0:T(8,128)(2,1)S(1)} %get-tuple-element.39), channel_id=1, source_target_pairs={{0,4},{4,0},{8,12},{12,8},{1,5},{5,1},{9,13},{13,9},{2,6},{6,2},{1... | collective-permute-start | bytes 1179656 | tf_op jit(solution)/shard_map/ppermute | solution.py:496
  7.9 2.4 %collective-permute-start.10 = (bf16[3,2,128,256]{3,2,1,0:T(8,128)(2,1)S(1)}, bf16[3,2,128,256]{3,2,1,0:T(8,128)(2,1)S(1)}, u32[]{:S(2)}, u32[]{:S(2)}) collective-permute-start(bf16[3,2,128,256]{3,2,1,0:T(8,128)(2,1)S(1)} %get-tuple-element.26._), channel_id=1, source_target_pairs={{0,8},{4,12},{8,0},{12,4},{1,9},{5,13},{9,1},{13,5},{2,10},{6,14},... | collective-permute-start | bytes 1179656 | tf_op jit(solution)/shard_map/ppermute | solution.py:496
  10.3 0.7 %collective-permute-done.1.refs_1_.refs_5_ = bf16[272,128]{1,0:T(8,128)(2,1)S(1)} collective-permute-done((bf16[272,128]{1,0:T(8,128)(2,1)S(1)}, bf16[272,128]{1,0:T(8,128)(2,1)S(1)}, u32[]{:S(2)}, u32[]{:S(2)}) %collective-permute-start.1) | collective-permute-done | bytes 69664 | tf_op jit(solution)/shard_map/ppermute | solution.py:413
  11.0 1.4 %collective-permute-done.2.refs_2_.refs_6_ = bf16[272,128]{1,0:T(8,128)(2,1)S(1)} collective-permute-done((bf16[272,128]{1,0:T(8,128)(2,1)S(1)}, bf16[272,128]{1,0:T(8,128)(2,1)S(1)}, u32[]{:S(2)}, u32[]{:S(2)}) %collective-permute-start.2) | collective-permute-done | bytes 69664 | tf_op jit(solution)/shard_map/ppermute | solution.py:413
  12.5 2.0 %rank_products.1 = (f32[32,128]{1,0:T(8,128)S(1)}, s32[64]{0:T(128)S(1)}) custom-call(s32[16]{0:T(128)S(1)} %copy-done.5, bf16[128,2048]{1,0:T(8,128)(2,1)S(1)} %bitcast.27, bf16[3,2,128,256]{3,2,1,0:T(8,128)(2,1)S(1)} %get-tuple-element.26._, bf16[272,128]{1,0:T(8,128)(2,1)S(1)} %collective-permute-done.refs_0_.refs_7_, ...), custom_call_target="tpu_custom_call" | custom-call | flops 10000000000 | bytes 30000000 | tf_op jit(solution)/shard_map/rank_products/pallas_call | solution.py:502
  14.5 0.1 collective-permute-start.5
  14.6 1.6 %collective-permute-start.4 = (f32[32,128]{1,0:T(8,128)S(1)}, f32[32,128]{1,0:T(8,128)S(1)}, u32[]{:S(2)}, u32[]{:S(2)}) collective-permute-start(f32[32,128]{1,0:T(8,128)S(1)} %get-tuple-element.32.refs_0_), channel_id=1, source_target_pairs={{0,2},{1,3},{2,0},{3,1},{4,6},{5,7},{6,4},{7,5},{8,10},{9,11},{10,... | collective-permute-start | bytes 49160 | tf_op jit(solution)/shard_map/ppermute | solution.py:413
  16.1 0.3 collective-permute-start.3
  16.4 0.6 %stage_pages.3._ = bf16[3,2,128,256]{3,2,1,0:T(8,128)(2,1)S(1)} custom-call(s32[28]{0:T(128)S(1)} %get-tuple-element.25.plan, s32[8,16]{1,0:T(8,128)S(1)} %bitcast.25, bf16[2,128,16,256]{3,2,1,0:T(8,128)(2,1)S(1)} %copy-done, f32[32,128]{1,0:T(8,128)S(1)} %get-tuple-element.32.refs_0_), custom_call_target="tpu_custom_call" | custom-call | flops 100000000 | bytes 300000 | tf_op jit(solution)/shard_map/stage_pages/pallas_call | solution.py:483
  17.1 0.8 %collective-permute-done.5.refs_3_ = f32[32,128]{1,0:T(8,128)S(1)} collective-permute-done((f32[32,128]{1,0:T(8,128)S(1)}, f32[32,128]{1,0:T(8,128)S(1)}, u32[]{:S(2)}, u32[]{:S(2)}) %collective-permute-start.5) | collective-permute-done | bytes 16416 | tf_op jit(solution)/shard_map/ppermute | solution.py:413
  17.9 0.5 %collective-permute-done.4.refs_2_ = f32[32,128]{1,0:T(8,128)S(1)} collective-permute-done((f32[32,128]{1,0:T(8,128)S(1)}, f32[32,128]{1,0:T(8,128)S(1)}, u32[]{:S(2)}, u32[]{:S(2)}) %collective-permute-start.4) | collective-permute-done | bytes 16416 | tf_op jit(solution)/shard_map/ppermute | solution.py:413
  18.4 0.8 %queries.1 = (bf16[128,128]{1,0:T(8,128)(2,1)S(1)}, bf16[128,128]{1,0:T(8,128)(2,1)S(1)}, bf16[128,128]{1,0:T(8,128)(2,1)S(1)}, bf16[128,128]{1,0:T(8,128)(2,1)S(1)}) custom-call(s32[64]{0:T(128)S(1)} %get-tuple-element.31.told, bf16[128,2048]{1,0:T(8,128)(2,1)S(1)} %bitcast.23, bf16[3,2,128,256]{3,2,1,0:T(8,128)(2,1)S(1)} %stage_pages.3._, ...), custom_call_target="tpu_custom_call" | custom-call | flops 100000000 | bytes 300000 | tf_op jit(solution)/shard_map/queries/pallas_call | solution.py:523
  19.3 0.9 %collective-permute-start.6 = (bf16[128,128]{1,0:T(8,128)(2,1)S(1)}, bf16[128,128]{1,0:T(8,128)(2,1)S(1)}, u32[]{:S(2)}, u32[]{:S(2)}) collective-permute-start(bf16[128,128]{1,0:T(8,128)(2,1)S(1)} %get-tuple-element.33), channel_id=1, source_target_pairs={{0,4},{4,0},{8,12},{12,8},{1,5},{5,1},{9,13},{13,9},{2,6},{6,2},{1... | collective-permute-start | bytes 98312 | tf_op jit(solution)/shard_map/ppermute | solution.py:413
  20.1 2.2 %collective-permute-start.7 = (bf16[128,128]{1,0:T(8,128)(2,1)S(1)}, bf16[128,128]{1,0:T(8,128)(2,1)S(1)}, u32[]{:S(2)}, u32[]{:S(2)}) collective-permute-start(bf16[128,128]{1,0:T(8,128)(2,1)S(1)} %get-tuple-element.37), channel_id=1, source_target_pairs={{0,8},{4,12},{8,0},{12,4},{1,9},{5,13},{9,1},{13,5},{2,10},{6,14},... | collective-permute-start | bytes 98312 | tf_op jit(solution)/shard_map/ppermute | solution.py:413
  22.3 0.5 %collective-permute-start.8 = (bf16[128,128]{1,0:T(8,128)(2,1)S(1)}, bf16[128,128]{1,0:T(8,128)(2,1)S(1)}, u32[]{:S(2)}, u32[]{:S(2)}) collective-permute-start(bf16[128,128]{1,0:T(8,128)(2,1)S(1)} %get-tuple-element.38), channel_id=1, source_target_pairs={{0,12},{4,8},{8,4},{12,0},{1,13},{5,9},{9,5},{13,1},{2,14},{6,10},... | collective-permute-start | bytes 98312 | tf_op jit(solution)/shard_map/ppermute | solution.py:413
  22.8 6.8 %collective-permute-done.6.refs_0_.refs_1_ = bf16[128,128]{1,0:T(8,128)(2,1)S(1)} collective-permute-done((bf16[128,128]{1,0:T(8,128)(2,1)S(1)}, bf16[128,128]{1,0:T(8,128)(2,1)S(1)}, u32[]{:S(2)}, u32[]{:S(2)}) %collective-permute-start.6) | collective-permute-done | bytes 32800 | tf_op jit(solution)/shard_map/ppermute | solution.py:413
  29.7 2.7 %place_pages.1 = (bf16[2,16,128,256]{3,2,1,0:T(8,128)(2,1)}, bf16[2,16,128,256]{3,2,1,0:T(8,128)(2,1)S(1)}) custom-call(s32[64]{0:T(128)S(1)} %get-tuple-element.31.told, s32[8,16]{1,0:T(8,128)S(1)} %bitcast.26, bf16[2,128,16,256]{3,2,1,0:T(8,128)(2,1)S(1)} %copy-done, bf16[128,128]{1,0:T(8,128)(2,1)S(1)} %collective-permute-done.6.refs_0_.refs_1_), custom_call_target="tpu_custom_call" | custom-call | flops 100000000 | bytes 300000 | tf_op jit(solution)/shard_map/place_pages/pallas_call | solution.py:536
  32.5 2.5 %attend_early.1 = (bf16[16,32,128]{2,1,0:T(8,128)(2,1)}, bf16[2,16,128,256]{3,2,1,0:T(8,128)(2,1)}, bf16[3,32,128]{2,1,0:T(8,128)(2,1)S(1)}, f32[3,32,160]{2,1,0...) custom-call(s32[28]{0:T(128)S(1)} %get-tuple-element.25.plan, ...), custom_call_target="tpu_custom_call", output_to_operand_aliasing={{1}: (4, {})} | custom-call | flops 60000002048 | bytes 180000000 | tf_op jit(solution)/shard_map/attend_early/pallas_call | solution.py:547
  35.0 13.0 %collective-permute-done.11.refs_0_ = bf16[3,2,128,256]{3,2,1,0:T(8,128)(2,1)S(1)} collective-permute-done((bf16[3,2,128,256]{3,2,1,0:T(8,128)(2,1)S(1)}, bf16[3,2,128,256]{3,2,1,0:T(8,128)(2,1)S(1)}, u32[]{:S(2)}, u32[]{:S(2)}) %collective-permute-start.11) | collective-permute-done | bytes 393248 | tf_op jit(solution)/shard_map/ppermute | solution.py:496
  48.0 1.4 %attend_arrived.1 = (bf16[16,32,128]{2,1,0:T(8,128)(2,1)}, bf16[2,16,128,256]{3,2,1,0:T(8,128)(2,1)}) custom-call(s32[64]{0:T(128)S(1)} %get-tuple-element.31.told, bf16[3,32,128]{2,1,0:T(8,128)(2,1)S(1)} %get-tuple-element.40.queries, f32[3,32,160]{2,1,0:T(8,128)S(1)} %get-tuple-element.41.masks, ...), custom_call_target="tpu_custom_call", output_to_operand_aliasing={{0}: (5, {}), {1}: (6, {})} | custom-call | flops 1000000000 | bytes 3000000 | tf_op jit(solution)/shard_map/attend_arrived/pallas_call | solution.py:571
  (20 shorter events, 0.1 us)
Async XLA Ops:
  0.6 5.9 %copy-start = (bf16[2,128,16,256]{3,2,1,0:T(8,128)(2,1)S(1)}, bf16[2,128,16,256]{3,2,1,0:T(8,128)(2,1)}, u32[]{:S(2)}) copy-start(bf16[2,128,16,256]{3,2,1,0:T(8,128)(2,1)} %pool.5) | copy-start | bytes 6291460
  0.6 5.9 %copy-start.2 = (s32[16,8]{0,1:T(8,128)S(1)}, s32[16,8]{0,1:T(8,128)}, u32[]{:S(2)}) copy-start(s32[16,8]{0,1:T(8,128)} %param.19) | copy-start | bytes 1540
  0.7 11.8 %copy-start.3 = (bf16[2,64,2048]{2,1,0:T(8,128)(2,1)S(1)}, bf16[2,64,2048]{2,1,0:T(8,128)(2,1)}, u32[]{:S(2)}) copy-start(bf16[2,64,2048]{2,1,0:T(8,128)(2,1)} %param.16) | copy-start | bytes 1572868
  0.7 11.8 %copy-start.5 = (s32[16]{0:T(128)S(1)}, s32[16]{0:T(128)}, u32[]{:S(2)}) copy-start(s32[16]{0:T(128)} %cached_len.3) | copy-start | bytes 196
  2.4 7.9 %collective-permute-start = (bf16[272,128]{1,0:T(8,128)(2,1)S(1)}, bf16[272,128]{1,0:T(8,128)(2,1)S(1)}, u32[]{:S(2)}, u32[]{:S(2)}) collective-permute-start(bf16[272,128]{1,0:T(8,128)(2,1)S(1)} %get-tuple-element.27), channel_id=1, source_target_pairs={{0,12},{4,8},{8,4},{12,0},{1,13},{5,9},{9,5},{13,1},{2,14},{6,10},... | collective-permute-start | bytes 208904 | tf_op jit(solution)/shard_map/ppermute | solution.py:413
  4.0 7.0 %collective-permute-start.1 = (bf16[272,128]{1,0:T(8,128)(2,1)S(1)}, bf16[272,128]{1,0:T(8,128)(2,1)S(1)}, u32[]{:S(2)}, u32[]{:S(2)}) collective-permute-start(bf16[272,128]{1,0:T(8,128)(2,1)S(1)} %get-tuple-element.28), channel_id=1, source_target_pairs={{0,4},{4,0},{8,12},{12,8},{1,5},{5,1},{9,13},{13,9},{2,6},{6,2},{1... | collective-permute-start | bytes 208904 | tf_op jit(solution)/shard_map/ppermute | solution.py:413
  6.5 6.0 %collective-permute-start.2 = (bf16[272,128]{1,0:T(8,128)(2,1)S(1)}, bf16[272,128]{1,0:T(8,128)(2,1)S(1)}, u32[]{:S(2)}, u32[]{:S(2)}) collective-permute-start(bf16[272,128]{1,0:T(8,128)(2,1)S(1)} %get-tuple-element.29), channel_id=1, source_target_pairs={{0,8},{4,12},{8,0},{12,4},{1,9},{5,13},{9,1},{13,5},{2,10},{6,14},... | collective-permute-start | bytes 208904 | tf_op jit(solution)/shard_map/ppermute | solution.py:413
  7.2 25.2 %collective-permute-start.9 = (bf16[3,2,128,256]{3,2,1,0:T(8,128)(2,1)S(1)}, bf16[3,2,128,256]{3,2,1,0:T(8,128)(2,1)S(1)}, u32[]{:S(2)}, u32[]{:S(2)}) collective-permute-start(bf16[3,2,128,256]{3,2,1,0:T(8,128)(2,1)S(1)} %get-tuple-element.39), channel_id=1, source_target_pairs={{0,4},{4,0},{8,12},{12,8},{1,5},{5,1},{9,13},{13,9},{2,6},{6,2},{1... | collective-permute-start | bytes 1179656 | tf_op jit(solution)/shard_map/ppermute | solution.py:496
  7.9 24.6 %collective-permute-start.10 = (bf16[3,2,128,256]{3,2,1,0:T(8,128)(2,1)S(1)}, bf16[3,2,128,256]{3,2,1,0:T(8,128)(2,1)S(1)}, u32[]{:S(2)}, u32[]{:S(2)}) collective-permute-start(bf16[3,2,128,256]{3,2,1,0:T(8,128)(2,1)S(1)} %get-tuple-element.26._), channel_id=1, source_target_pairs={{0,8},{4,12},{8,0},{12,4},{1,9},{5,13},{9,1},{13,5},{2,10},{6,14},... | collective-permute-start | bytes 1179656 | tf_op jit(solution)/shard_map/ppermute | solution.py:496
  14.5 3.9 %copy-start.1 = (bf16[2,64,2048]{2,1,0:T(8,128)(2,1)S(1)}, bf16[2,64,2048]{2,1,0:T(8,128)(2,1)}, u32[]{:S(2)}) copy-start(bf16[2,64,2048]{2,1,0:T(8,128)(2,1)} %param.17) | copy-start | bytes 1572868
  14.5 3.4 %collective-permute-start.5 = (f32[32,128]{1,0:T(8,128)S(1)}, f32[32,128]{1,0:T(8,128)S(1)}, u32[]{:S(2)}, u32[]{:S(2)}) collective-permute-start(f32[32,128]{1,0:T(8,128)S(1)} %get-tuple-element.32.refs_0_), channel_id=1, source_target_pairs={{0,3},{1,2},{2,1},{3,0},{4,7},{5,6},{6,5},{7,4},{8,11},{9,10},{10,... | collective-permute-start | bytes 49160 | tf_op jit(solution)/shard_map/ppermute | solution.py:413
  14.6 3.8 %collective-permute-start.4 = (f32[32,128]{1,0:T(8,128)S(1)}, f32[32,128]{1,0:T(8,128)S(1)}, u32[]{:S(2)}, u32[]{:S(2)}) collective-permute-start(f32[32,128]{1,0:T(8,128)S(1)} %get-tuple-element.32.refs_0_), channel_id=1, source_target_pairs={{0,2},{1,3},{2,0},{3,1},{4,6},{5,7},{6,4},{7,5},{8,10},{9,11},{10,... | collective-permute-start | bytes 49160 | tf_op jit(solution)/shard_map/ppermute | solution.py:413
  16.1 2.3 %collective-permute-start.3 = (f32[32,128]{1,0:T(8,128)S(1)}, f32[32,128]{1,0:T(8,128)S(1)}, u32[]{:S(2)}, u32[]{:S(2)}) collective-permute-start(f32[32,128]{1,0:T(8,128)S(1)} %get-tuple-element.32.refs_0_), channel_id=1, source_target_pairs={{0,1},{1,0},{2,3},{3,2},{4,5},{5,4},{6,7},{7,6},{8,9},{9,8},{10,11... | collective-permute-start | bytes 49160 | tf_op jit(solution)/shard_map/ppermute | solution.py:413
  17.1 15.4 %copy-start.4 = (bf16[16,2,2,256]{3,2,1,0:T(2,128)(2,1)S(1)}, bf16[16,2,2,256]{3,2,1,0:T(2,128)(2,1)}, u32[]{:S(2)}) copy-start(bf16[16,2,2,256]{3,2,1,0:T(2,128)(2,1)} %param.13) | copy-start | bytes 98308
  19.3 10.4 %collective-permute-start.6 = (bf16[128,128]{1,0:T(8,128)(2,1)S(1)}, bf16[128,128]{1,0:T(8,128)(2,1)S(1)}, u32[]{:S(2)}, u32[]{:S(2)}) collective-permute-start(bf16[128,128]{1,0:T(8,128)(2,1)S(1)} %get-tuple-element.33), channel_id=1, source_target_pairs={{0,4},{4,0},{8,12},{12,8},{1,5},{5,1},{9,13},{13,9},{2,6},{6,2},{1... | collective-permute-start | bytes 98312 | tf_op jit(solution)/shard_map/ppermute | solution.py:413
  20.1 12.3 %collective-permute-start.7 = (bf16[128,128]{1,0:T(8,128)(2,1)S(1)}, bf16[128,128]{1,0:T(8,128)(2,1)S(1)}, u32[]{:S(2)}, u32[]{:S(2)}) collective-permute-start(bf16[128,128]{1,0:T(8,128)(2,1)S(1)} %get-tuple-element.37), channel_id=1, source_target_pairs={{0,8},{4,12},{8,0},{12,4},{1,9},{5,13},{9,1},{13,5},{2,10},{6,14},... | collective-permute-start | bytes 98312 | tf_op jit(solution)/shard_map/ppermute | solution.py:413
  22.3 10.1 %collective-permute-start.8 = (bf16[128,128]{1,0:T(8,128)(2,1)S(1)}, bf16[128,128]{1,0:T(8,128)(2,1)S(1)}, u32[]{:S(2)}, u32[]{:S(2)}) collective-permute-start(bf16[128,128]{1,0:T(8,128)(2,1)S(1)} %get-tuple-element.38), channel_id=1, source_target_pairs={{0,12},{4,8},{8,4},{12,0},{1,13},{5,9},{9,5},{13,1},{2,14},{6,10},... | collective-permute-start | bytes 98312 | tf_op jit(solution)/shard_map/ppermute | solution.py:413
  29.7 18.3 %collective-permute-start.11 = (bf16[3,2,128,256]{3,2,1,0:T(8,128)(2,1)S(1)}, bf16[3,2,128,256]{3,2,1,0:T(8,128)(2,1)S(1)}, u32[]{:S(2)}, u32[]{:S(2)}) collective-permute-start(bf16[3,2,128,256]{3,2,1,0:T(8,128)(2,1)S(1)} %stage_pages.3._), channel_id=1, source_target_pairs={{0,12},{4,8},{8,4},{12,0},{1,13},{5,9},{9,5},{13,1},{2,14},{6,10},... | collective-permute-start | bytes 1179656 | tf_op jit(solution)/shard_map/ppermute | solution.py:496

commit v10 on v8

--- a/solution.py
+++ b/solution.py
@@ -236,28 +236,32 @@
     return (column < length) | ((fresh_at >= 0) & (fresh_at <= step))
 
 
-def attend(queries, keys, values, fresh, masks):
-    depth = queries[0].shape[0]
+def chances_of(queries, keys, fresh_keys, masks):
     heads = keys[0].shape[1] // HEAD
-    per = depth // heads
     scale = HEAD**-0.5
     scores = []
     for query, key, mask in zip(queries, keys, masks):
         product = lax.dot_general(
             by_head(query, heads),
-            jnp.concatenate([key, fresh[0]], axis=0),
+            jnp.concatenate([key, fresh_keys], axis=0),
             (((1,), (1,)), ((), ())),
             preferred_element_type=jnp.float32,
         )
         scores.append(jnp.where(mask, product * scale, NEG_FILL))
     scores = jnp.concatenate(scores, axis=0)
     weights = jnp.exp(scores - jnp.max(scores, axis=1, keepdims=True))
-    chances = (weights / jnp.sum(weights, axis=1, keepdims=True)).astype(jnp.bfloat16)
+    return (weights / jnp.sum(weights, axis=1, keepdims=True)).astype(jnp.bfloat16)
+
+
+def mixed(chances, values, fresh_values):
+    depth = chances.shape[0] // len(values)
+    heads = values[0].shape[1] // HEAD
+    per = depth // heads
     results = []
     for n, value in enumerate(values):
         out = jnp.dot(
             chances[n * depth : (n + 1) * depth],
-            jnp.concatenate([value, fresh[1]], axis=0),
+            jnp.concatenate([value, fresh_values], axis=0),
             preferred_element_type=jnp.float32,
         )
         out = jnp.concatenate(
@@ -334,12 +338,14 @@
 
     every = list(range(count))
     fresh = fresh_rows(new_kv, x, width // HEAD)
-    results = attend(
+    chances = chances_of(
         [sorted_queries[at] for at in every + places],
         [kv[0, r] for r in every] + [block[0] for block in blocks],
-        [kv[1, r] for r in every] + [block[1] for block in blocks],
-        fresh,
+        fresh[0],
         [mask(at) for at in every + places],
+    )
+    results = mixed(
+        chances, [kv[1, r] for r in every] + [block[1] for block in blocks], fresh[1]
     )
     for r in every:
         attended[r] = results[r]
@@ -366,11 +372,10 @@
     blocks = [ref.at[k] for ref in pages for k in range(dims[2])]
     told_copy = pltpu.make_async_copy(told, slots_held, told_sem)
     told_copy.start()
-    outs = attend(
+    chances = chances_of(
         [queries[n] for n in range(number)],
         [block[0] for block in blocks],
-        [block[1] for block in blocks],
-        (new_keys[...], new_values[...]),
+        new_keys[...],
         [masks[n] > 0.5 for n in range(number)],
     )
     told_copy.wait()
@@ -384,7 +389,7 @@
     ]
     for slot, (copy, _) in zip(slots, copies):
         pl.when(slot >= 0)(copy.start)
-    for n, out in enumerate(outs):
+    for n, out in enumerate(mixed(chances, [block[1] for block in blocks], new_values[...])):
         results[n] = out
     for slot, (_, copy) in zip(slots, copies):
         pl.when(slot >= 0)(copy.start)

time: 49.7 us -> 49.8 us (level)
  no operation moved by 1% of the time
where the time goes in v10:
time: 49.8 us; the launch traced here: 49.5 us
  waiting for transfers between devices  23.2 us (47%)
  Pallas kernels  12.7 us (26%)
  starting transfers between devices  12.7 us (26%)
  between operations  0.8 us (2%)
    ppermute x3, waiting for transfers between devices, send_pages(): pages[route] = lax.ppermute(x, 'req', pairs)  12.9 us
    ppermute x9, waiting for transfers between devices, swap(): lax.ppermute(x, axis, [(i, i ^ j) for i in range(lax.axis_size(axis))])  10.3 us
    ppermute x9, starting transfers between devices, swap(): lax.ppermute(x, axis, [(i, i ^ j) for i in range(lax.axis_size(axis))])  9.62 us
    ppermute x3, starting transfers between devices, send_pages(): pages[route] = lax.ppermute(x, 'req', pairs)  3.1 us
    pallas_call x1, Pallas kernels, per_device(): pl.pallas_call(functools.partial(place_kernel, dims), out_shape=[shape((2...  2.87 us
    pallas_call x1, Pallas kernels, per_device(): pl.pallas_call(functools.partial(early_kernel, dims, first, last), out_sh...  2.52 us
    pallas_call x1, Pallas kernels, per_device(): pl.pallas_call(functools.partial(rank_kernel, dims, order), out_shape=[sh...  2.01 us
    pallas_call x1, Pallas kernels, per_device(): pl.pallas_call(functools.partial(stage_rows_kernel, dims), out_shape=[mes...  1.78 us
  transfers between devices with their start and end apart: 12, of which 6 were waited for; matrix products, arithmetic and copies ran while one was open for 0% of the time, Pallas kernels for 19%

profile of v10, /device:TPU:8, one launch (start us, length us, event | category | flops | bytes accessed | tf_op | source)
XLA Modules:
  0.0 49.5 jit_solution(939985616756062527)
XLA Ops:
  0.7 1.8 %stage_rows.1 = (bf16[272,128]{1,0:T(8,128)(2,1)S(1)}, bf16[272,128]{1,0:T(8,128)(2,1)S(1)}, bf16[272,128]{1,0:T(8,128)(2,1)S(1)}, bf16[272,128]{1,0:T(8,128)(2,1)S(1)}, s32[28]{0:T(128)S(1)}) custom-call(s32[16]{0:T(128)} %adapter_of.1, s32[8]{0:T(128)} %adapter_home.1, s32[16]{0:T(128)} %new_group.1, s32[16]{0:T(128)} %cached_len.3, ...), custom_call_target="tpu_custom_call" | custom-call | flops 1000000000 | bytes 3000000 | tf_op jit(solution)/shard_map/stage_rows/pallas_call | solution.py:456
  2.5 1.6 %collective-permute-start = (bf16[272,128]{1,0:T(8,128)(2,1)S(1)}, bf16[272,128]{1,0:T(8,128)(2,1)S(1)}, u32[]{:S(2)}, u32[]{:S(2)}) collective-permute-start(bf16[272,128]{1,0:T(8,128)(2,1)S(1)} %get-tuple-element.27), channel_id=1, source_target_pairs={{0,12},{4,8},{8,4},{12,0},{1,13},{5,9},{9,5},{13,1},{2,14},{6,10},... | collective-permute-start | bytes 208904 | tf_op jit(solution)/shard_map/ppermute | solution.py:415
  4.1 2.5 %collective-permute-start.1 = (bf16[272,128]{1,0:T(8,128)(2,1)S(1)}, bf16[272,128]{1,0:T(8,128)(2,1)S(1)}, u32[]{:S(2)}, u32[]{:S(2)}) collective-permute-start(bf16[272,128]{1,0:T(8,128)(2,1)S(1)} %get-tuple-element.28), channel_id=1, source_target_pairs={{0,4},{4,0},{8,12},{12,8},{1,5},{5,1},{9,13},{13,9},{2,6},{6,2},{1... | collective-permute-start | bytes 208904 | tf_op jit(solution)/shard_map/ppermute | solution.py:415
  6.6 0.7 %stage_pages.2 = (bf16[3,2,128,256]{3,2,1,0:T(8,128)(2,1)S(1)}, bf16[3,2,128,256]{3,2,1,0:T(8,128)(2,1)S(1)}) custom-call(s32[28]{0:T(128)S(1)} %get-tuple-element.25.plan, s32[8,16]{1,0:T(8,128)S(1)} %bitcast.25, bf16[2,128,16,256]{3,2,1,0:T(8,128)(2,1)S(1)} %copy-done), custom_call_target="tpu_custom_call" | custom-call | flops 100000000 | bytes 300000 | tf_op jit(solution)/shard_map/stage_pages/pallas_call | solution.py:484
  7.3 0.7 %collective-permute-start.9 = (bf16[3,2,128,256]{3,2,1,0:T(8,128)(2,1)S(1)}, bf16[3,2,128,256]{3,2,1,0:T(8,128)(2,1)S(1)}, u32[]{:S(2)}, u32[]{:S(2)}) collective-permute-start(bf16[3,2,128,256]{3,2,1,0:T(8,128)(2,1)S(1)} %get-tuple-element.39), channel_id=1, source_target_pairs={{0,4},{4,0},{8,12},{12,8},{1,5},{5,1},{9,13},{13,9},{2,6},{6,2},{1... | collective-permute-start | bytes 1179656 | tf_op jit(solution)/shard_map/ppermute | solution.py:497
  8.0 2.4 %collective-permute-start.10 = (bf16[3,2,128,256]{3,2,1,0:T(8,128)(2,1)S(1)}, bf16[3,2,128,256]{3,2,1,0:T(8,128)(2,1)S(1)}, u32[]{:S(2)}, u32[]{:S(2)}) collective-permute-start(bf16[3,2,128,256]{3,2,1,0:T(8,128)(2,1)S(1)} %get-tuple-element.26._), channel_id=1, source_target_pairs={{0,8},{4,12},{8,0},{12,4},{1,9},{5,13},{9,1},{13,5},{2,10},{6,14},... | collective-permute-start | bytes 1179656 | tf_op jit(solution)/shard_map/ppermute | solution.py:497
  10.4 0.7 %collective-permute-done.1.refs_1_.refs_5_ = bf16[272,128]{1,0:T(8,128)(2,1)S(1)} collective-permute-done((bf16[272,128]{1,0:T(8,128)(2,1)S(1)}, bf16[272,128]{1,0:T(8,128)(2,1)S(1)}, u32[]{:S(2)}, u32[]{:S(2)}) %collective-permute-start.1) | collective-permute-done | bytes 69664 | tf_op jit(solution)/shard_map/ppermute | solution.py:415
  11.1 1.4 %collective-permute-done.2.refs_2_.refs_6_ = bf16[272,128]{1,0:T(8,128)(2,1)S(1)} collective-permute-done((bf16[272,128]{1,0:T(8,128)(2,1)S(1)}, bf16[272,128]{1,0:T(8,128)(2,1)S(1)}, u32[]{:S(2)}, u32[]{:S(2)}) %collective-permute-start.2) | collective-permute-done | bytes 69664 | tf_op jit(solution)/shard_map/ppermute | solution.py:415
  12.6 2.0 %rank_products.1 = (f32[32,128]{1,0:T(8,128)S(1)}, s32[64]{0:T(128)S(1)}) custom-call(s32[16]{0:T(128)S(1)} %copy-done.5, bf16[128,2048]{1,0:T(8,128)(2,1)S(1)} %bitcast.27, bf16[3,2,128,256]{3,2,1,0:T(8,128)(2,1)S(1)} %get-tuple-element.26._, bf16[272,128]{1,0:T(8,128)(2,1)S(1)} %collective-permute-done.refs_0_.refs_7_, ...), custom_call_target="tpu_custom_call" | custom-call | flops 10000000000 | bytes 30000000 | tf_op jit(solution)/shard_map/rank_products/pallas_call | solution.py:503
  14.6 0.1 collective-permute-start.5
  14.7 1.6 %collective-permute-start.4 = (f32[32,128]{1,0:T(8,128)S(1)}, f32[32,128]{1,0:T(8,128)S(1)}, u32[]{:S(2)}, u32[]{:S(2)}) collective-permute-start(f32[32,128]{1,0:T(8,128)S(1)} %get-tuple-element.32.refs_0_), channel_id=1, source_target_pairs={{0,2},{1,3},{2,0},{3,1},{4,6},{5,7},{6,4},{7,5},{8,10},{9,11},{10,... | collective-permute-start | bytes 49160 | tf_op jit(solution)/shard_map/ppermute | solution.py:415
  16.2 0.3 collective-permute-start.3
  16.5 0.6 %stage_pages.3._ = bf16[3,2,128,256]{3,2,1,0:T(8,128)(2,1)S(1)} custom-call(s32[28]{0:T(128)S(1)} %get-tuple-element.25.plan, s32[8,16]{1,0:T(8,128)S(1)} %bitcast.26, bf16[2,128,16,256]{3,2,1,0:T(8,128)(2,1)S(1)} %copy-done, f32[32,128]{1,0:T(8,128)S(1)} %get-tuple-element.32.refs_0_), custom_call_target="tpu_custom_call" | custom-call | flops 100000000 | bytes 300000 | tf_op jit(solution)/shard_map/stage_pages/pallas_call | solution.py:484
  17.2 0.8 %collective-permute-done.5.refs_3_ = f32[32,128]{1,0:T(8,128)S(1)} collective-permute-done((f32[32,128]{1,0:T(8,128)S(1)}, f32[32,128]{1,0:T(8,128)S(1)}, u32[]{:S(2)}, u32[]{:S(2)}) %collective-permute-start.5) | collective-permute-done | bytes 16416 | tf_op jit(solution)/shard_map/ppermute | solution.py:415
  18.0 0.5 %collective-permute-done.4.refs_2_ = f32[32,128]{1,0:T(8,128)S(1)} collective-permute-done((f32[32,128]{1,0:T(8,128)S(1)}, f32[32,128]{1,0:T(8,128)S(1)}, u32[]{:S(2)}, u32[]{:S(2)}) %collective-permute-start.4) | collective-permute-done | bytes 16416 | tf_op jit(solution)/shard_map/ppermute | solution.py:415
  18.5 0.8 %queries.1 = (bf16[128,128]{1,0:T(8,128)(2,1)S(1)}, bf16[128,128]{1,0:T(8,128)(2,1)S(1)}, bf16[128,128]{1,0:T(8,128)(2,1)S(1)}, bf16[128,128]{1,0:T(8,128)(2,1)S(1)}) custom-call(s32[64]{0:T(128)S(1)} %get-tuple-element.31.told, bf16[128,2048]{1,0:T(8,128)(2,1)S(1)} %bitcast.23, bf16[3,2,128,256]{3,2,1,0:T(8,128)(2,1)S(1)} %stage_pages.3._, ...), custom_call_target="tpu_custom_call" | custom-call | flops 100000000 | bytes 300000 | tf_op jit(solution)/shard_map/queries/pallas_call | solution.py:524
  19.3 0.9 %collective-permute-start.6 = (bf16[128,128]{1,0:T(8,128)(2,1)S(1)}, bf16[128,128]{1,0:T(8,128)(2,1)S(1)}, u32[]{:S(2)}, u32[]{:S(2)}) collective-permute-start(bf16[128,128]{1,0:T(8,128)(2,1)S(1)} %get-tuple-element.33), channel_id=1, source_target_pairs={{0,4},{4,0},{8,12},{12,8},{1,5},{5,1},{9,13},{13,9},{2,6},{6,2},{1... | collective-permute-start | bytes 98312 | tf_op jit(solution)/shard_map/ppermute | solution.py:415
  20.2 2.2 %collective-permute-start.7 = (bf16[128,128]{1,0:T(8,128)(2,1)S(1)}, bf16[128,128]{1,0:T(8,128)(2,1)S(1)}, u32[]{:S(2)}, u32[]{:S(2)}) collective-permute-start(bf16[128,128]{1,0:T(8,128)(2,1)S(1)} %get-tuple-element.37), channel_id=1, source_target_pairs={{0,8},{4,12},{8,0},{12,4},{1,9},{5,13},{9,1},{13,5},{2,10},{6,14},... | collective-permute-start | bytes 98312 | tf_op jit(solution)/shard_map/ppermute | solution.py:415
  22.4 0.5 %collective-permute-start.8 = (bf16[128,128]{1,0:T(8,128)(2,1)S(1)}, bf16[128,128]{1,0:T(8,128)(2,1)S(1)}, u32[]{:S(2)}, u32[]{:S(2)}) collective-permute-start(bf16[128,128]{1,0:T(8,128)(2,1)S(1)} %get-tuple-element.38), channel_id=1, source_target_pairs={{0,12},{4,8},{8,4},{12,0},{1,13},{5,9},{9,5},{13,1},{2,14},{6,10},... | collective-permute-start | bytes 98312 | tf_op jit(solution)/shard_map/ppermute | solution.py:415
  22.9 6.8 %collective-permute-done.6.refs_0_.refs_1_ = bf16[128,128]{1,0:T(8,128)(2,1)S(1)} collective-permute-done((bf16[128,128]{1,0:T(8,128)(2,1)S(1)}, bf16[128,128]{1,0:T(8,128)(2,1)S(1)}, u32[]{:S(2)}, u32[]{:S(2)}) %collective-permute-start.6) | collective-permute-done | bytes 32800 | tf_op jit(solution)/shard_map/ppermute | solution.py:415
  29.8 2.9 %place_pages.1 = (bf16[2,16,128,256]{3,2,1,0:T(8,128)(2,1)}, bf16[2,16,128,256]{3,2,1,0:T(8,128)(2,1)S(1)}) custom-call(s32[64]{0:T(128)S(1)} %get-tuple-element.31.told, s32[8,16]{1,0:T(8,128)} %bitcast.24, bf16[2,128,16,256]{3,2,1,0:T(8,128)(2,1)} %pool.5, bf16[128,128]{1,0:T(8,128)(2,1)S(1)} %collective-permute-done.6.refs_0_.refs_1_), custom_call_target="tpu_custom_call" | custom-call | flops 100000000 | bytes 300000 | tf_op jit(solution)/shard_map/place_pages/pallas_call | solution.py:537
  32.7 2.5 %attend_early.1 = (bf16[16,32,128]{2,1,0:T(8,128)(2,1)}, bf16[2,16,128,256]{3,2,1,0:T(8,128)(2,1)}, bf16[3,32,128]{2,1,0:T(8,128)(2,1)S(1)}, f32[3,32,160]{2,1,0...) custom-call(s32[28]{0:T(128)S(1)} %get-tuple-element.25.plan, ...), custom_call_target="tpu_custom_call", output_to_operand_aliasing={{1}: (4, {})} | custom-call | flops 60000002048 | bytes 180000000 | tf_op jit(solution)/shard_map/attend_early/pallas_call | solution.py:548
  35.2 12.9 %collective-permute-done.11.refs_0_ = bf16[3,2,128,256]{3,2,1,0:T(8,128)(2,1)S(1)} collective-permute-done((bf16[3,2,128,256]{3,2,1,0:T(8,128)(2,1)S(1)}, bf16[3,2,128,256]{3,2,1,0:T(8,128)(2,1)S(1)}, u32[]{:S(2)}, u32[]{:S(2)}) %collective-permute-start.11) | collective-permute-done | bytes 393248 | tf_op jit(solution)/shard_map/ppermute | solution.py:497
  48.1 1.4 %attend_arrived.1 = (bf16[16,32,128]{2,1,0:T(8,128)(2,1)}, bf16[2,16,128,256]{3,2,1,0:T(8,128)(2,1)}) custom-call(s32[64]{0:T(128)S(1)} %get-tuple-element.31.told, bf16[3,32,128]{2,1,0:T(8,128)(2,1)S(1)} %get-tuple-element.40.queries, f32[3,32,160]{2,1,0:T(8,128)S(1)} %get-tuple-element.41.masks, ...), custom_call_target="tpu_custom_call", output_to_operand_aliasing={{0}: (5, {}), {1}: (6, {})} | custom-call | flops 1000000000 | bytes 3000000 | tf_op jit(solution)/shard_map/attend_arrived/pallas_call | solution.py:572
  (20 shorter events, 0.1 us)
Async XLA Ops:
  0.6 6.0 %copy-start = (bf16[2,128,16,256]{3,2,1,0:T(8,128)(2,1)S(1)}, bf16[2,128,16,256]{3,2,1,0:T(8,128)(2,1)}, u32[]{:S(2)}) copy-start(bf16[2,128,16,256]{3,2,1,0:T(8,128)(2,1)} %pool.5) | copy-start | bytes 6291460
  0.6 5.9 %copy-start.2 = (s32[16,8]{0,1:T(8,128)S(1)}, s32[16,8]{0,1:T(8,128)}, u32[]{:S(2)}) copy-start(s32[16,8]{0,1:T(8,128)} %param.19) | copy-start | bytes 1540
  0.7 11.9 %copy-start.3 = (bf16[2,64,2048]{2,1,0:T(8,128)(2,1)S(1)}, bf16[2,64,2048]{2,1,0:T(8,128)(2,1)}, u32[]{:S(2)}) copy-start(bf16[2,64,2048]{2,1,0:T(8,128)(2,1)} %param.16) | copy-start | bytes 1572868
  0.7 11.9 %copy-start.5 = (s32[16]{0:T(128)S(1)}, s32[16]{0:T(128)}, u32[]{:S(2)}) copy-start(s32[16]{0:T(128)} %cached_len.3) | copy-start | bytes 196
  2.5 7.9 %collective-permute-start = (bf16[272,128]{1,0:T(8,128)(2,1)S(1)}, bf16[272,128]{1,0:T(8,128)(2,1)S(1)}, u32[]{:S(2)}, u32[]{:S(2)}) collective-permute-start(bf16[272,128]{1,0:T(8,128)(2,1)S(1)} %get-tuple-element.27), channel_id=1, source_target_pairs={{0,12},{4,8},{8,4},{12,0},{1,13},{5,9},{9,5},{13,1},{2,14},{6,10},... | collective-permute-start | bytes 208904 | tf_op jit(solution)/shard_map/ppermute | solution.py:415
  4.1 7.0 %collective-permute-start.1 = (bf16[272,128]{1,0:T(8,128)(2,1)S(1)}, bf16[272,128]{1,0:T(8,128)(2,1)S(1)}, u32[]{:S(2)}, u32[]{:S(2)}) collective-permute-start(bf16[272,128]{1,0:T(8,128)(2,1)S(1)} %get-tuple-element.28), channel_id=1, source_target_pairs={{0,4},{4,0},{8,12},{12,8},{1,5},{5,1},{9,13},{13,9},{2,6},{6,2},{1... | collective-permute-start | bytes 208904 | tf_op jit(solution)/shard_map/ppermute | solution.py:415
  6.6 6.0 %collective-permute-start.2 = (bf16[272,128]{1,0:T(8,128)(2,1)S(1)}, bf16[272,128]{1,0:T(8,128)(2,1)S(1)}, u32[]{:S(2)}, u32[]{:S(2)}) collective-permute-start(bf16[272,128]{1,0:T(8,128)(2,1)S(1)} %get-tuple-element.29), channel_id=1, source_target_pairs={{0,8},{4,12},{8,0},{12,4},{1,9},{5,13},{9,1},{13,5},{2,10},{6,14},... | collective-permute-start | bytes 208904 | tf_op jit(solution)/shard_map/ppermute | solution.py:415
  7.3 25.4 %collective-permute-start.9 = (bf16[3,2,128,256]{3,2,1,0:T(8,128)(2,1)S(1)}, bf16[3,2,128,256]{3,2,1,0:T(8,128)(2,1)S(1)}, u32[]{:S(2)}, u32[]{:S(2)}) collective-permute-start(bf16[3,2,128,256]{3,2,1,0:T(8,128)(2,1)S(1)} %get-tuple-element.39), channel_id=1, source_target_pairs={{0,4},{4,0},{8,12},{12,8},{1,5},{5,1},{9,13},{13,9},{2,6},{6,2},{1... | collective-permute-start | bytes 1179656 | tf_op jit(solution)/shard_map/ppermute | solution.py:497
  8.0 24.7 %collective-permute-start.10 = (bf16[3,2,128,256]{3,2,1,0:T(8,128)(2,1)S(1)}, bf16[3,2,128,256]{3,2,1,0:T(8,128)(2,1)S(1)}, u32[]{:S(2)}, u32[]{:S(2)}) collective-permute-start(bf16[3,2,128,256]{3,2,1,0:T(8,128)(2,1)S(1)} %get-tuple-element.26._), channel_id=1, source_target_pairs={{0,8},{4,12},{8,0},{12,4},{1,9},{5,13},{9,1},{13,5},{2,10},{6,14},... | collective-permute-start | bytes 1179656 | tf_op jit(solution)/shard_map/ppermute | solution.py:497
  14.6 3.9 %copy-start.1 = (bf16[2,64,2048]{2,1,0:T(8,128)(2,1)S(1)}, bf16[2,64,2048]{2,1,0:T(8,128)(2,1)}, u32[]{:S(2)}) copy-start(bf16[2,64,2048]{2,1,0:T(8,128)(2,1)} %param.17) | copy-start | bytes 1572868
  14.6 3.4 %collective-permute-start.5 = (f32[32,128]{1,0:T(8,128)S(1)}, f32[32,128]{1,0:T(8,128)S(1)}, u32[]{:S(2)}, u32[]{:S(2)}) collective-permute-start(f32[32,128]{1,0:T(8,128)S(1)} %get-tuple-element.32.refs_0_), channel_id=1, source_target_pairs={{0,3},{1,2},{2,1},{3,0},{4,7},{5,6},{6,5},{7,4},{8,11},{9,10},{10,... | collective-permute-start | bytes 49160 | tf_op jit(solution)/shard_map/ppermute | solution.py:415
  14.7 3.8 %collective-permute-start.4 = (f32[32,128]{1,0:T(8,128)S(1)}, f32[32,128]{1,0:T(8,128)S(1)}, u32[]{:S(2)}, u32[]{:S(2)}) collective-permute-start(f32[32,128]{1,0:T(8,128)S(1)} %get-tuple-element.32.refs_0_), channel_id=1, source_target_pairs={{0,2},{1,3},{2,0},{3,1},{4,6},{5,7},{6,4},{7,5},{8,10},{9,11},{10,... | collective-permute-start | bytes 49160 | tf_op jit(solution)/shard_map/ppermute | solution.py:415
  16.2 2.3 %collective-permute-start.3 = (f32[32,128]{1,0:T(8,128)S(1)}, f32[32,128]{1,0:T(8,128)S(1)}, u32[]{:S(2)}, u32[]{:S(2)}) collective-permute-start(f32[32,128]{1,0:T(8,128)S(1)} %get-tuple-element.32.refs_0_), channel_id=1, source_target_pairs={{0,1},{1,0},{2,3},{3,2},{4,5},{5,4},{6,7},{7,6},{8,9},{9,8},{10,11... | collective-permute-start | bytes 49160 | tf_op jit(solution)/shard_map/ppermute | solution.py:415
  17.2 15.5 %copy-start.4 = (bf16[16,2,2,256]{3,2,1,0:T(2,128)(2,1)S(1)}, bf16[16,2,2,256]{3,2,1,0:T(2,128)(2,1)}, u32[]{:S(2)}) copy-start(bf16[16,2,2,256]{3,2,1,0:T(2,128)(2,1)} %param.13) | copy-start | bytes 98308
  19.3 10.4 %collective-permute-start.6 = (bf16[128,128]{1,0:T(8,128)(2,1)S(1)}, bf16[128,128]{1,0:T(8,128)(2,1)S(1)}, u32[]{:S(2)}, u32[]{:S(2)}) collective-permute-start(bf16[128,128]{1,0:T(8,128)(2,1)S(1)} %get-tuple-element.33), channel_id=1, source_target_pairs={{0,4},{4,0},{8,12},{12,8},{1,5},{5,1},{9,13},{13,9},{2,6},{6,2},{1... | collective-permute-start | bytes 98312 | tf_op jit(solution)/shard_map/ppermute | solution.py:415
  20.2 12.4 %collective-permute-start.7 = (bf16[128,128]{1,0:T(8,128)(2,1)S(1)}, bf16[128,128]{1,0:T(8,128)(2,1)S(1)}, u32[]{:S(2)}, u32[]{:S(2)}) collective-permute-start(bf16[128,128]{1,0:T(8,128)(2,1)S(1)} %get-tuple-element.37), channel_id=1, source_target_pairs={{0,8},{4,12},{8,0},{12,4},{1,9},{5,13},{9,1},{13,5},{2,10},{6,14},... | collective-permute-start | bytes 98312 | tf_op jit(solution)/shard_map/ppermute | solution.py:415
  22.4 10.2 %collective-permute-start.8 = (bf16[128,128]{1,0:T(8,128)(2,1)S(1)}, bf16[128,128]{1,0:T(8,128)(2,1)S(1)}, u32[]{:S(2)}, u32[]{:S(2)}) collective-permute-start(bf16[128,128]{1,0:T(8,128)(2,1)S(1)} %get-tuple-element.38), channel_id=1, source_target_pairs={{0,12},{4,8},{8,4},{12,0},{1,13},{5,9},{9,5},{13,1},{2,14},{6,10},... | collective-permute-start | bytes 98312 | tf_op jit(solution)/shard_map/ppermute | solution.py:415
  29.8 18.3 %collective-permute-start.11 = (bf16[3,2,128,256]{3,2,1,0:T(8,128)(2,1)S(1)}, bf16[3,2,128,256]{3,2,1,0:T(8,128)(2,1)S(1)}, u32[]{:S(2)}, u32[]{:S(2)}) collective-permute-start(bf16[3,2,128,256]{3,2,1,0:T(8,128)(2,1)S(1)} %stage_pages.3._), channel_id=1, source_target_pairs={{0,12},{4,8},{8,4},{12,0},{1,13},{5,9},{9,5},{13,1},{2,14},{6,10},... | collective-permute-start | bytes 1179656 | tf_op jit(solution)/shard_map/ppermute | solution.py:497
